TPU v7x, 128 devices: a whole 4x4x4 slice. The times are simulated.
128 devices in a mesh: inst: 8 (over z, x_lo), tp: 16 (over x_hi, y, core).
Axes of the slice: x: 4 (x_hi: 2, x_lo: 2; x = x_hi * 2 + x_lo), y: 4, z: 4, core: 2. Of those that a mesh axis runs over, the one named last changes fastest.
Arguments:
- x_steps: bfloat16 [2, 512, 8192], P(None, 'inst', 'tp'), may hold values from -6 to 6
- norm_gain: float32 [8192], replicated, may hold values from 0.1 to 1.9
- w_query: bfloat16 [8192, 8192], P(None, 'tp'), may hold values from -0.0625 to 0.0625
- w_keyval: bfloat16 [8192, 2048], P(None, 'tp'), may hold values from -0.0625 to 0.0625
- w_out: bfloat16 [8192, 8192], P('tp'), may hold values from -0.375 to 0.375
- key_cache: bfloat16 [512, 16, 128, 256], P('inst', 'tp')
- lengths: int32 [512], replicated, may hold values from 1 to 256, as said below
- moved_slots: int32 [8, 8], replicated, may hold values from 0 to 63, as said below
- partner_mask: int32 [8], replicated, may hold values from 1 to 7
Outputs:
- attention_out: bfloat16 [2, 512, 8192], P(None, 'inst', 'tp')
- arrived: bfloat16 [64, 16, 128, 256], P('inst', 'tp')
Inputs may be any that keep to these rules, and one draw needn't show every extreme that they name: `lengths`: some request has 256 cached tokens and some has 1. `moved_slots`: the 8 slots of one instance are distinct.
All inputs are finite; a program needn't handle non-finite values.
Results may differ from a plain program's by a relative error of at most 0.012.
The roundings to bfloat16 on the way count: a program that leaves them out, or rounds other values in their place, can miss the bound.
Values may be sent and summed in bfloat16 or wider, within the bound.
No kernel may reach another device: no remote copies, remote signals or barrier semaphores. Data moves between devices by JAX's collectives and lax.ppermute only.
A program may use at most 128 MiB of HBM per device.

v0:
```python
from functools import reduce
import math

import jax
import jax.numpy as jnp
from jax import lax
from jax.sharding import PartitionSpec as P

KVH = 8


eps_norm = 1e-05
rope_base = 500000.0
floor_score = -1e30


def from_partner(block, axis, bit):
    count = lax.axis_size(axis)
    route = []
    for low in range(count):
        high = low | 1 << bit
        if high != low and high < count:
            route += [(low, high), (high, low)]
    return lax.ppermute(block, axis, route)


def as_sent(value):

    def short(part):
        return part.astype(jnp.bfloat16) if part.dtype == jnp.float32 else part

    return jax.tree.map(short, value)


def rotary(vectors, positions):
    half_dim = vectors.shape[-1] // 2
    frequency = rope_base ** (-(jnp.arange(half_dim, dtype=jnp.float32) * 2.0) / vectors.shape[-1])
    angles = positions.astype(jnp.float32)[..., None] * frequency
    cosine = jnp.cos(angles)[..., None, :]
    sine_part = jnp.sin(angles)[..., None, :]
    first_half = vectors[..., :half_dim]
    second_half = vectors[..., half_dim:]
    return jnp.concatenate(
        [
            first_half * cosine - second_half * sine_part,
            second_half * cosine + first_half * sine_part,
        ],
        -1,
    )


def block_terms(queries, block, start, length_rows):
    head_dim = queries.shape[-1]
    block_len = block.shape[1]
    scores = jnp.einsum(
        "rhd,rtd->rht", queries, block[..., :head_dim], preferred_element_type=jnp.float32
    ) / math.sqrt(head_dim)
    places = start + jnp.arange(block_len, dtype=jnp.int32)
    visible = (places[None, :] < length_rows[:, None])[:, None, :]
    scores = jnp.where(visible, scores, floor_score)
    block_max = jnp.max(scores, -1)
    weights = jnp.where(visible, jnp.exp(scores - block_max[..., None]), 0.0).astype(jnp.bfloat16)
    block_sum = jnp.sum(weights.astype(jnp.float32), -1)
    block_mix = jnp.einsum(
        "rht,rtd->rhd", weights, block[..., head_dim:], preferred_element_type=jnp.float32
    )
    return (block_max, block_sum, block_mix)


def fresh_terms(queries, fresh_kv):
    head_dim = queries.shape[-1]
    score = jnp.einsum(
        "rhd,rd->rh", queries, fresh_kv[:, :head_dim], preferred_element_type=jnp.float32
    ) / math.sqrt(head_dim)
    block_mix = jnp.broadcast_to(fresh_kv[:, None, head_dim:].astype(jnp.float32), queries.shape)
    return (score, jnp.ones_like(score), block_mix)


def combine(pieces):
    overall_max = reduce(jnp.maximum, [piece[0] for piece in pieces])
    numerator = reduce(
        jnp.add, [jnp.exp(piece[0] - overall_max)[..., None] * piece[2] for piece in pieces]
    )
    denominator = reduce(jnp.add, [jnp.exp(piece[0] - overall_max) * piece[1] for piece in pieces])
    return numerator / denominator[..., None]


def shards(
    x_steps, norm_gain, w_query, w_keyval, w_out, key_cache, lengths, moved_slots, partner_mask
):
    row_count = x_steps.shape[1]
    head_dim = key_cache.shape[-1] // 2
    block_len = key_cache.shape[2]
    group_size = lax.axis_size("tp") // KVH
    member = lax.axis_index("tp") % group_size
    instance = lax.axis_index("inst")
    own_heads = w_query.shape[1] // head_dim
    own_lengths = lax.dynamic_slice_in_dim(lengths, instance * row_count, row_count)

    def collect(value, swapper):
        stacked = jax.tree.map(lambda leaf: leaf[None], value)
        received = swapper(stacked, 0)
        low_side = member >> 0 & 1 == 0
        stacked = jax.tree.map(
            lambda mine_part, their_part: jnp.where(
                low_side,
                jnp.concatenate([mine_part, their_part], 0),
                jnp.concatenate([their_part, mine_part], 0),
            ),
            stacked,
            received,
        )
        return stacked

    def decode(step_index, positions, cache_rows, length_rows, earlier):
        gathered = lax.all_gather(x_steps[step_index], "tp", axis=1, tiled=True)
        widened = gathered.astype(jnp.float32)
        normed = (
            widened
            * lax.rsqrt(jnp.mean(widened * widened, -1, keepdims=True) + eps_norm)
            * norm_gain
        ).astype(jnp.bfloat16)
        query_raw = jnp.dot(normed, w_query, preferred_element_type=jnp.float32)
        keyval_raw = jnp.dot(normed, w_keyval, preferred_element_type=jnp.float32)
        joined = collect(
            jnp.concatenate([query_raw, keyval_raw], 1),
            lambda value, bit_index: from_partner(value, "tp", bit_index),
        )
        query_width = own_heads * head_dim
        query_all = jnp.moveaxis(joined[:, :, :query_width], 0, 1).reshape(
            row_count, group_size * own_heads, head_dim
        )
        keyval = jnp.moveaxis(joined[:, :, query_width:], 0, 1).reshape(row_count, 2 * head_dim)
        queries = rotary(query_all, positions).astype(jnp.bfloat16)
        partial_value = block_terms(queries, cache_rows[:, 0], member * block_len, length_rows)
        shared = collect(
            partial_value, lambda value, bit_index: from_partner(value, "tp", bit_index)
        )
        own_queries = lax.dynamic_slice_in_dim(queries, member * own_heads, own_heads, 1)
        pieces = [
            tuple(
                (
                    lax.dynamic_slice_in_dim(
                        member_part[block_index], member * own_heads, own_heads, 1
                    )
                    for member_part in shared
                )
            )
            for block_index in range(group_size)
        ]
        fresh_kv = jnp.concatenate(
            [rotary(keyval[:, None, :head_dim], positions)[:, 0], keyval[:, head_dim:]], -1
        ).astype(jnp.bfloat16)
        for fresh_item in earlier + [fresh_kv]:
            pieces.append(fresh_terms(own_queries, fresh_item))
        attended = combine(pieces).reshape(row_count, own_heads * head_dim).astype(jnp.bfloat16)
        head_terms = jnp.dot(attended, w_out, preferred_element_type=jnp.float32)
        return (
            lax.psum_scatter(head_terms, "tp", scatter_dimension=1, tiled=True).astype(
                jnp.bfloat16
            ),
            fresh_kv,
        )

    first_out, first_fresh = decode(0, own_lengths, key_cache, own_lengths, [])
    move_count = moved_slots.shape[1]
    move_ids = jnp.arange(move_count, dtype=jnp.int32)
    partner = jnp.bitwise_xor(instance, partner_mask)
    slots_self = moved_slots[instance]
    slots_partner = moved_slots[partner, move_ids]
    payload = (key_cache[slots_self], first_fresh[slots_self])
    moving = payload
    for bit_index in range(lax.axis_size("inst").bit_length() - 1):
        received = jax.tree.map(
            lambda part, own: part.astype(own.dtype),
            from_partner(as_sent(moving), "inst", bit_index),
            moving,
        )
        use_swap = partner_mask >> bit_index & 1 == 1
        moving = jax.tree.map(
            lambda their_part, mine_part: jnp.where(
                use_swap.reshape((move_count,) + (1,) * (mine_part.ndim - 1)), their_part, mine_part
            ),
            received,
            moving,
        )
    arrived_rows, arrived_fresh = moving
    cache_next = key_cache.at[slots_self].set(arrived_rows)
    fresh_next = first_fresh.at[slots_self].set(arrived_fresh)
    length_next = own_lengths.at[slots_self].set(lengths[partner * row_count + slots_partner])
    second_out, unused = decode(1, length_next + 1, cache_next, length_next, [fresh_next])
    return (jnp.stack([first_out, second_out]), arrived_rows)


def solution(mesh):
    placed = (
        P(None, "inst", "tp"),
        P(),
        P(None, "tp"),
        P(None, "tp"),
        P("tp", None),
        P("inst", "tp", None, None),
        P(),
        P(),
        P(),
    )
    return jax.shard_map(
        shards,
        mesh=mesh,
        in_specs=placed,
        out_specs=(P(None, "inst", "tp"), P("inst", "tp", None, None)),
        check_vma=False,
    )
```

profile of v0, /device:TPU:0, one launch (start us, length us, event | category | flops | bytes accessed | tf_op | source)
XLA Modules:
  0.0 302.4 jit_solution(13148248503262133347)
XLA Ops:
  7.3 4.8 %copy.140 = bf16[64,1,128,256]{3,2,1,0:T(8,128)(2,1)} copy(bf16[64,1,128,256]{3,2,1,0:T(8,128)(2,1)} %param.14) | data formatting | bytes 8388608
  12.9 2.8 gather_fusion.2
  15.6 1.7 collective-permute-start.5
  18.1 11.8 %collective-permute-done.5 = bf16[8,1,128,256]{3,2,0,1:T(8,128)(2,1)S(1)} collective-permute-done((bf16[8,1,128,256]{3,2,0,1:T(8,128)(2,1)S(1)}, bf16[8,1,128,256]{3,2,0,1:T(8,128)(2,1)S(1)}, u32[]{:S(2)}, u32[]{:S(2)}) %collective-permute-start.5) | collective-permute-done | bytes 524320 | tf_op jit(solution)/shard_map/ppermute | solution.py:24
  30.7 1.2 broadcast_select_fusion
  31.9 2.3 collective-permute-start.6
  35.6 9.7 %collective-permute-done.6 = bf16[8,1,128,256]{3,2,0,1:T(8,128)(2,1)S(1)} collective-permute-done((bf16[8,1,128,256]{3,2,0,1:T(8,128)(2,1)S(1)}, bf16[8,1,128,256]{3,2,0,1:T(8,128)(2,1)S(1)}, u32[]{:S(2)}, u32[]{:S(2)}) %collective-permute-start.6) | collective-permute-done | bytes 524320 | tf_op jit(solution)/shard_map/ppermute | solution.py:24
  46.1 1.2 broadcast_select_fusion.1
  47.3 3.8 %collective-permute-start.7 = (bf16[8,1,128,256]{3,2,0,1:T(8,128)(2,1)S(1)}, bf16[8,1,128,256]{3,2,0,1:T(8,128)(2,1)S(1)}, u32[]{:S(2)}, u32[]{:S(2)}) collective-permute-start(bf16[8,1,128,256]{3,2,0,1:T(8,128)(2,1)S(1)} %broadcast_select_fusion.1), channel_id=1, source_target_pairs={{0,64},{64,0},{16,80},{80,16},{32,96},{96,32},{48,112},{112,48},{1... | collective-permute-start | bytes 1572872 | tf_op jit(solution)/shard_map/ppermute | solution.py:24
  51.9 9.4 %collective-permute-done.7 = bf16[8,1,128,256]{3,2,0,1:T(8,128)(2,1)S(1)} collective-permute-done((bf16[8,1,128,256]{3,2,0,1:T(8,128)(2,1)S(1)}, bf16[8,1,128,256]{3,2,0,1:T(8,128)(2,1)S(1)}, u32[]{:S(2)}, u32[]{:S(2)}) %collective-permute-start.7) | collective-permute-done | bytes 524320 | tf_op jit(solution)/shard_map/ppermute | solution.py:24
  62.2 1.6 fusion
  63.9 1.7 fusion.36
  65.7 5.0 %fusion.38 = f32[64,512]{1,0:T(8,128)S(1)} fusion(bf16[8192,512]{1,0:T(8,128)(2,1)} %param.11, bf16[1,64,8192]{2,1,0:T(8,128)(2,1)S(1)} %copy-done.3, f32[8192]{0:T(1024)S(1)} %copy-done.5, f32[64]{0:T(128)S(1)} %add_rsqrt_fusion.1), kind=kOutput, calls=%fused_computation.41 | convolution fusion | flops 538968064 | bytes 9601280 | tf_op jit(solution)/shard_map/dot_general | solution.py:123
  70.8 32.6 %all-gather.7.cloned.1.call-done = bf16[1,64,8192]{2,1,0:T(8,128)(2,1)} async-done(((bf16[1,64,512]{2,1,0:T(8,128)(2,1)}), bf16[1,64,8192]{2,1,0:T(8,128)(2,1)}) %all-gather.7.cloned.1.call-update) | async-done | bytes 1048592 | tf_op jit(solution)/shard_map/all_gather | solution.py:116
  103.5 1.6 fusion.3
  105.1 5.0 %fusion.34 = f32[64,512]{1,0:T(8,128)S(1)} fusion(bf16[8192,512]{1,0:T(8,128)(2,1)} %param.11, bf16[1,64,8192]{2,1,0:T(8,128)(2,1)S(1)} %copy-done.4, f32[64]{0:T(128)S(1)} %add_rsqrt_fusion, f32[8192]{0:T(1024)S(1)} %copy-done.5), kind=kOutput, calls=%fused_computation.39 | convolution fusion | flops 538968064 | bytes 9601280 | tf_op jit(solution)/shard_map/dot_general | solution.py:123
  112.9 3.6 %fusion.125 = (f32[64,8]{1,0:T(8,128)}, f32[64,8,128]{2,1,0:T(8,128)S(1)}) fusion(bf16[64,128,256]{2,1,0:T(8,128)(2,1)} %bitcast.244, bf16[64,8,64]{2,1,0:T(8,128)(2,1)S(1)} %get-tuple-element.32, bf16[64,8,64]{2,1,0:T(8,128)(2,1)S(1)} %get-tuple-element.31, pred[64,128]{1,0:T(8,128)(4,1)S(1)} %get-tuple-element.59), kind=kOutput, calls=%fused_computation.222 | convolution fusion | flops 17235456 | bytes 2500608 | tf_op jit(solution)/shard_map/rhd,rtd->rht/dot_general | solution.py:55
  116.5 2.3 fusion.26
  119.8 1.4 copy.52
  121.2 1.6 convert_reduce_fusion.1
  122.8 1.2 maximum_select_fusion.3
  125.6 2.6 scatter_fusion.1
  129.1 2.9 fusion.124
  132.1 2.4 fusion.29
  141.9 6.3 %fusion.52 = f32[64,8192]{1,0:T(8,128)} fusion(bf16[512,8192]{1,0:T(8,128)(2,1)} %param.13, f32[8,8,4,128]{3,2,1,0:T(4,128)S(1)} %bitcast.257, f32[8,8,4,128]{3,2,1,0:T(4,128)S(1)} %bitcast.260, f32[8,8,4,128]{3,2,1,0:T(4,128)S(1)} %bitcast.250, f32[8,8,4,128]{3,2,1,0:T(4,128)S(1)} %bitcast.255, f32[8,8,4,128]{3,2,1,0:T(4,128)S(1)} %bitcast.251, ...), kind=kOutput, calls=%fused_computation.80 | convolution fusion | flops 537067520 | bytes 11272192 | tf_op jit(solution)/shard_map/dot_general | solution.py:157
  149.0 1.6 collective-permute-start.10
  150.6 2.0 collective-permute-done.10
  152.7 3.2 %collective-permute-start.11 = (bf16[8,256]{1,0:T(8,128)(2,1)S(1)}, bf16[8,256]{1,0:T(8,128)(2,1)S(1)}, u32[]{:S(2)}, u32[]{:S(2)}) collective-permute-start(bf16[8,256]{1,0:T(8,128)(2,1)S(1)} %broadcast_select_fusion.4), channel_id=1, source_target_pairs={{0,64},{64,0},{16,80},{80,16},{32,96},{96,32},{48,112},{112,48},{1... | collective-permute-start | bytes 12296 | tf_op jit(solution)/shard_map/ppermute | solution.py:24
  155.9 1.9 collective-permute-done.11
  160.3 6.5 %fusion.54 = f32[64,8192]{1,0:T(8,128)} fusion(bf16[512,8192]{1,0:T(8,128)(2,1)} %param.13, f32[8,8,4,128]{3,2,1,0:T(4,128)S(1)} %bitcast.256, f32[8,8,4,128]{3,2,1,0:T(4,128)S(1)} %bitcast.259, f32[8,8,4,128]{3,2,1,0:T(4,128)S(1)} %bitcast.258, f32[8,8,4,128]{3,2,1,0:T(4,128)S(1)} %bitcast.248, f32[8,8,4,128]{3,2,1,0:T(4,128)S(1)} %bitcast.254, ...), kind=kOutput, calls=%fused_computation.81 | convolution fusion | flops 537100288 | bytes 11403264 | tf_op jit(solution)/shard_map/dot_general | solution.py:157
  166.9 53.2 %reduce-scatter.3.cloned.1.call-done = f32[64,512]{1,0:T(8,128)} async-done(((f32[64,8192]{1,0:T(8,128)}), f32[64,512]{1,0:T(8,128)}) %reduce-scatter.3.cloned.1.call-update) | async-done | bytes 131088 | tf_op jit(solution)/shard_map/reduce_scatter | solution.py:159
  221.0 73.2 %reduce-scatter.5.cloned.1.call-done = f32[64,512]{1,0:T(8,128)} async-done(((f32[64,8192]{1,0:T(8,128)}), f32[64,512]{1,0:T(8,128)}) %reduce-scatter.5.cloned.1.call-update) | async-done | bytes 131088 | tf_op jit(solution)/shard_map/reduce_scatter | solution.py:159
  (191 shorter events, 25.6 us)
Async XLA Ops:
  7.2 56.7 %copy-start = (bf16[8192,128]{1,0:T(8,128)(2,1)S(1)}, bf16[8192,128]{1,0:T(8,128)(2,1)}, u32[]{:S(2)}) copy-start(bf16[8192,128]{1,0:T(8,128)(2,1)} %param.12) | copy-start | bytes 6291460
  7.2 10.2 %copy-start.33 = (s32[8]{0:T(128)S(1)}, s32[8]{0:T(128)}, u32[]{:S(2)}) copy-start(s32[8]{0:T(128)} %param.17) | copy-start | bytes 100
  7.2 55.0 %all-gather.5.cloned.1.call-start = ((), (), s32[]{:S(2)}) async-start(), calls=%async_computation.4 | async-start | bytes 1114112 | tf_op jit(solution)/shard_map/all_gather | solution.py:116
  12.1 22.1 %copy-start.1 = (s32[512]{0:T(512)S(1)}, s32[512]{0:T(512)}, u32[]{:S(2)}) copy-start(s32[512]{0:T(512)} %param.15) | copy-start | bytes 6148
  12.7 90.7 %all-gather.7.cloned.1.call-start = ((), (), s32[]{:S(2)}) async-start(), calls=%async_computation.5 | async-start | bytes 1114112 | tf_op jit(solution)/shard_map/all_gather | solution.py:116
  12.8 22.7 %copy-start.20 = (s32[8]{0:T(128)}, s32[8]{0:T(128)S(1)}, u32[]{:S(2)}) copy-start(s32[8]{0:T(128)S(1)} %fusion.103) | copy-start | bytes 100
  15.6 14.3 %collective-permute-start.5 = (bf16[8,1,128,256]{3,2,0,1:T(8,128)(2,1)S(1)}, bf16[8,1,128,256]{3,2,0,1:T(8,128)(2,1)S(1)}, u32[]{:S(2)}, u32[]{:S(2)}) collective-permute-start(bf16[8,1,128,256]{3,2,0,1:T(8,128)(2,1)S(1)} %bitcast.247), channel_id=1, source_target_pairs={{0,16},{16,0},{32,48},{48,32},{64,80},{80,64},{96,112},{112,96},{1... | collective-permute-start | bytes 1572872 | tf_op jit(solution)/shard_map/ppermute | solution.py:24
  17.3 202.8 %reduce-scatter.3.cloned.1.call-start = ((), (), s32[]{:S(2)}) async-start(), calls=%async_computation.2 | async-start | bytes 2228224 | tf_op jit(solution)/shard_map/reduce_scatter | solution.py:159
  18.1 16.2 %copy-start.25 = (pred[8]{0:T(512)(128)(4,1)}, pred[8]{0:T(512)(128)(4,1)S(1)}, u32[]{:S(2)}) copy-start(pred[8]{0:T(512)(128)(4,1)S(1)} %get-tuple-element.64) | copy-start | bytes 28
  18.1 52.6 %copy-start.23 = (pred[8]{0:T(512)(128)(4,1)}, pred[8]{0:T(512)(128)(4,1)S(1)}, u32[]{:S(2)}) copy-start(pred[8]{0:T(512)(128)(4,1)S(1)} %get-tuple-element.65) | copy-start | bytes 28
  18.1 52.6 %copy-start.27 = (pred[8]{0:T(512)(128)(4,1)}, pred[8]{0:T(512)(128)(4,1)S(1)}, u32[]{:S(2)}) copy-start(pred[8]{0:T(512)(128)(4,1)S(1)} %get-tuple-element.63) | copy-start | bytes 28
  31.9 13.4 %collective-permute-start.6 = (bf16[8,1,128,256]{3,2,0,1:T(8,128)(2,1)S(1)}, bf16[8,1,128,256]{3,2,0,1:T(8,128)(2,1)S(1)}, u32[]{:S(2)}, u32[]{:S(2)}) collective-permute-start(bf16[8,1,128,256]{3,2,0,1:T(8,128)(2,1)S(1)} %broadcast_select_fusion), channel_id=1, source_target_pairs={{0,32},{32,0},{16,48},{48,16},{64,96},{96,64},{80,112},{112,80},{1... | collective-permute-start | bytes 1572872 | tf_op jit(solution)/shard_map/ppermute | solution.py:24
  34.2 28.0 %copy-start.21 = (f32[64]{0:T(128)}, f32[64]{0:T(128)S(1)}, u32[]{:S(2)}) copy-start(f32[64]{0:T(128)S(1)} %get-tuple-element.23) | copy-start | bytes 772
  46.1 17.8 %copy-start.5 = (f32[8192]{0:T(1024)S(1)}, f32[8192]{0:T(1024)}, u32[]{:S(2)}) copy-start(f32[8192]{0:T(1024)} %param.10) | copy-start | bytes 98308
  47.3 14.0 %collective-permute-start.7 = (bf16[8,1,128,256]{3,2,0,1:T(8,128)(2,1)S(1)}, bf16[8,1,128,256]{3,2,0,1:T(8,128)(2,1)S(1)}, u32[]{:S(2)}, u32[]{:S(2)}) collective-permute-start(bf16[8,1,128,256]{3,2,0,1:T(8,128)(2,1)S(1)} %broadcast_select_fusion.1), channel_id=1, source_target_pairs={{0,64},{64,0},{16,80},{80,16},{32,96},{96,32},{48,112},{112,48},{1... | collective-permute-start | bytes 1572872 | tf_op jit(solution)/shard_map/ppermute | solution.py:24
  51.1 14.6 %copy-start.29 = (f32[64]{0:T(128)}, f32[64]{0:T(128)S(1)}, u32[]{:S(2)}) copy-start(f32[64]{0:T(128)S(1)} %add_convert_fusion.2) | copy-start | bytes 772
  51.1 14.6 %copy-start.31 = (f32[64]{0:T(128)}, f32[64]{0:T(128)S(1)}, u32[]{:S(2)}) copy-start(f32[64]{0:T(128)S(1)} %multiply_power_fusion) | copy-start | bytes 772
  70.7 40.9 %collective-permute-start = (f32[1,64,640]{2,1,0:T(8,128)S(1)}, f32[1,64,640]{2,1,0:T(8,128)S(1)}, u32[]{:S(2)}, u32[]{:S(2)}) collective-permute-start(f32[1,64,640]{2,1,0:T(8,128)S(1)} %maximum_bitcast_fusion), channel_id=1, source_target_pairs={{0,1},{1,0},{2,3},{3,2},{4,5},{5,4},{6,7},{7,6},{8,9},{9,8},{10,11... | collective-permute-start | bytes 491528 | tf_op jit(solution)/shard_map/ppermute | solution.py:24
  111.4 11.4 %collective-permute-start.4 = (f32[1,64,640]{2,1,0:T(8,128)}, f32[1,64,640]{2,1,0:T(8,128)}, u32[]{:S(2)}, u32[]{:S(2)}) collective-permute-start(f32[1,64,640]{2,1,0:T(8,128)} %maximum_bitcast_fusion.1), channel_id=1, source_target_pairs={{0,1},{1,0},{2,3},{3,2},{4,5},{5,4},{6,7},{7,6},{8,9},{9,8},{10,11... | collective-permute-start | bytes 491528 | tf_op jit(solution)/shard_map/ppermute | solution.py:24
  119.5 18.7 %collective-permute-start.1 = (f32[1,64,8]{2,1,0:T(8,128)}, f32[1,64,8]{2,1,0:T(8,128)}, u32[]{:S(2)}, u32[]{:S(2)}) collective-permute-start(f32[1,64,8]{2,1,0:T(8,128)} %bitcast.5), channel_id=1, source_target_pairs={{0,1},{1,0},{2,3},{3,2},{4,5},{5,4},{6,7},{7,6},{8,9},{9,8},{10,11... | collective-permute-start | bytes 6152 | tf_op jit(solution)/shard_map/ppermute | solution.py:24
  124.6 15.7 %collective-permute-start.2 = (f32[1,64,8,128]{3,2,1,0:T(8,128)S(1)}, f32[1,64,8,128]{3,2,1,0:T(8,128)}, u32[]{:S(2)}, u32[]{:S(2)}) collective-permute-start(f32[1,64,8,128]{3,2,1,0:T(8,128)S(1)} %fusion.26), channel_id=1, source_target_pairs={{0,1},{1,0},{2,3},{3,2},{4,5},{5,4},{6,7},{7,6},{8,9},{9,8},{10,11... | collective-permute-start | bytes 786440 | tf_op jit(solution)/shard_map/ppermute | solution.py:24
  132.1 7.5 %copy-start.18 = (f32[1,64,8]{1,2,0:T(8,128)S(1)}, f32[1,64,8]{1,2,0:T(8,128)}, u32[]{:S(2)}) copy-start(f32[1,64,8]{1,2,0:T(8,128)} %copy.52) | copy-start | bytes 6148
  132.1 8.1 %copy-start.15 = (f32[64,128]{1,0:T(8,128)S(1)}, f32[64,128]{1,0:T(8,128)}, u32[]{:S(2)}) copy-start(f32[64,128]{1,0:T(8,128)} %get-tuple-element.12) | copy-start | bytes 98308
  135.7 2.1 collective-permute-start.3
  136.0 4.1 %collective-permute-start.13 = (f32[1,64,8]{2,1,0:T(8,128)S(1)}, f32[1,64,8]{2,1,0:T(8,128)S(1)}, u32[]{:S(2)}, u32[]{:S(2)}) collective-permute-start(f32[1,64,8]{2,1,0:T(8,128)S(1)} %bitcast.263), channel_id=1, source_target_pairs={{0,1},{1,0},{2,3},{3,2},{4,5},{5,4},{6,7},{7,6},{8,9},{9,8},{10,11... | collective-permute-start | bytes 6152 | tf_op jit(solution)/shard_map/ppermute | solution.py:24
  136.2 3.9 %collective-permute-start.8 = (f32[1,64,8]{2,1,0:T(8,128)S(1)}, f32[1,64,8]{2,1,0:T(8,128)S(1)}, u32[]{:S(2)}, u32[]{:S(2)}) collective-permute-start(f32[1,64,8]{2,1,0:T(8,128)S(1)} %bitcast.261), channel_id=1, source_target_pairs={{0,1},{1,0},{2,3},{3,2},{4,5},{5,4},{6,7},{7,6},{8,9},{9,8},{10,11... | collective-permute-start | bytes 6152 | tf_op jit(solution)/shard_map/ppermute | solution.py:24
  137.8 22.0 %collective-permute-start.12 = (f32[1,64,8,128]{3,2,1,0:T(8,128)S(1)}, f32[1,64,8,128]{3,2,1,0:T(8,128)S(1)}, u32[]{:S(2)}, u32[]{:S(2)}) collective-permute-start(f32[1,64,8,128]{3,2,1,0:T(8,128)S(1)} %fusion.29), channel_id=1, source_target_pairs={{0,1},{1,0},{2,3},{3,2},{4,5},{5,4},{6,7},{7,6},{8,9},{9,8},{10,11... | collective-permute-start | bytes 786440 | tf_op jit(solution)/shard_map/ppermute | solution.py:24
  138.2 10.2 %collective-permute-start.9 = (bf16[8,256]{1,0:T(8,128)(2,1)S(1)}, bf16[8,256]{1,0:T(8,128)(2,1)S(1)}, u32[]{:S(2)}, u32[]{:S(2)}) collective-permute-start(bf16[8,256]{1,0:T(8,128)(2,1)S(1)} %gather_fusion.3), channel_id=1, source_target_pairs={{0,16},{16,0},{32,48},{48,32},{64,80},{80,64},{96,112},{112,96},{1... | collective-permute-start | bytes 12296 | tf_op jit(solution)/shard_map/ppermute | solution.py:24
  148.3 9.5 %copy-start.28 = (pred[8]{0:T(512)(128)(4,1)S(1)}, pred[8]{0:T(512)(128)(4,1)}, u32[]{:S(2)}) copy-start(pred[8]{0:T(512)(128)(4,1)} %copy-done.27) | copy-start | bytes 28
  148.3 145.9 %reduce-scatter.5.cloned.1.call-start = ((), (), s32[]{:S(2)}) async-start(), calls=%async_computation.3 | async-start | bytes 2228224 | tf_op jit(solution)/shard_map/reduce_scatter | solution.py:159
  149.0 3.6 %collective-permute-start.10 = (bf16[8,256]{1,0:T(8,128)(2,1)S(1)}, bf16[8,256]{1,0:T(8,128)(2,1)S(1)}, u32[]{:S(2)}, u32[]{:S(2)}) collective-permute-start(bf16[8,256]{1,0:T(8,128)(2,1)S(1)} %broadcast_select_fusion.3), channel_id=1, source_target_pairs={{0,32},{32,0},{16,48},{48,16},{64,96},{96,64},{80,112},{112,80},{1... | collective-permute-start | bytes 12296 | tf_op jit(solution)/shard_map/ppermute | solution.py:24
  152.7 5.1 %collective-permute-start.11 = (bf16[8,256]{1,0:T(8,128)(2,1)S(1)}, bf16[8,256]{1,0:T(8,128)(2,1)S(1)}, u32[]{:S(2)}, u32[]{:S(2)}) collective-permute-start(bf16[8,256]{1,0:T(8,128)(2,1)S(1)} %broadcast_select_fusion.4), channel_id=1, source_target_pairs={{0,64},{64,0},{16,80},{80,16},{32,96},{96,32},{48,112},{112,48},{1... | collective-permute-start | bytes 12296 | tf_op jit(solution)/shard_map/ppermute | solution.py:24
  (20 other events, 63.7 us)
Sparse Core Ops, SparseCore 0:
  12.9 45.5 all-gather.4
  60.7 42.6 all-gather.6
  148.4 71.6 reduce-scatter.2
  224.3 69.8 reduce-scatter.4
where the time goes:
time: 303 us; the launch traced here: 302 us
  waiting for transfers between devices  194 us (64%)
  matrix products  37 us (12%)
  local copies, waits for them, and re-layouts  22.5 us (7%)
  other arithmetic  18.7 us (6%)
  starting transfers between devices  15.5 us (5%)
  between operations  14.6 us (5%)
    reduce_scatter x2, waiting for transfers between devices, decode(): lax.psum_scatter(head_terms, 'tp', scatter_dimension=1, tiled=True)  126 us
    ppermute x14, waiting for transfers between devices, from_partner(): return lax.ppermute(block, axis, route)  34.8 us
    all_gather x2, waiting for transfers between devices, decode(): gathered = lax.all_gather(x_steps[step_index], 'tp', axis=1, tiled=True)  32.6 us
    ppermute x14, starting transfers between devices, from_partner(): return lax.ppermute(block, axis, route)  15.4 us
    dot_general x2, matrix products, decode(): head_terms = jnp.dot(attended, w_out, preferred_element_type=jnp.float32)  12.9 us
    dot_general x2, matrix products, decode(): query_raw = jnp.dot(normed, w_query, preferred_element_type=jnp.float32)  10 us
    unnamed x70, local copies, waits for them, and re-layouts  7.1 us
    dot_general x2, matrix products, block_terms(): jnp.einsum('rhd,rtd->rht', queries, block[..., :head_dim], preferred_elem...  6.47 us
  transfers between devices with their start and end apart: 18, of which 8 were waited for; matrix products, arithmetic and copies ran while one was open for 23% of the time, Pallas kernels for 0%

commit v1 on v0

v1 whole, which is shorter than its diff:
```python
import functools
import math

import jax
import jax.numpy as jnp
from jax import lax
from jax.experimental import pallas as pl
from jax.experimental.pallas import tpu as pltpu
from jax.sharding import PartitionSpec as P

BF = jnp.bfloat16
F32 = jnp.float32
EPS = 1e-05
ROPE_BASE = 500000.0
FLOOR = -1e30
HD = 128
BLK = 128
REQ = 64
HEADS = 8
SHARD = 512
CHIPS = 8
MOVE = 8
QW = HEADS * HD
PW = QW + 2 * HD + HD
ANY = pl.BlockSpec(memory_space=pl.ANY)
VMEM = pl.BlockSpec(memory_space=pltpu.VMEM)
SMEM = pl.BlockSpec(memory_space=pltpu.SMEM)
LIMIT = 48 * 1024 * 1024


def call(body, ins, outs, scratch, out_shapes, flops, moved):
    return pl.pallas_call(
        body,
        out_shape=out_shapes,
        in_specs=ins,
        out_specs=outs,
        scratch_shapes=scratch,
        compiler_params=pltpu.CompilerParams(vmem_limit_bytes=LIMIT),
        cost_estimate=pl.CostEstimate(flops=flops, bytes_accessed=moved, transcendentals=0),
    )


def shape(dims, kind):
    return jax.ShapeDtypeStruct(dims, kind)


def swap(value, axis, mask):
    count = lax.axis_size(axis)
    return lax.ppermute(value, axis, [(i, i ^ mask) for i in range(count)])


def pick_qkv(where, wq, wkv, wq_out, wkv_out, sems):
    other = 1 - where[0] % 2
    copies = []
    for b in range(CHIPS):
        rows = pl.ds(pl.multiple_of((2 * b + other) * SHARD, SHARD), SHARD)
        copies.append(pltpu.make_async_copy(wq.at[rows, :], wq_out.at[b], sems.at[2 * b]))
        copies.append(pltpu.make_async_copy(wkv.at[rows, :], wkv_out.at[b], sems.at[2 * b + 1]))
    for copy in copies:
        copy.start()
    for copy in copies:
        copy.wait()


def pick_out(where, wo, wo_out, sems):
    other = 1 - where[0] % 2
    copies = []
    for b in range(CHIPS):
        cols = pl.ds(pl.multiple_of((2 * b + other) * SHARD, SHARD), SHARD)
        copies.append(pltpu.make_async_copy(wo.at[:, cols], wo_out.at[b], sems.at[b]))
    for copy in copies:
        copy.start()
    for copy in copies:
        copy.wait()


def pick_rows(slots, cache, rows_a, rows_b, sems):
    half = MOVE // 2
    copies = []
    for j in range(MOVE):
        out = rows_a.at[j] if j < half else rows_b.at[j - half]
        copies.append(pltpu.make_async_copy(cache.at[slots[j]], out, sems.at[j]))
    for copy in copies:
        copy.start()
    for copy in copies:
        copy.wait()


def project(where, *refs):
    xs = refs[:CHIPS]
    gain, wq, wkv, wqs, wkvs, out, buf, acc, sems = refs[CHIPS:]
    me = where[0]
    core = me % 2
    pending = []
    for i in range(CHIPS):
        src = me ^ (2 * i)
        rows = pl.ds(pl.multiple_of(src * SHARD, SHARD), SHARD)
        group = [
            pltpu.make_async_copy(wq.at[rows, :], buf.at[i, :, pl.ds(0, SHARD)], sems.at[i, 0]),
            pltpu.make_async_copy(wqs.at[src // 2], buf.at[i, :, pl.ds(SHARD, SHARD)], sems.at[i, 1]),
            pltpu.make_async_copy(wkv.at[rows, :], buf.at[i, :, pl.ds(QW, HD)], sems.at[i, 2]),
            pltpu.make_async_copy(wkvs.at[src // 2], buf.at[i, :, pl.ds(QW + HD, HD)], sems.at[i, 3]),
        ]
        for copy in group:
            copy.start()
        pending.append(group)
    squares = None
    for i in range(CHIPS):
        src = me ^ (2 * i)
        wide = xs[i][...].astype(F32)
        scaled = (wide * gain[pl.ds(src, 1), :]).astype(BF)
        sq = wide * wide
        part = sq[:, :HD] + sq[:, HD : 2 * HD] + sq[:, 2 * HD : 3 * HD] + sq[:, 3 * HD :]
        squares = part if squares is None else squares + part
        for copy in pending[i]:
            copy.wait()
        term = jnp.dot(scaled, buf[i], preferred_element_type=F32)
        if i == 0:
            acc[...] = term
        else:
            acc[...] += term
    mine = core * SHARD
    theirs = SHARD - mine
    out[:, pl.ds(pl.multiple_of(mine, SHARD), SHARD)] = acc[:, :SHARD]
    out[:, pl.ds(pl.multiple_of(theirs, SHARD), SHARD)] = acc[:, SHARD:QW]
    out[:, pl.ds(pl.multiple_of(QW + core * HD, HD), HD)] = acc[:, QW : QW + HD]
    out[:, pl.ds(pl.multiple_of(QW + HD - core * HD, HD), HD)] = acc[:, QW + HD :]
    out[:, pl.ds(QW + 2 * HD, HD)] = squares


def softmax_pair(q_pair, keys, values, len_a, len_b):
    rows = q_pair.shape[0]
    half = rows // 2
    scores = lax.dot_general(
        q_pair, keys, (((1,), (1,)), ((), ())), preferred_element_type=F32
    ) * (1.0 / math.sqrt(HD))
    lane = lax.broadcasted_iota(jnp.int32, (rows, 2 * BLK), 1)
    upper = lax.broadcasted_iota(jnp.int32, (rows, 2 * BLK), 0) >= half
    low = jnp.where(upper, BLK, 0)
    high = jnp.where(upper, BLK + len_b, len_a)
    visible = jnp.logical_and(lane >= low, lane < high)
    scores = jnp.where(visible, scores, FLOOR)
    top = jnp.max(scores, -1, keepdims=True)
    weights = jnp.where(visible, jnp.exp(scores - top), 0.0).astype(BF)
    total = jnp.sum(weights.astype(F32), -1, keepdims=True)
    mix = jnp.dot(weights, values, preferred_element_type=F32)
    return top, total, mix


def attend(step, moving, where, lens, slots, *refs):
    if moving:
        mine, recv, cosine, sine, cache, arr_a, arr_b, terms, q_out, fresh_out, kv, arr, wide, sems = refs
    else:
        mine, recv, cosine, sine, cache, terms, q_out, fresh_out, sent_out, kv, wide, sems = refs
    core = where[0] % 2
    base = core * BLK
    chunks = 4
    per = REQ // chunks
    copies = []
    for i in range(chunks):
        copies.append(
            pltpu.make_async_copy(cache.at[pl.ds(i * per, per)], kv.at[pl.ds(i * per, per)], sems.at[i])
        )
    if moving:
        half = MOVE // 2
        copies.append(pltpu.make_async_copy(arr_a, arr.at[pl.ds(0, half)], sems.at[chunks]))
        copies.append(pltpu.make_async_copy(arr_b, arr.at[pl.ds(half, half)], sems.at[chunks + 1]))
    for copy in copies:
        copy.start()
    rows = pl.ds(step * REQ, REQ)
    squares = mine[rows, pl.ds(QW + 2 * HD, HD)] + recv[rows, pl.ds(QW + 2 * HD, HD)]
    mean = jnp.sum(squares, -1, keepdims=True) * (1.0 / (2 * CHIPS * SHARD))
    scale = lax.rsqrt(mean + EPS)
    cos = cosine[...]
    sin = sine[...]

    def taken(col):
        return (mine[rows, pl.ds(col, HD)] + recv[rows, pl.ds(col, HD)]) * scale

    def turned(vec):
        return vec * cos + pltpu.roll(vec, HD // 2, 1) * sin

    for h in range(HEADS):
        q_out[pl.ds(h, REQ, stride=HEADS), :] = turned(taken(h * HD)).astype(BF).astype(F32)
    key = turned(taken(QW)).astype(BF).astype(F32)
    value = taken(QW + HD).astype(BF).astype(F32)
    wide[:, pl.ds(0, HD)] = key
    wide[:, pl.ds(HD, HD)] = value
    fresh_out[...] = wide[...]
    if not moving:
        for j in range(MOVE):
            sent_out[pl.ds(j, 1), :] = wide[pl.ds(slots[j], 1), :]

    lane8 = lax.broadcasted_iota(jnp.int32, (HEADS, HD), 1)

    def noted(stats, slot, top, total):
        stats = jnp.where(lane8 == slot, top, stats)
        return jnp.where(lane8 == slot + REQ, total, stats)

    def clipped(length):
        return jnp.clip(length - base, 0, BLK)

    def pair(p, stats):
        q_pair = q_out[pl.ds(pl.multiple_of(p * 2 * HEADS, 2 * HEADS), 2 * HEADS), :].astype(BF)
        block = kv[pl.ds(2 * p, 2)].reshape(2 * BLK, 2 * HD)
        top, total, mix = softmax_pair(
            q_pair, block[:, :HD], block[:, HD:], clipped(lens[2 * p]), clipped(lens[2 * p + 1])
        )
        terms[pl.ds(pl.multiple_of(p * 2 * HEADS, 2 * HEADS), 2 * HEADS), :] = mix
        stats = noted(stats, 2 * p, top[:HEADS], total[:HEADS])
        return noted(stats, 2 * p + 1, top[HEADS:], total[HEADS:])

    stats = jnp.zeros((HEADS, HD), F32)
    for i in range(chunks):
        copies[i].wait()
        stats = lax.fori_loop(i * per // 2, (i + 1) * per // 2, pair, stats, unroll=True)
    if moving:
        copies[chunks].wait()
        copies[chunks + 1].wait()
        for p in range(MOVE // 2):
            one, two = slots[2 * p], slots[2 * p + 1]
            at_one = pl.ds(pl.multiple_of(one * HEADS, HEADS), HEADS)
            at_two = pl.ds(pl.multiple_of(two * HEADS, HEADS), HEADS)
            q_pair = jnp.concatenate([q_out[at_one, :], q_out[at_two, :]], 0).astype(BF)
            block = arr[pl.ds(2 * p, 2)].reshape(2 * BLK, 2 * HD)
            top, total, mix = softmax_pair(
                q_pair, block[:, :HD], block[:, HD:], clipped(lens[one]), clipped(lens[two])
            )
            terms[at_one, :] = mix[:HEADS]
            terms[at_two, :] = mix[HEADS:]
            stats = noted(stats, one, top[:HEADS], total[:HEADS])
            stats = noted(stats, two, top[HEADS:], total[HEADS:])
    terms[pl.ds(REQ * HEADS, HEADS), :] = stats


def finish(where, slots, *refs):
    (t1m, t1r, q1, f1, t2m, t2r, q2, f2, came, wo, wos) = refs[:11]
    outs = refs[11 : 11 + CHIPS]
    own_buf, sib_buf, carried, flat, att, sems = refs[11 + CHIPS :]
    me = where[0]
    core = me % 2
    pending = []
    for i in range(CHIPS):
        k = 8 + 2 * i if i < 4 else 2 * (i - 4)
        dst = me ^ k
        cols = pl.ds(pl.multiple_of(dst * SHARD, SHARD), SHARD)
        group = [
            pltpu.make_async_copy(wo.at[:, cols], own_buf.at[i], sems.at[i, 0]),
            pltpu.make_async_copy(wos.at[dst // 2], sib_buf.at[i], sems.at[i, 1]),
        ]
        for copy in group:
            copy.start()
        pending.append(group)
    carried[...] = f1[...]
    for j in range(MOVE):
        carried[pl.ds(slots[j], 1), :] = came[pl.ds(j, 1), :]

    def combine(step, mine, recv, q, fresh):
        stats_m = mine[pl.ds(REQ * HEADS, HEADS), :]
        stats_r = recv[pl.ds(REQ * HEADS, HEADS), :]
        for r in range(REQ):
            at = pl.ds(r * HEADS, HEADS)
            query = q[at, :]
            tops = [stats_m[:, r : r + 1], stats_r[:, r : r + 1]]
            sums = [stats_m[:, r + REQ : r + REQ + 1], stats_r[:, r + REQ : r + REQ + 1]]
            mixes = [mine[at, :], recv[at, :]]
            for row in fresh:
                key = row[pl.ds(r, 1), pl.ds(0, HD)]
                tops.append(jnp.sum(query * key, -1, keepdims=True) * (1.0 / math.sqrt(HD)))
                sums.append(None)
                mixes.append(row[pl.ds(r, 1), pl.ds(HD, HD)])
            overall = functools.reduce(jnp.maximum, tops)
            numerator = denominator = None
            for top, total, mix in zip(tops, sums, mixes):
                factor = jnp.exp(top - overall)
                low = factor if total is None else factor * total
                numerator = factor * mix if numerator is None else numerator + factor * mix
                denominator = low if denominator is None else denominator + low
            flat[at, :] = numerator / denominator
        for h in range(HEADS):
            att[pl.ds(step * REQ, REQ), pl.ds(h * HD, HD)] = flat[
                pl.ds(h, REQ, stride=HEADS), :
            ].astype(BF)

    combine(0, t1m, t1r, q1, [f1])
    combine(1, t2m, t2r, q2, [carried, f2])
    own = att[:, pl.ds(pl.multiple_of(core * SHARD, SHARD), SHARD)]
    sib = att[:, pl.ds(pl.multiple_of(SHARD - core * SHARD, SHARD), SHARD)]
    for i in range(CHIPS):
        for copy in pending[i]:
            copy.wait()
        outs[i][...] = (
            jnp.dot(own, own_buf[i], preferred_element_type=F32)
            + jnp.dot(sib, sib_buf[i], preferred_element_type=F32)
        ).astype(BF)


def shards(
    x_steps, norm_gain, w_query, w_keyval, w_out, key_cache, lengths, moved_slots, partner_mask
):
    dma = pltpu.SemaphoreType.DMA
    me = lax.axis_index("tp")
    instance = lax.axis_index("inst")
    where = jnp.reshape(me, (1,)).astype(jnp.int32)
    cache = key_cache[:, 0]

    own_x = x_steps.reshape(2 * REQ, SHARD)
    far_x = swap(own_x, "tp", 8)
    near = [own_x] + [swap(own_x, "tp", 2 * i) for i in (1, 2, 3)]
    far = [far_x] + [swap(far_x, "tp", 2 * i) for i in (1, 2, 3)]

    wq_send, wkv_send = call(
        pick_qkv,
        [SMEM, ANY, ANY],
        [ANY, ANY],
        [dma((2 * CHIPS,))],
        [shape((CHIPS, SHARD, SHARD), BF), shape((CHIPS, SHARD, HD), BF)],
        0,
        10 << 20,
    )(where, w_query, w_keyval)
    wqs = swap(wq_send, "tp", 1)
    wkvs = swap(wkv_send, "tp", 1)
    wo_send = call(
        pick_out,
        [SMEM, ANY],
        ANY,
        [dma((CHIPS,))],
        shape((CHIPS, SHARD, SHARD), BF),
        0,
        8 << 20,
    )(where, w_out)
    wos = swap(wo_send, "tp", 1)

    move_ids = jnp.arange(MOVE, dtype=jnp.int32)
    partner = jnp.bitwise_xor(instance, partner_mask)
    slots = lax.dynamic_index_in_dim(moved_slots, instance, 0, False)
    slots_partner = moved_slots[partner, move_ids]
    own_lengths = lax.dynamic_slice_in_dim(lengths, instance * REQ, REQ)
    next_lengths = own_lengths.at[slots].set(lengths[partner * REQ + slots_partner])
    half = MOVE // 2
    rows_a, rows_b = call(
        pick_rows,
        [SMEM, ANY],
        [ANY, ANY],
        [dma((MOVE,))],
        [shape((half, BLK, 2 * HD), BF)] * 2,
        0,
        1 << 20,
    )(slots, cache)

    def hop(part, bit, masks):
        took = ((masks >> bit) & 1 == 1).reshape((-1,) + (1,) * (part.ndim - 1))
        return jnp.where(took, swap(part, "inst", 1 << bit), part)

    for bit_a, bit_b in ((1, 2), (2, 0), (0, 1)):
        rows_a = hop(rows_a, bit_a, partner_mask[:half])
        rows_b = hop(rows_b, bit_b, partner_mask[half:])
    arrived = jnp.concatenate([rows_a, rows_b], 0)[:, None]

    def tables(positions):
        frequency = ROPE_BASE ** (-(jnp.arange(HD // 2, dtype=F32) * 2.0) / HD)
        angles = positions.astype(F32)[:, None] * frequency
        cos, sin = jnp.cos(angles), jnp.sin(angles)
        return jnp.concatenate([cos, cos], 1), jnp.concatenate([-sin, sin], 1)

    cos1, sin1 = tables(own_lengths)
    cos2, sin2 = tables(next_lengths + 1)

    rows = 2 * REQ
    proj = call(
        project,
        [SMEM] + [VMEM] * CHIPS + [VMEM] + [ANY] * 4,
        VMEM,
        [
            pltpu.VMEM((CHIPS, SHARD, QW + 2 * HD), BF),
            pltpu.VMEM((rows, QW + 2 * HD), F32),
            dma((CHIPS, 4)),
        ],
        shape((rows, PW), F32),
        2 * rows * CHIPS * SHARD * (QW + 2 * HD),
        12 << 20,
    )(where, *near, *far, norm_gain.reshape(2 * CHIPS, SHARD), w_query, w_keyval, wqs, wkvs)
    proj_sib = swap(proj, "tp", 1)

    term_shape = shape((REQ * HEADS + HEADS, HD), F32)
    q_shape = shape((REQ * HEADS, HD), F32)
    fresh_shape = shape((REQ, 2 * HD), F32)
    kv_scratch = pltpu.VMEM((REQ, BLK, 2 * HD), BF)
    wide_scratch = pltpu.VMEM((REQ, 2 * HD), F32)
    t1, q1, f1, sent = call(
        functools.partial(attend, 0, False),
        [SMEM] * 3 + [VMEM] * 4 + [ANY],
        [VMEM] * 4,
        [kv_scratch, wide_scratch, dma((4,))],
        [term_shape, q_shape, fresh_shape, shape((MOVE, 2 * HD), F32)],
        4 * REQ * HEADS * BLK * HD,
        6 << 20,
    )(where, own_lengths, slots, proj, proj_sib, cos1, sin1, cache)
    t1_sib = swap(t1, "tp", 1)
    came = sent.astype(BF)
    for bit in range(3):
        came = hop(came, bit, partner_mask)
    came = came.astype(F32)
    t2, q2, f2 = call(
        functools.partial(attend, 1, True),
        [SMEM] * 3 + [VMEM] * 4 + [ANY] * 3,
        [VMEM] * 3,
        [kv_scratch, pltpu.VMEM((MOVE, BLK, 2 * HD), BF), wide_scratch, dma((6,))],
        [term_shape, q_shape, fresh_shape],
        4 * REQ * HEADS * BLK * HD,
        6 << 20,
    )(where, next_lengths, slots, proj, proj_sib, cos2, sin2, cache, rows_a, rows_b)
    t2_sib = swap(t2, "tp", 1)

    parts = call(
        finish,
        [SMEM] * 2 + [VMEM] * 9 + [ANY] * 2,
        [VMEM] * CHIPS,
        [
            pltpu.VMEM((CHIPS, SHARD, SHARD), BF),
            pltpu.VMEM((CHIPS, SHARD, SHARD), BF),
            pltpu.VMEM((REQ, 2 * HD), F32),
            pltpu.VMEM((REQ * HEADS, HD), F32),
            pltpu.VMEM((rows, QW), BF),
            dma((CHIPS, 2)),
        ],
        [shape((rows, SHARD), BF)] * CHIPS,
        2 * rows * QW * CHIPS * SHARD,
        10 << 20,
    )(where, slots, t1, t1_sib, q1, f1, t2, t2_sib, q2, f2, came, w_out, wos)

    def added(values):
        return functools.reduce(jnp.add, [value.astype(F32) for value in values])

    other = added([parts[0]] + [swap(parts[i], "tp", 2 * i) for i in (1, 2, 3)]).astype(BF)
    crossed = swap(other, "tp", 8)
    same = added([parts[4]] + [swap(parts[4 + i], "tp", 2 * i) for i in (1, 2, 3)])
    out = (same + crossed.astype(F32)).astype(BF)
    return out.reshape(2, REQ, SHARD), arrived


def solution(mesh):
    placed = (
        P(None, "inst", "tp"),
        P(),
        P(None, "tp"),
        P(None, "tp"),
        P("tp", None),
        P("inst", "tp", None, None),
        P(),
        P(),
        P(),
    )
    return jax.shard_map(
        shards,
        mesh=mesh,
        in_specs=placed,
        out_specs=(P(None, "inst", "tp"), P("inst", "tp", None, None)),
        check_vma=False,
    )
```

time: 303 us -> 386 us (1.27)
  Pallas kernels: 0 us -> 296 us
  waiting for transfers between devices: 194 us -> 31.5 us
  matrix products: 37 us -> 0 us
  starting transfers between devices: 15.5 us -> 37.5 us
  between operations: 14.6 us -> 1.05 us
  other arithmetic: 18.7 us -> 7.37 us
  local copies, waits for them, and re-layouts: 22.5 us -> 12.5 us
    pallas_call x0 -> x7, Pallas kernels: none -> 296 us  [the longest x1 128 us: shards(): call(pick_qkv, [SMEM, ANY, ANY], [ANY, ANY], [dma((2 * CHIPS,))], [shape(...]
    reduce_scatter x2 -> x0, waiting for transfers between devices: 126 us -> none  [decode(): lax.psum_scatter(head_terms, 'tp', scatter_dimension=1, tiled=True)]
    dot_general x13 -> x0, matrix products: 37 us -> none  [the longest x2 12.9 us: decode(): head_terms = jnp.dot(attended, w_out, preferred_element_type=jnp.float32)]
    all_gather x2 -> x0, waiting for transfers between devices: 32.6 us -> none  [decode(): gathered = lax.all_gather(x_steps[step_index], 'tp', axis=1, tiled=True)]
    ppermute x14 -> x29, starting transfers between devices: 15.4 us -> 37.5 us  [swap(): return lax.ppermute(value, axis, [(i, i ^ mask) for i in range(count)])]
    reduce_sum x4 -> x0, other arithmetic: 5.08 us -> none  [the longest x2 3.25 us: decode(): jnp.mean(widened * widened, -1, keepdims=True) + eps_norm]
    another operation x6 -> x0, other arithmetic: 3.9 us -> none  [the longest x3 2.5 us: shards(): return (jnp.stack([first_out, second_out]), arrived_rows)]
    ppermute x14 -> x29, waiting for transfers between devices: 34.8 us -> 31.5 us  [swap(): return lax.ppermute(value, axis, [(i, i ^ mask) for i in range(count)])]
  transfers between devices with their start and end apart: 18 -> 29, of which waited for: 8 -> 11; matrix products, arithmetic and copies ran while one was open for 23% -> 3% of each run, Pallas kernels for 0% -> 40%
where the time goes in v1:
time: 386 us
  Pallas kernels  296 us (77%)
  starting transfers between devices  37.5 us (10%)
  waiting for transfers between devices  31.5 us (8%)
  local copies, waits for them, and re-layouts  12.5 us (3%)
  other arithmetic  7.37 us (2%)
    pallas_call x1, Pallas kernels, shards(): call(pick_qkv, [SMEM, ANY, ANY], [ANY, ANY], [dma((2 * CHIPS,))], [shape(...  128 us
    pallas_call x1, Pallas kernels, shards(): call(pick_out, [SMEM, ANY], ANY, [dma((CHIPS,))], shape((CHIPS, SHARD, SH...  128 us
    ppermute x29, starting transfers between devices, swap(): return lax.ppermute(value, axis, [(i, i ^ mask) for i in range(count)])  37.5 us
    ppermute x29, waiting for transfers between devices, swap(): return lax.ppermute(value, axis, [(i, i ^ mask) for i in range(count)])  31.5 us
    pallas_call x1, Pallas kernels, shards(): call(finish, [SMEM] * 2 + [VMEM] * 9 + [ANY] * 2, [VMEM] * CHIPS, [pltpu....  11.6 us
    pallas_call x1, Pallas kernels, shards(): call(functools.partial(attend, 1, True), [SMEM] * 3 + [VMEM] * 4 + [ANY]...  10.9 us
    pallas_call x1, Pallas kernels, shards(): call(functools.partial(attend, 0, False), [SMEM] * 3 + [VMEM] * 4 + [ANY]...  9.82 us
    unnamed x53, local copies, waits for them, and re-layouts  9.26 us
  transfers between devices with their start and end apart: 29, of which 11 were waited for; matrix products, arithmetic and copies ran while one was open for 3% of the time, Pallas kernels for 40%

profile of v1, /device:TPU:0, one launch (start us, length us, event | category | flops | bytes accessed | tf_op | source)
XLA Modules:
  0.0 385.6 jit_solution(12479574443234788540)
XLA Ops:
  0.6 1.6 copy-done.1
  2.2 128.3 %shard_map.104 = (bf16[8,512,512]{2,1,0:T(8,128)(2,1)}, bf16[8,512,128]{2,1,0:T(8,128)(2,1)}) custom-call(s32[1]{0:T(128)} %bitcast.where, bf16[8192,512]{1,0:T(8,128)(2,1)} %refs_9_.2, bf16[8192,128]{1,0:T(8,128)(2,1)S(1)} %copy-done.1), custom_call_target="tpu_custom_call" | custom-call | bytes 10485760 | tf_op jit(solution)/shard_map/pallas_call | solution.py:312
  130.6 3.2 collective-permute-start.3
  133.8 1.6 collective-permute-start
  135.4 128.2 %shard_map.109 = bf16[8,512,512]{2,1,0:T(8,128)(2,1)} custom-call(s32[1]{0:T(128)} %bitcast.where, bf16[512,8192]{1,0:T(8,128)(2,1)} %refs_9_.3), custom_call_target="tpu_custom_call" | custom-call | bytes 8388608 | tf_op jit(solution)/shard_map/pallas_call | solution.py:323
  266.9 2.2 copy-done
  269.0 1.6 shard_map.107
  270.7 3.0 collective-permute-start.1
  274.9 2.8 collective-permute-done.1.refs_2_
  279.6 1.4 collective-permute-done.2.refs_3_
  281.7 3.9 %collective-permute-start.14 = (bf16[4,128,256]{2,1,0:T(8,128)(2,1)}, bf16[4,128,256]{2,1,0:T(8,128)(2,1)}, u32[]{:S(2)}, u32[]{:S(2)}) collective-permute-start(bf16[4,128,256]{2,1,0:T(8,128)(2,1)} %get-tuple-element.27), channel_id=1, source_target_pairs={{0,64},{16,80},{32,96},{48,112},{64,0},{80,16},{96,32},{112,48},{1... | collective-permute-start | bytes 786440 | tf_op jit(solution)/shard_map/ppermute | solution.py:49
  286.2 2.2 collective-permute-start.5
  289.0 1.4 reshape.73.refs_8_
  291.3 1.7 collective-permute-done.5.refs_6_
  294.0 1.9 collective-permute-start.6
  297.0 3.3 collective-permute-done.6.refs_7_
  304.5 5.2 %shard_map.105.refs_0_ = f32[128,1408]{1,0:T(8,128)S(1)} custom-call(s32[1]{0:T(128)} %bitcast.where, bf16[128,512]{1,0:T(8,128)(2,1)S(1)} %bitcast.29, bf16[128,512]{1,0:T(8,128)(2,1)} %collective-permute-done.refs_1_, bf16[128,512]{1,0:T(8,128)(2,1)S(1)} %copy-done.5, bf16[128,512]{1,0:T(8,128)(2,1)S(1)} %copy-done.7, ...), custom_call_target="tpu_custom_call" | custom-call | flops 1342177280 | bytes 12582912 | tf_op jit(solution)/shard_map/pallas_call | solution.py:370
  309.9 2.6 collective-permute-start.12
  312.8 7.8 %collective-permute-done.12 = bf16[4,128,256]{2,1,0:T(8,128)(2,1)S(1)} collective-permute-done((bf16[4,128,256]{2,1,0:T(8,128)(2,1)S(1)}, bf16[4,128,256]{2,1,0:T(8,128)(2,1)S(1)}, u32[]{:S(2)}, u32[]{:S(2)}) %collective-permute-start.12) | collective-permute-done | bytes 262176 | tf_op jit(solution)/shard_map/ppermute | solution.py:49
  320.7 1.5 collective-permute-start.13
  322.2 9.8 %shard_map.106 = (f32[520,128]{1,0:T(8,128)S(1)}, f32[512,128]{1,0:T(8,128)S(1)}, f32[64,256]{1,0:T(8,128)S(1)}, f32[8,256]{1,0:T(8,128)S(1)}) custom-call(s32[1]{0:T(128)} %bitcast.where, s32[64]{0:T(128)S(1)} %get-tuple-element.45.lens, s32[8]{0:T(128)S(1)} %fusion.8.slots, f32[128,1408]{1,0:T(8,128)S(1)} %shard_map.105.refs_0_, ...), custom_call_target="tpu_custom_call" | custom-call | flops 33554432 | bytes 6291456 | tf_op jit(solution)/shard_map/pallas_call | solution.py:390
  332.8 2.9 collective-permute-done.18
  337.1 10.9 %shard_map.108 = (f32[520,128]{1,0:T(8,128)S(1)}, f32[512,128]{1,0:T(8,128)S(1)}, f32[64,256]{1,0:T(8,128)S(1)}) custom-call(s32[1]{0:T(128)} %bitcast.where, s32[64]{0:T(128)S(1)} %scatter_fusion, s32[8]{0:T(128)S(1)} %fusion.8.slots, f32[128,1408]{1,0:T(8,128)S(1)} %shard_map.105.refs_0_, f32[128,1408]{1,0:T(8,128)S(1)} %collective-permute-done.9.refs_1_, ...), custom_call_target="tpu_custom_call" | custom-call | flops 33554432 | bytes 6291456 | tf_op jit(solution)/shard_map/pallas_call | solution.py:404
  348.7 1.9 collective-permute-start.20
  350.6 3.2 collective-permute-done.20
  353.9 11.6 %shard_map.110 = (bf16[128,512]{1,0:T(8,128)(2,1)S(1)}, bf16[128,512]{1,0:T(8,128)(2,1)S(1)}, bf16[128,512]{1,0:T(8,128)(2,1)S(1)}, bf16[128,512]{1,0:T(8,128)(2...) custom-call(s32[1]{0:T(128)} %bitcast.where, ...), custom_call_target="tpu_custom_call" | custom-call | flops 1073741824 | bytes 10485760 | tf_op jit(solution)/shard_map/pallas_call | solution.py:415
  365.6 3.3 collective-permute-start.26
  368.9 1.4 collective-permute-start.27
  370.3 3.3 collective-permute-start.23
  375.9 2.4 collective-permute-done.27
  379.9 1.9 collective-permute-done.24
  381.8 3.1 collective-permute-done.28
  (116 shorter events, 23.5 us)
Async XLA Ops:
  130.5 170.4 %collective-permute-start.7 = (bf16[8,512,512]{2,1,0:T(8,128)(2,1)}, bf16[8,512,512]{2,1,0:T(8,128)(2,1)}, u32[]{:S(2)}, u32[]{:S(2)}) collective-permute-start(bf16[8,512,512]{2,1,0:T(8,128)(2,1)} %get-tuple-element.21), channel_id=1, source_target_pairs={{0,1},{1,0},{2,3},{3,2},{4,5},{5,4},{6,7},{7,6},{8,9},{9,8},{10,11... | collective-permute-start | bytes 12582920 | tf_op jit(solution)/shard_map/ppermute | solution.py:49
  130.6 140.0 %collective-permute-start.3 = (bf16[128,512]{1,0:T(8,128)(2,1)S(1)}, bf16[128,512]{1,0:T(8,128)(2,1)}, u32[]{:S(2)}, u32[]{:S(2)}) collective-permute-start(bf16[128,512]{1,0:T(8,128)(2,1)S(1)} %bitcast.25), channel_id=1, source_target_pairs={{0,8},{1,9},{2,10},{3,11},{4,12},{5,13},{6,14},{7,15},{8,0},{9,1},... | collective-permute-start | bytes 393224 | tf_op jit(solution)/shard_map/ppermute | solution.py:49
  133.8 140.8 %collective-permute-start = (bf16[128,512]{1,0:T(8,128)(2,1)S(1)}, bf16[128,512]{1,0:T(8,128)(2,1)}, u32[]{:S(2)}, u32[]{:S(2)}) collective-permute-start(bf16[128,512]{1,0:T(8,128)(2,1)S(1)} %bitcast.26), channel_id=1, source_target_pairs={{0,2},{1,3},{2,0},{3,1},{4,6},{5,7},{6,4},{7,5},{8,10},{9,11},{10,... | collective-permute-start | bytes 393224 | tf_op jit(solution)/shard_map/ppermute | solution.py:49
  135.4 128.8 %copy-start.11 = (s32[512]{0:T(512)S(1)}, s32[512]{0:T(512)}, u32[]{:S(2)}) copy-start(s32[512]{0:T(512)} %param.15) | copy-start | bytes 6148
  135.4 129.4 %copy-start.16 = (s32[8]{0:T(128)S(1)}, s32[8]{0:T(128)}, u32[]{:S(2)}) copy-start(s32[8]{0:T(128)} %param.17) | copy-start | bytes 100
  135.4 129.4 %copy-start.12 = (s32[8,8]{1,0:T(8,128)S(1)}, s32[8,8]{1,0:T(8,128)}, u32[]{:S(2)}) copy-start(s32[8,8]{1,0:T(8,128)} %param.16) | copy-start | bytes 772
  135.4 165.6 %collective-permute-start.8 = (bf16[8,512,128]{2,1,0:T(8,128)(2,1)}, bf16[8,512,128]{2,1,0:T(8,128)(2,1)S(1)}, u32[]{:S(2)}, u32[]{:S(2)}) collective-permute-start(bf16[8,512,128]{2,1,0:T(8,128)(2,1)} %get-tuple-element.22), channel_id=1, source_target_pairs={{0,1},{1,0},{2,3},{3,2},{4,5},{5,4},{6,7},{7,6},{8,9},{9,8},{10,11... | collective-permute-start | bytes 3145736 | tf_op jit(solution)/shard_map/ppermute | solution.py:49
  263.7 90.2 %collective-permute-start.21 = (bf16[8,512,512]{2,1,0:T(8,128)(2,1)}, bf16[8,512,512]{2,1,0:T(8,128)(2,1)}, u32[]{:S(2)}, u32[]{:S(2)}) collective-permute-start(bf16[8,512,512]{2,1,0:T(8,128)(2,1)} %shard_map.109), channel_id=1, source_target_pairs={{0,1},{1,0},{2,3},{3,2},{4,5},{5,4},{6,7},{7,6},{8,9},{9,8},{10,11... | collective-permute-start | bytes 12582920 | tf_op jit(solution)/shard_map/ppermute | solution.py:49
  270.7 7.0 %collective-permute-start.1 = (bf16[128,512]{1,0:T(8,128)(2,1)S(1)}, bf16[128,512]{1,0:T(8,128)(2,1)S(1)}, u32[]{:S(2)}, u32[]{:S(2)}) collective-permute-start(bf16[128,512]{1,0:T(8,128)(2,1)S(1)} %bitcast.27), channel_id=1, source_target_pairs={{0,4},{1,5},{2,6},{3,7},{4,0},{5,1},{6,2},{7,3},{8,12},{9,13},{10,... | collective-permute-start | bytes 393224 | tf_op jit(solution)/shard_map/ppermute | solution.py:49
  274.6 6.4 %collective-permute-start.2 = (bf16[128,512]{1,0:T(8,128)(2,1)S(1)}, bf16[128,512]{1,0:T(8,128)(2,1)S(1)}, u32[]{:S(2)}, u32[]{:S(2)}) collective-permute-start(bf16[128,512]{1,0:T(8,128)(2,1)S(1)} %bitcast.28), channel_id=1, source_target_pairs={{0,6},{1,7},{2,4},{3,5},{4,2},{5,3},{6,0},{7,1},{8,14},{9,15},{10,... | collective-permute-start | bytes 393224 | tf_op jit(solution)/shard_map/ppermute | solution.py:49
  278.4 7.2 %collective-permute-start.4 = (bf16[128,512]{1,0:T(8,128)(2,1)}, bf16[128,512]{1,0:T(8,128)(2,1)S(1)}, u32[]{:S(2)}, u32[]{:S(2)}) collective-permute-start(bf16[128,512]{1,0:T(8,128)(2,1)} %collective-permute-done.3.refs_4_), channel_id=1, source_target_pairs={{0,2},{1,3},{2,0},{3,1},{4,6},{5,7},{6,4},{7,5},{8,10},{9,11},{10,... | collective-permute-start | bytes 393224 | tf_op jit(solution)/shard_map/ppermute | solution.py:49
  281.7 12.3 %collective-permute-start.14 = (bf16[4,128,256]{2,1,0:T(8,128)(2,1)}, bf16[4,128,256]{2,1,0:T(8,128)(2,1)}, u32[]{:S(2)}, u32[]{:S(2)}) collective-permute-start(bf16[4,128,256]{2,1,0:T(8,128)(2,1)} %get-tuple-element.27), channel_id=1, source_target_pairs={{0,64},{16,80},{32,96},{48,112},{64,0},{80,16},{96,32},{112,48},{1... | collective-permute-start | bytes 786440 | tf_op jit(solution)/shard_map/ppermute | solution.py:49
  286.2 6.8 %collective-permute-start.5 = (bf16[128,512]{1,0:T(8,128)(2,1)}, bf16[128,512]{1,0:T(8,128)(2,1)}, u32[]{:S(2)}, u32[]{:S(2)}) collective-permute-start(bf16[128,512]{1,0:T(8,128)(2,1)} %collective-permute-done.3.refs_4_), channel_id=1, source_target_pairs={{0,4},{1,5},{2,6},{3,7},{4,0},{5,1},{6,2},{7,3},{8,12},{9,13},{10,... | collective-permute-start | bytes 393224 | tf_op jit(solution)/shard_map/ppermute | solution.py:49
  293.0 16.8 %collective-permute-start.11 = (bf16[4,128,256]{2,1,0:T(8,128)(2,1)S(1)}, bf16[4,128,256]{2,1,0:T(8,128)(2,1)S(1)}, u32[]{:S(2)}, u32[]{:S(2)}) collective-permute-start(bf16[4,128,256]{2,1,0:T(8,128)(2,1)S(1)} %get-tuple-element.26), channel_id=1, source_target_pairs={{0,32},{16,48},{32,0},{48,16},{64,96},{80,112},{96,64},{112,80},{1... | collective-permute-start | bytes 786440 | tf_op jit(solution)/shard_map/ppermute | solution.py:49
  294.0 6.4 %collective-permute-start.6 = (bf16[128,512]{1,0:T(8,128)(2,1)}, bf16[128,512]{1,0:T(8,128)(2,1)S(1)}, u32[]{:S(2)}, u32[]{:S(2)}) collective-permute-start(bf16[128,512]{1,0:T(8,128)(2,1)} %collective-permute-done.3.refs_4_), channel_id=1, source_target_pairs={{0,6},{1,7},{2,4},{3,5},{4,2},{5,3},{6,0},{7,1},{8,14},{9,15},{10,... | collective-permute-start | bytes 393224 | tf_op jit(solution)/shard_map/ppermute | solution.py:49
  300.4 12.1 %collective-permute-start.15 = (bf16[4,128,256]{2,1,0:T(8,128)(2,1)S(1)}, bf16[4,128,256]{2,1,0:T(8,128)(2,1)S(1)}, u32[]{:S(2)}, u32[]{:S(2)}) collective-permute-start(bf16[4,128,256]{2,1,0:T(8,128)(2,1)S(1)} %broadcast_select_fusion), channel_id=1, source_target_pairs={{0,16},{16,0},{32,48},{48,32},{64,80},{80,64},{96,112},{112,96},{1... | collective-permute-start | bytes 786440 | tf_op jit(solution)/shard_map/ppermute | solution.py:49
  309.6 12.6 %collective-permute-start.9 = (f32[128,1408]{1,0:T(8,128)S(1)}, f32[128,1408]{1,0:T(8,128)S(1)}, u32[]{:S(2)}, u32[]{:S(2)}) collective-permute-start(f32[128,1408]{1,0:T(8,128)S(1)} %shard_map.105.refs_0_), channel_id=1, source_target_pairs={{0,1},{1,0},{2,3},{3,2},{4,5},{5,4},{6,7},{7,6},{8,9},{9,8},{10,11... | collective-permute-start | bytes 2162696 | tf_op jit(solution)/shard_map/ppermute | solution.py:49
  309.9 10.7 %collective-permute-start.12 = (bf16[4,128,256]{2,1,0:T(8,128)(2,1)S(1)}, bf16[4,128,256]{2,1,0:T(8,128)(2,1)S(1)}, u32[]{:S(2)}, u32[]{:S(2)}) collective-permute-start(bf16[4,128,256]{2,1,0:T(8,128)(2,1)S(1)} %broadcast_select_fusion.3), channel_id=1, source_target_pairs={{0,64},{16,80},{32,96},{48,112},{64,0},{80,16},{96,32},{112,48},{1... | collective-permute-start | bytes 786440 | tf_op jit(solution)/shard_map/ppermute | solution.py:49
  312.6 20.2 %collective-permute-start.16 = (bf16[4,128,256]{2,1,0:T(8,128)(2,1)S(1)}, bf16[4,128,256]{2,1,0:T(8,128)(2,1)S(1)}, u32[]{:S(2)}, u32[]{:S(2)}) collective-permute-start(bf16[4,128,256]{2,1,0:T(8,128)(2,1)S(1)} %broadcast_select_fusion.1), channel_id=1, source_target_pairs={{0,32},{16,48},{32,0},{48,16},{64,96},{80,112},{96,64},{112,80},{1... | collective-permute-start | bytes 786440 | tf_op jit(solution)/shard_map/ppermute | solution.py:49
  320.7 16.3 %collective-permute-start.13 = (bf16[4,128,256]{2,1,0:T(8,128)(2,1)S(1)}, bf16[4,128,256]{2,1,0:T(8,128)(2,1)S(1)}, u32[]{:S(2)}, u32[]{:S(2)}) collective-permute-start(bf16[4,128,256]{2,1,0:T(8,128)(2,1)S(1)} %broadcast_select_fusion.4), channel_id=1, source_target_pairs={{0,16},{16,0},{32,48},{48,32},{64,80},{80,64},{96,112},{112,96},{1... | collective-permute-start | bytes 786440 | tf_op jit(solution)/shard_map/ppermute | solution.py:49
  332.1 3.7 collective-permute-start.18
  335.8 12.8 %collective-permute-start.19 = (bf16[8,256]{1,0:T(8,128)(2,1)S(1)}, bf16[8,256]{1,0:T(8,128)(2,1)S(1)}, u32[]{:S(2)}, u32[]{:S(2)}) collective-permute-start(bf16[8,256]{1,0:T(8,128)(2,1)S(1)} %broadcast_select_fusion.6), channel_id=1, source_target_pairs={{0,32},{16,48},{32,0},{48,16},{64,96},{80,112},{96,64},{112,80},{1... | collective-permute-start | bytes 12296 | tf_op jit(solution)/shard_map/ppermute | solution.py:49
  348.0 5.9 %collective-permute-start.17 = (f32[520,128]{1,0:T(8,128)S(1)}, f32[520,128]{1,0:T(8,128)S(1)}, u32[]{:S(2)}, u32[]{:S(2)}) collective-permute-start(f32[520,128]{1,0:T(8,128)S(1)} %get-tuple-element.28.refs_4_), channel_id=1, source_target_pairs={{0,1},{1,0},{2,3},{3,2},{4,5},{5,4},{6,7},{7,6},{8,9},{9,8},{10,11... | collective-permute-start | bytes 798728 | tf_op jit(solution)/shard_map/ppermute | solution.py:49
  348.1 5.8 %collective-permute-start.10 = (f32[520,128]{1,0:T(8,128)S(1)}, f32[520,128]{1,0:T(8,128)S(1)}, u32[]{:S(2)}, u32[]{:S(2)}) collective-permute-start(f32[520,128]{1,0:T(8,128)S(1)} %get-tuple-element.23.refs_0_), channel_id=1, source_target_pairs={{0,1},{1,0},{2,3},{3,2},{4,5},{5,4},{6,7},{7,6},{8,9},{9,8},{10,11... | collective-permute-start | bytes 798728 | tf_op jit(solution)/shard_map/ppermute | solution.py:49
  348.7 5.1 %collective-permute-start.20 = (bf16[8,256]{1,0:T(8,128)(2,1)S(1)}, bf16[8,256]{1,0:T(8,128)(2,1)S(1)}, u32[]{:S(2)}, u32[]{:S(2)}) collective-permute-start(bf16[8,256]{1,0:T(8,128)(2,1)S(1)} %broadcast_select_fusion.7), channel_id=1, source_target_pairs={{0,64},{16,80},{32,96},{48,112},{64,0},{80,16},{96,32},{112,48},{1... | collective-permute-start | bytes 12296 | tf_op jit(solution)/shard_map/ppermute | solution.py:49
  365.5 8.1 %collective-permute-start.25 = (bf16[128,512]{1,0:T(8,128)(2,1)S(1)}, bf16[128,512]{1,0:T(8,128)(2,1)S(1)}, u32[]{:S(2)}, u32[]{:S(2)}) collective-permute-start(bf16[128,512]{1,0:T(8,128)(2,1)S(1)} %get-tuple-element.37), channel_id=1, source_target_pairs={{0,2},{1,3},{2,0},{3,1},{4,6},{5,7},{6,4},{7,5},{8,10},{9,11},{10,... | collective-permute-start | bytes 393224 | tf_op jit(solution)/shard_map/ppermute | solution.py:49
  365.6 10.2 %collective-permute-start.26 = (bf16[128,512]{1,0:T(8,128)(2,1)S(1)}, bf16[128,512]{1,0:T(8,128)(2,1)S(1)}, u32[]{:S(2)}, u32[]{:S(2)}) collective-permute-start(bf16[128,512]{1,0:T(8,128)(2,1)S(1)} %get-tuple-element.38), channel_id=1, source_target_pairs={{0,4},{1,5},{2,6},{3,7},{4,0},{5,1},{6,2},{7,3},{8,12},{9,13},{10,... | collective-permute-start | bytes 393224 | tf_op jit(solution)/shard_map/ppermute | solution.py:49
  368.9 9.3 %collective-permute-start.27 = (bf16[128,512]{1,0:T(8,128)(2,1)S(1)}, bf16[128,512]{1,0:T(8,128)(2,1)S(1)}, u32[]{:S(2)}, u32[]{:S(2)}) collective-permute-start(bf16[128,512]{1,0:T(8,128)(2,1)S(1)} %get-tuple-element.39), channel_id=1, source_target_pairs={{0,6},{1,7},{2,4},{3,5},{4,2},{5,3},{6,0},{7,1},{8,14},{9,15},{10,... | collective-permute-start | bytes 393224 | tf_op jit(solution)/shard_map/ppermute | solution.py:49
  370.3 9.6 %collective-permute-start.22 = (bf16[128,512]{1,0:T(8,128)(2,1)S(1)}, bf16[128,512]{1,0:T(8,128)(2,1)S(1)}, u32[]{:S(2)}, u32[]{:S(2)}) collective-permute-start(bf16[128,512]{1,0:T(8,128)(2,1)S(1)} %get-tuple-element.33), channel_id=1, source_target_pairs={{0,2},{1,3},{2,0},{3,1},{4,6},{5,7},{6,4},{7,5},{8,10},{9,11},{10,... | collective-permute-start | bytes 393224 | tf_op jit(solution)/shard_map/ppermute | solution.py:49
  370.3 9.6 %collective-permute-start.23 = (bf16[128,512]{1,0:T(8,128)(2,1)S(1)}, bf16[128,512]{1,0:T(8,128)(2,1)S(1)}, u32[]{:S(2)}, u32[]{:S(2)}) collective-permute-start(bf16[128,512]{1,0:T(8,128)(2,1)S(1)} %get-tuple-element.34), channel_id=1, source_target_pairs={{0,4},{1,5},{2,6},{3,7},{4,0},{5,1},{6,2},{7,3},{8,12},{9,13},{10,... | collective-permute-start | bytes 393224 | tf_op jit(solution)/shard_map/ppermute | solution.py:49
  373.6 8.1 %collective-permute-start.24 = (bf16[128,512]{1,0:T(8,128)(2,1)S(1)}, bf16[128,512]{1,0:T(8,128)(2,1)S(1)}, u32[]{:S(2)}, u32[]{:S(2)}) collective-permute-start(bf16[128,512]{1,0:T(8,128)(2,1)S(1)} %get-tuple-element.35), channel_id=1, source_target_pairs={{0,6},{1,7},{2,4},{3,5},{4,2},{5,3},{6,0},{7,1},{8,14},{9,15},{10,... | collective-permute-start | bytes 393224 | tf_op jit(solution)/shard_map/ppermute | solution.py:49
  378.3 6.6 %collective-permute-start.28 = (bf16[128,512]{1,0:T(8,128)(2,1)S(1)}, bf16[128,512]{1,0:T(8,128)(2,1)S(1)}, u32[]{:S(2)}, u32[]{:S(2)}) collective-permute-start(bf16[128,512]{1,0:T(8,128)(2,1)S(1)} %add_convert_fusion.1), channel_id=1, source_target_pairs={{0,8},{1,9},{2,10},{3,11},{4,12},{5,13},{6,14},{7,15},{8,0},{9,1},... | collective-permute-start | bytes 393224 | tf_op jit(solution)/shard_map/ppermute | solution.py:49
  (23 other events, 401.9 us)

commit v2 on v1

--- a/solution.py
+++ b/solution.py
@@ -88,7 +88,7 @@
 
 def project(where, *refs):
     xs = refs[:CHIPS]
-    gain, wq, wkv, wqs, wkvs, out, buf, acc, sems = refs[CHIPS:]
+    gain, wq, wkv, wqs, wkvs, out, buf, held, acc, sems = refs[CHIPS:]
     me = where[0]
     core = me % 2
     pending = []
@@ -96,6 +96,7 @@
         src = me ^ (2 * i)
         rows = pl.ds(pl.multiple_of(src * SHARD, SHARD), SHARD)
         group = [
+            pltpu.make_async_copy(xs[i], held.at[i], sems.at[i, 4]),
             pltpu.make_async_copy(wq.at[rows, :], buf.at[i, :, pl.ds(0, SHARD)], sems.at[i, 0]),
             pltpu.make_async_copy(wqs.at[src // 2], buf.at[i, :, pl.ds(SHARD, SHARD)], sems.at[i, 1]),
             pltpu.make_async_copy(wkv.at[rows, :], buf.at[i, :, pl.ds(QW, HD)], sems.at[i, 2]),
@@ -107,13 +108,13 @@
     squares = None
     for i in range(CHIPS):
         src = me ^ (2 * i)
-        wide = xs[i][...].astype(F32)
+        for copy in pending[i]:
+            copy.wait()
+        wide = held[i].astype(F32)
         scaled = (wide * gain[pl.ds(src, 1), :]).astype(BF)
         sq = wide * wide
         part = sq[:, :HD] + sq[:, HD : 2 * HD] + sq[:, 2 * HD : 3 * HD] + sq[:, 3 * HD :]
         squares = part if squares is None else squares + part
-        for copy in pending[i]:
-            copy.wait()
         term = jnp.dot(scaled, buf[i], preferred_element_type=F32)
         if i == 0:
             acc[...] = term
@@ -128,23 +129,30 @@
     out[:, pl.ds(QW + 2 * HD, HD)] = squares
 
 
-def softmax_pair(q_pair, keys, values, len_a, len_b):
-    rows = q_pair.shape[0]
-    half = rows // 2
-    scores = lax.dot_general(
-        q_pair, keys, (((1,), (1,)), ((), ())), preferred_element_type=F32
-    ) * (1.0 / math.sqrt(HD))
-    lane = lax.broadcasted_iota(jnp.int32, (rows, 2 * BLK), 1)
-    upper = lax.broadcasted_iota(jnp.int32, (rows, 2 * BLK), 0) >= half
-    low = jnp.where(upper, BLK, 0)
-    high = jnp.where(upper, BLK + len_b, len_a)
-    visible = jnp.logical_and(lane >= low, lane < high)
-    scores = jnp.where(visible, scores, FLOOR)
+def block_terms(queries, blocks, lens):
+    scores = []
+    for p, block in enumerate(blocks):
+        both = jnp.concatenate(queries[2 * p : 2 * p + 2], 0).astype(BF)
+        pair = lax.dot_general(
+            both, block[:, :HD], (((1,), (1,)), ((), ())), preferred_element_type=F32
+        )
+        scores += [pair[:HEADS, :BLK], pair[HEADS:, BLK:]]
+    lane = lax.broadcasted_iota(jnp.int32, (HEADS, BLK), 1)
+    visible = jnp.concatenate([(lane < length).astype(F32) for length in lens], 0) > 0.0
+    scores = jnp.where(visible, jnp.concatenate(scores, 0) * (1.0 / math.sqrt(HD)), FLOOR)
     top = jnp.max(scores, -1, keepdims=True)
-    weights = jnp.where(visible, jnp.exp(scores - top), 0.0).astype(BF)
-    total = jnp.sum(weights.astype(F32), -1, keepdims=True)
-    mix = jnp.dot(weights, values, preferred_element_type=F32)
-    return top, total, mix
+    weights = jnp.where(visible, jnp.exp(scores - top), 0.0).astype(BF).astype(F32)
+    total = jnp.sum(weights, -1, keepdims=True)
+    zero = jnp.zeros((HEADS, BLK), F32)
+    mixes = []
+    for p, block in enumerate(blocks):
+        at = 2 * p * HEADS
+        one, two = weights[at : at + HEADS], weights[at + HEADS : at + 2 * HEADS]
+        both = jnp.concatenate(
+            [jnp.concatenate([one, zero], 1), jnp.concatenate([zero, two], 1)], 0
+        ).astype(BF)
+        mixes.append(jnp.dot(both, block[:, HD:], preferred_element_type=F32))
+    return top, total, mixes
 
 
 def attend(step, moving, where, lens, slots, *refs):
@@ -200,36 +208,33 @@
     def clipped(length):
         return jnp.clip(length - base, 0, BLK)
 
-    def pair(p, stats):
-        q_pair = q_out[pl.ds(pl.multiple_of(p * 2 * HEADS, 2 * HEADS), 2 * HEADS), :].astype(BF)
-        block = kv[pl.ds(2 * p, 2)].reshape(2 * BLK, 2 * HD)
-        top, total, mix = softmax_pair(
-            q_pair, block[:, :HD], block[:, HD:], clipped(lens[2 * p]), clipped(lens[2 * p + 1])
-        )
-        terms[pl.ds(pl.multiple_of(p * 2 * HEADS, 2 * HEADS), 2 * HEADS), :] = mix
-        stats = noted(stats, 2 * p, top[:HEADS], total[:HEADS])
-        return noted(stats, 2 * p + 1, top[HEADS:], total[HEADS:])
-
     stats = jnp.zeros((HEADS, HD), F32)
     for i in range(chunks):
         copies[i].wait()
-        stats = lax.fori_loop(i * per // 2, (i + 1) * per // 2, pair, stats, unroll=True)
+        mine_r = range(i * per, (i + 1) * per)
+        top, total, mixes = block_terms(
+            [q_out[pl.ds(r * HEADS, HEADS), :] for r in mine_r],
+            [kv[pl.ds(r, 2)].reshape(2 * BLK, 2 * HD) for r in mine_r[::2]],
+            [clipped(lens[r]) for r in mine_r],
+        )
+        for j, r in enumerate(mine_r):
+            at = slice(j * HEADS, (j + 1) * HEADS)
+            stats = noted(stats, r, top[at], total[at])
+            if j % 2 == 0:
+                terms[pl.ds(r * HEADS, 2 * HEADS), :] = mixes[j // 2]
     if moving:
         copies[chunks].wait()
         copies[chunks + 1].wait()
-        for p in range(MOVE // 2):
-            one, two = slots[2 * p], slots[2 * p + 1]
-            at_one = pl.ds(pl.multiple_of(one * HEADS, HEADS), HEADS)
-            at_two = pl.ds(pl.multiple_of(two * HEADS, HEADS), HEADS)
-            q_pair = jnp.concatenate([q_out[at_one, :], q_out[at_two, :]], 0).astype(BF)
-            block = arr[pl.ds(2 * p, 2)].reshape(2 * BLK, 2 * HD)
-            top, total, mix = softmax_pair(
-                q_pair, block[:, :HD], block[:, HD:], clipped(lens[one]), clipped(lens[two])
-            )
-            terms[at_one, :] = mix[:HEADS]
-            terms[at_two, :] = mix[HEADS:]
-            stats = noted(stats, one, top[:HEADS], total[:HEADS])
-            stats = noted(stats, two, top[HEADS:], total[HEADS:])
+        places = [pl.ds(pl.multiple_of(slots[j] * HEADS, HEADS), HEADS) for j in range(MOVE)]
+        top, total, mixes = block_terms(
+            [q_out[place, :] for place in places],
+            [arr[pl.ds(j, 2)].reshape(2 * BLK, 2 * HD) for j in range(0, MOVE, 2)],
+            [clipped(lens[slots[j]]) for j in range(MOVE)],
+        )
+        for j in range(MOVE):
+            at = slice(j * HEADS, (j + 1) * HEADS)
+            stats = noted(stats, slots[j], top[at], total[at])
+            terms[places[j], :] = mixes[j // 2][(j % 2) * HEADS : (j % 2 + 1) * HEADS]
     terms[pl.ds(REQ * HEADS, HEADS), :] = stats
 
 
@@ -255,28 +260,35 @@
     for j in range(MOVE):
         carried[pl.ds(slots[j], 1), :] = came[pl.ds(j, 1), :]
 
+    lane = lax.broadcasted_iota(jnp.int32, (HEADS, REQ), 1)
+
     def combine(step, mine, recv, q, fresh):
         stats_m = mine[pl.ds(REQ * HEADS, HEADS), :]
         stats_r = recv[pl.ds(REQ * HEADS, HEADS), :]
+        tops = [stats_m[:, :REQ], stats_r[:, :REQ]]
+        sums = [stats_m[:, REQ:], stats_r[:, REQ:]]
+        for row in fresh:
+            keys = row[:, pl.ds(0, HD)].astype(BF)
+            scores = lax.dot_general(
+                q[...].astype(BF), keys, (((1,), (1,)), ((), ())), preferred_element_type=F32
+            )
+            taken = [
+                jnp.where(lane == r, scores[r * HEADS : (r + 1) * HEADS], 0.0) for r in range(REQ)
+            ]
+            while len(taken) > 1:
+                taken = [taken[i] + taken[i + 1] for i in range(0, len(taken), 2)]
+            tops.append(taken[0] * (1.0 / math.sqrt(HD)))
+            sums.append(1.0)
+        overall = functools.reduce(jnp.maximum, tops)
+        factors = [jnp.exp(top - overall) for top in tops]
+        below = functools.reduce(jnp.add, [f * s for f, s in zip(factors, sums)])
+        factors = [f / below for f in factors]
         for r in range(REQ):
             at = pl.ds(r * HEADS, HEADS)
-            query = q[at, :]
-            tops = [stats_m[:, r : r + 1], stats_r[:, r : r + 1]]
-            sums = [stats_m[:, r + REQ : r + REQ + 1], stats_r[:, r + REQ : r + REQ + 1]]
-            mixes = [mine[at, :], recv[at, :]]
-            for row in fresh:
-                key = row[pl.ds(r, 1), pl.ds(0, HD)]
-                tops.append(jnp.sum(query * key, -1, keepdims=True) * (1.0 / math.sqrt(HD)))
-                sums.append(None)
-                mixes.append(row[pl.ds(r, 1), pl.ds(HD, HD)])
-            overall = functools.reduce(jnp.maximum, tops)
-            numerator = denominator = None
-            for top, total, mix in zip(tops, sums, mixes):
-                factor = jnp.exp(top - overall)
-                low = factor if total is None else factor * total
-                numerator = factor * mix if numerator is None else numerator + factor * mix
-                denominator = low if denominator is None else denominator + low
-            flat[at, :] = numerator / denominator
+            mixes = [mine[at, :], recv[at, :]] + [row[pl.ds(r, 1), pl.ds(HD, HD)] for row in fresh]
+            flat[at, :] = functools.reduce(
+                jnp.add, [f[:, r : r + 1] * mix for f, mix in zip(factors, mixes)]
+            )
         for h in range(HEADS):
             att[pl.ds(step * REQ, REQ), pl.ds(h * HD, HD)] = flat[
                 pl.ds(h, REQ, stride=HEADS), :
@@ -307,12 +319,13 @@
     own_x = x_steps.reshape(2 * REQ, SHARD)
     far_x = swap(own_x, "tp", 8)
     near = [own_x] + [swap(own_x, "tp", 2 * i) for i in (1, 2, 3)]
+    far_x, where = lax.optimization_barrier((far_x, where))
     far = [far_x] + [swap(far_x, "tp", 2 * i) for i in (1, 2, 3)]
 
     wq_send, wkv_send = call(
         pick_qkv,
         [SMEM, ANY, ANY],
-        [ANY, ANY],
+        [VMEM, VMEM],
         [dma((2 * CHIPS,))],
         [shape((CHIPS, SHARD, SHARD), BF), shape((CHIPS, SHARD, HD), BF)],
         0,
@@ -323,7 +336,7 @@
     wo_send = call(
         pick_out,
         [SMEM, ANY],
-        ANY,
+        VMEM,
         [dma((CHIPS,))],
         shape((CHIPS, SHARD, SHARD), BF),
         0,
@@ -341,7 +354,7 @@
     rows_a, rows_b = call(
         pick_rows,
         [SMEM, ANY],
-        [ANY, ANY],
+        [VMEM, VMEM],
         [dma((MOVE,))],
         [shape((half, BLK, 2 * HD), BF)] * 2,
         0,
@@ -369,12 +382,13 @@
     rows = 2 * REQ
     proj = call(
         project,
-        [SMEM] + [VMEM] * CHIPS + [VMEM] + [ANY] * 4,
+        [SMEM] + [ANY] * CHIPS + [VMEM] + [ANY] * 4,
         VMEM,
         [
             pltpu.VMEM((CHIPS, SHARD, QW + 2 * HD), BF),
+            pltpu.VMEM((CHIPS, rows, SHARD), BF),
             pltpu.VMEM((rows, QW + 2 * HD), F32),
-            dma((CHIPS, 4)),
+            dma((CHIPS, 5)),
         ],
         shape((rows, PW), F32),
         2 * rows * CHIPS * SHARD * (QW + 2 * HD),

time: 386 us -> 124 us (0.32)
  Pallas kernels: 296 us -> 28.5 us
  waiting for transfers between devices: 31.5 us -> 36.5 us
    pallas_call x4, Pallas kernels: 263 us -> 15.3 us  [the longest x1 4.56 us: shards(): call(project, [SMEM] + [ANY] * CHIPS + [VMEM] + [ANY] * 4, VMEM, [pltpu.V...]
    pallas_call x1, Pallas kernels: 10.9 us -> 4.06 us  [shards(): call(functools.partial(attend, 1, True), [SMEM] * 3 + [VMEM] * 4 + [ANY]...]
    pallas_call x1, Pallas kernels: 9.82 us -> 3.65 us  [shards(): call(functools.partial(attend, 0, False), [SMEM] * 3 + [VMEM] * 4 + [ANY]...]
    pallas_call x1, Pallas kernels: 11.6 us -> 5.46 us  [shards(): call(finish, [SMEM] * 2 + [VMEM] * 9 + [ANY] * 2, [VMEM] * CHIPS, [pltpu....]
    ppermute x29, waiting for transfers between devices: 31.5 us -> 36.5 us  [swap(): return lax.ppermute(value, axis, [(i, i ^ mask) for i in range(count)])]
  transfers between devices with their start and end apart: 29 -> 29, of which waited for: 11 -> 9; matrix products, arithmetic and copies ran while one was open for 3% -> 9% of each run, Pallas kernels for 40% -> 15%
where the time goes in v2:
time: 124 us; the launch traced here: 123 us
  waiting for transfers between devices  36.5 us (29%)
  starting transfers between devices  35.7 us (29%)
  Pallas kernels  28.5 us (23%)
  local copies, waits for them, and re-layouts  13.5 us (11%)
  other arithmetic  8.03 us (6%)
    ppermute x29, waiting for transfers between devices, swap(): return lax.ppermute(value, axis, [(i, i ^ mask) for i in range(count)])  36.5 us
    ppermute x29, starting transfers between devices, swap(): return lax.ppermute(value, axis, [(i, i ^ mask) for i in range(count)])  35.7 us
    unnamed x53, local copies, waits for them, and re-layouts  10.3 us
    pallas_call x1, Pallas kernels, shards(): call(finish, [SMEM] * 2 + [VMEM] * 9 + [ANY] * 2, [VMEM] * CHIPS, [pltpu....  5.46 us
    pallas_call x1, Pallas kernels, shards(): call(project, [SMEM] + [ANY] * CHIPS + [VMEM] + [ANY] * 4, VMEM, [pltpu.V...  4.56 us
    pallas_call x1, Pallas kernels, shards(): call(pick_qkv, [SMEM, ANY, ANY], [VMEM, VMEM], [dma((2 * CHIPS,))], [shap...  4.48 us
    pallas_call x1, Pallas kernels, shards(): call(pick_out, [SMEM, ANY], VMEM, [dma((CHIPS,))], shape((CHIPS, SHARD, S...  4.28 us
    pallas_call x1, Pallas kernels, shards(): call(functools.partial(attend, 1, True), [SMEM] * 3 + [VMEM] * 4 + [ANY]...  4.06 us
  transfers between devices with their start and end apart: 29, of which 9 were waited for; matrix products, arithmetic and copies ran while one was open for 9% of the time, Pallas kernels for 15%

profile of v2, /device:TPU:0, one launch (start us, length us, event | category | flops | bytes accessed | tf_op | source)
XLA Modules:
  0.0 123.3 jit_solution(10127768987150302081)
XLA Ops:
  0.6 3.2 %collective-permute-start = (bf16[128,512]{1,0:T(8,128)(2,1)}, bf16[128,512]{1,0:T(8,128)(2,1)S(1)}, u32[]{:S(2)}, u32[]{:S(2)}) collective-permute-start(bf16[128,512]{1,0:T(8,128)(2,1)} %bitcast.25), channel_id=1, source_target_pairs={{0,8},{1,9},{2,10},{3,11},{4,12},{5,13},{6,14},{7,15},{8,0},{9,1},... | collective-permute-start | bytes 393224 | tf_op jit(solution)/shard_map/ppermute | solution.py:49
  3.8 3.7 %collective-permute-done.refs_4_ = bf16[128,512]{1,0:T(8,128)(2,1)S(1)} collective-permute-done((bf16[128,512]{1,0:T(8,128)(2,1)}, bf16[128,512]{1,0:T(8,128)(2,1)S(1)}, u32[]{:S(2)}, u32[]{:S(2)}) %collective-permute-start) | collective-permute-done | bytes 131104 | tf_op jit(solution)/shard_map/ppermute | solution.py:49
  8.2 1.6 %copy-done.1 = bf16[8192,128]{1,0:T(8,128)(2,1)S(1)} copy-done((bf16[8192,128]{1,0:T(8,128)(2,1)S(1)}, bf16[8192,128]{1,0:T(8,128)(2,1)}, u32[]{:S(2)}) %copy-start.1) | copy-done | bytes 2097176
  9.8 4.5 %shard_map.104 = (bf16[8,512,512]{2,1,0:T(8,128)(2,1)}, bf16[8,512,128]{2,1,0:T(8,128)(2,1)S(1)}) custom-call(s32[1]{0:T(128)} %bitcast.1.where, bf16[8192,512]{1,0:T(8,128)(2,1)} %refs_9_.2, bf16[8192,128]{1,0:T(8,128)(2,1)S(1)} %copy-done.1), custom_call_target="tpu_custom_call" | custom-call | bytes 10485760 | tf_op jit(solution)/shard_map/pallas_call | solution.py:325
  15.3 1.8 %collective-permute-start.1 = (bf16[128,512]{1,0:T(8,128)(2,1)S(1)}, bf16[128,512]{1,0:T(8,128)(2,1)}, u32[]{:S(2)}, u32[]{:S(2)}) collective-permute-start(bf16[128,512]{1,0:T(8,128)(2,1)S(1)} %bitcast.26), channel_id=1, source_target_pairs={{0,2},{1,3},{2,0},{3,1},{4,6},{5,7},{6,4},{7,5},{8,10},{9,11},{10,... | collective-permute-start | bytes 393224 | tf_op jit(solution)/shard_map/ppermute | solution.py:49
  17.1 2.9 %collective-permute-start.2 = (bf16[128,512]{1,0:T(8,128)(2,1)S(1)}, bf16[128,512]{1,0:T(8,128)(2,1)}, u32[]{:S(2)}, u32[]{:S(2)}) collective-permute-start(bf16[128,512]{1,0:T(8,128)(2,1)S(1)} %bitcast.27), channel_id=1, source_target_pairs={{0,4},{1,5},{2,6},{3,7},{4,0},{5,1},{6,2},{7,3},{8,12},{9,13},{10,... | collective-permute-start | bytes 393224 | tf_op jit(solution)/shard_map/ppermute | solution.py:49
  20.6 4.3 %shard_map.109 = bf16[8,512,512]{2,1,0:T(8,128)(2,1)} custom-call(s32[1]{0:T(128)} %bitcast.1.where, bf16[512,8192]{1,0:T(8,128)(2,1)} %refs_9_.3), custom_call_target="tpu_custom_call" | custom-call | bytes 8388608 | tf_op jit(solution)/shard_map/pallas_call | solution.py:336
  27.5 2.2 %copy-done = bf16[64,1,128,256]{3,2,1,0:T(8,128)(2,1)S(1)} copy-done((bf16[64,1,128,256]{3,2,1,0:T(8,128)(2,1)S(1)}, bf16[64,1,128,256]{3,2,1,0:T(8,128)(2,1)}, u32[]{:S(2)}) %copy-start) | copy-done | bytes 4194328
  29.7 2.0 %shard_map.107 = (bf16[4,128,256]{2,1,0:T(8,128)(2,1)S(1)}, bf16[4,128,256]{2,1,0:T(8,128)(2,1)}) custom-call(s32[8]{0:T(128)S(1)} %fusion.8.slots, bf16[64,128,256]{2,1,0:T(8,128)(2,1)S(1)} %bitcast.24), custom_call_target="tpu_custom_call" | custom-call | bytes 1048576 | tf_op jit(solution)/shard_map/pallas_call | solution.py:354
  31.7 1.6 %fusion.1 = (f32[64,64]{1,0:T(8,128)}, f32[64,64]{1,0:T(8,128)}, f32[64,64]{1,0:T(8,128)}, f32[64,64]{1,0:T(8,128)}, f32[64,64]{1,0:T(8,128)}, /*index=5*/f32[64,64]{1,0:T(8,128)}) fusion(f32[64]{0:T(128)S(1)} %multiply_power_fusion, f32[64]{0:T(128)S(1)} %add_convert_fusion.2, f32[64]{0:T(128)} %get-tuple-element.48), kind=kLoop, calls=%fused_computation.21 | loop fusion | flops 16384 | bytes 99072 | tf_op jit(solution)/shard_map/neg | solution.py:377
  34.6 5.4 %collective-permute-done.3.refs_3_ = bf16[128,512]{1,0:T(8,128)(2,1)S(1)} collective-permute-done((bf16[128,512]{1,0:T(8,128)(2,1)S(1)}, bf16[128,512]{1,0:T(8,128)(2,1)S(1)}, u32[]{:S(2)}, u32[]{:S(2)}) %collective-permute-start.3) | collective-permute-done | bytes 131104 | tf_op jit(solution)/shard_map/ppermute | solution.py:49
  40.7 3.9 %collective-permute-start.14 = (bf16[4,128,256]{2,1,0:T(8,128)(2,1)}, bf16[4,128,256]{2,1,0:T(8,128)(2,1)}, u32[]{:S(2)}, u32[]{:S(2)}) collective-permute-start(bf16[4,128,256]{2,1,0:T(8,128)(2,1)} %get-tuple-element.31), channel_id=1, source_target_pairs={{0,64},{16,80},{32,96},{48,112},{64,0},{80,16},{96,32},{112,48},{1... | collective-permute-start | bytes 786440 | tf_op jit(solution)/shard_map/ppermute | solution.py:49
  45.8 1.4 %reshape.73.refs_8_ = f32[16,512]{1,0:T(8,128)} reshape(f32[8192]{0:T(1024)} %param.10) | data formatting | bytes 65536 | tf_op jit(solution)/shard_map/reshape | solution.py:396
  48.1 3.9 %collective-permute-done.5.refs_6_ = bf16[128,512]{1,0:T(8,128)(2,1)} collective-permute-done((bf16[128,512]{1,0:T(8,128)(2,1)}, bf16[128,512]{1,0:T(8,128)(2,1)}, u32[]{:S(2)}, u32[]{:S(2)}) %collective-permute-start.5) | collective-permute-done | bytes 131104 | tf_op jit(solution)/shard_map/ppermute | solution.py:49
  54.5 4.9 %collective-permute-done.6.refs_7_ = bf16[128,512]{1,0:T(8,128)(2,1)S(1)} collective-permute-done((bf16[128,512]{1,0:T(8,128)(2,1)}, bf16[128,512]{1,0:T(8,128)(2,1)S(1)}, u32[]{:S(2)}, u32[]{:S(2)}) %collective-permute-start.6) | collective-permute-done | bytes 131104 | tf_op jit(solution)/shard_map/ppermute | solution.py:49
  59.4 1.5 %collective-permute-start.15 = (bf16[4,128,256]{2,1,0:T(8,128)(2,1)S(1)}, bf16[4,128,256]{2,1,0:T(8,128)(2,1)S(1)}, u32[]{:S(2)}, u32[]{:S(2)}) collective-permute-start(bf16[4,128,256]{2,1,0:T(8,128)(2,1)S(1)} %broadcast_select_fusion), channel_id=1, source_target_pairs={{0,16},{16,0},{32,48},{48,32},{64,80},{80,64},{96,112},{112,96},{1... | collective-permute-start | bytes 786440 | tf_op jit(solution)/shard_map/ppermute | solution.py:49
  64.4 4.6 %shard_map.105.refs_0_ = f32[128,1408]{1,0:T(8,128)S(1)} custom-call(s32[1]{0:T(128)} %bitcast.1.where, bf16[128,512]{1,0:T(8,128)(2,1)S(1)} %bitcast.29, bf16[128,512]{1,0:T(8,128)(2,1)} %collective-permute-done.1.refs_1_, bf16[128,512]{1,0:T(8,128)(2,1)} %collective-permute-done.2.refs_2_, bf16[128,512]{1,0:T(8,128)(2,1)S(1)} %copy-done.7, ...), custom_call_target="tpu_custom_call" | custom-call | flops 1342177280 | bytes 12582912 | tf_op jit(solution)/shard_map/pallas_call | solution.py:383
  71.3 8.6 %collective-permute-done.12 = bf16[4,128,256]{2,1,0:T(8,128)(2,1)S(1)} collective-permute-done((bf16[4,128,256]{2,1,0:T(8,128)(2,1)S(1)}, bf16[4,128,256]{2,1,0:T(8,128)(2,1)S(1)}, u32[]{:S(2)}, u32[]{:S(2)}) %collective-permute-start.12) | collective-permute-done | bytes 262176 | tf_op jit(solution)/shard_map/ppermute | solution.py:49
  80.6 3.6 %shard_map.106 = (f32[520,128]{1,0:T(8,128)S(1)}, f32[512,128]{1,0:T(8,128)S(1)}, f32[64,256]{1,0:T(8,128)S(1)}, f32[8,256]{1,0:T(8,128)S(1)}) custom-call(s32[1]{0:T(128)} %bitcast.1.where, s32[64]{0:T(128)S(1)} %get-tuple-element.49.lens, s32[8]{0:T(128)S(1)} %fusion.8.slots, f32[128,1408]{1,0:T(8,128)S(1)} %shard_map.105.refs_0_, ...), custom_call_target="tpu_custom_call" | custom-call | flops 33554432 | bytes 6291456 | tf_op jit(solution)/shard_map/pallas_call | solution.py:404
  84.3 1.6 %collective-permute-start.18 = (bf16[8,256]{1,0:T(8,128)(2,1)S(1)}, bf16[8,256]{1,0:T(8,128)(2,1)S(1)}, u32[]{:S(2)}, u32[]{:S(2)}) collective-permute-start(bf16[8,256]{1,0:T(8,128)(2,1)S(1)} %convert_element_type.47), channel_id=1, source_target_pairs={{0,16},{16,0},{32,48},{48,32},{64,80},{80,64},{96,112},{112,96},{1... | collective-permute-start | bytes 12296 | tf_op jit(solution)/shard_map/ppermute | solution.py:49
  86.0 2.0 %collective-permute-done.18 = bf16[8,256]{1,0:T(8,128)(2,1)S(1)} collective-permute-done((bf16[8,256]{1,0:T(8,128)(2,1)S(1)}, bf16[8,256]{1,0:T(8,128)(2,1)S(1)}, u32[]{:S(2)}, u32[]{:S(2)}) %collective-permute-start.18) | collective-permute-done | bytes 4128 | tf_op jit(solution)/shard_map/ppermute | solution.py:49
  89.2 4.1 %shard_map.108 = (f32[520,128]{1,0:T(8,128)S(1)}, f32[512,128]{1,0:T(8,128)S(1)}, f32[64,256]{1,0:T(8,128)S(1)}) custom-call(s32[1]{0:T(128)} %bitcast.1.where, s32[64]{0:T(128)S(1)} %scatter_fusion, s32[8]{0:T(128)S(1)} %fusion.8.slots, f32[128,1408]{1,0:T(8,128)S(1)} %shard_map.105.refs_0_, f32[128,1408]{1,0:T(8,128)S(1)} %collective-permute-done.9.refs_1_, ...), custom_call_target="tpu_custom_call" | custom-call | flops 33554432 | bytes 6291456 | tf_op jit(solution)/shard_map/pallas_call | solution.py:418
  94.1 1.4 %collective-permute-start.20 = (bf16[8,256]{1,0:T(8,128)(2,1)S(1)}, bf16[8,256]{1,0:T(8,128)(2,1)S(1)}, u32[]{:S(2)}, u32[]{:S(2)}) collective-permute-start(bf16[8,256]{1,0:T(8,128)(2,1)S(1)} %broadcast_select_fusion.7), channel_id=1, source_target_pairs={{0,64},{16,80},{32,96},{48,112},{64,0},{80,16},{96,32},{112,48},{1... | collective-permute-start | bytes 12296 | tf_op jit(solution)/shard_map/ppermute | solution.py:49
  95.5 3.7 %collective-permute-done.20 = bf16[8,256]{1,0:T(8,128)(2,1)S(1)} collective-permute-done((bf16[8,256]{1,0:T(8,128)(2,1)S(1)}, bf16[8,256]{1,0:T(8,128)(2,1)S(1)}, u32[]{:S(2)}, u32[]{:S(2)}) %collective-permute-start.20) | collective-permute-done | bytes 4128 | tf_op jit(solution)/shard_map/ppermute | solution.py:49
  99.3 5.5 %shard_map.110 = (bf16[128,512]{1,0:T(8,128)(2,1)S(1)}, bf16[128,512]{1,0:T(8,128)(2,1)S(1)}, bf16[128,512]{1,0:T(8,128)(2,1)S(1)}, bf16[128,512]{1,0:T(8,128)(2...) custom-call(s32[1]{0:T(128)} %bitcast.1.where, ...), custom_call_target="tpu_custom_call" | custom-call | flops 1073741824 | bytes 10485760 | tf_op jit(solution)/shard_map/pallas_call | solution.py:429
  104.9 1.7 %collective-permute-start.26 = (bf16[128,512]{1,0:T(8,128)(2,1)S(1)}, bf16[128,512]{1,0:T(8,128)(2,1)S(1)}, u32[]{:S(2)}, u32[]{:S(2)}) collective-permute-start(bf16[128,512]{1,0:T(8,128)(2,1)S(1)} %get-tuple-element.42), channel_id=1, source_target_pairs={{0,4},{1,5},{2,6},{3,7},{4,0},{5,1},{6,2},{7,3},{8,12},{9,13},{10,... | collective-permute-start | bytes 393224 | tf_op jit(solution)/shard_map/ppermute | solution.py:49
  106.6 3.0 %collective-permute-start.27 = (bf16[128,512]{1,0:T(8,128)(2,1)S(1)}, bf16[128,512]{1,0:T(8,128)(2,1)S(1)}, u32[]{:S(2)}, u32[]{:S(2)}) collective-permute-start(bf16[128,512]{1,0:T(8,128)(2,1)S(1)} %get-tuple-element.43), channel_id=1, source_target_pairs={{0,6},{1,7},{2,4},{3,5},{4,2},{5,3},{6,0},{7,1},{8,14},{9,15},{10,... | collective-permute-start | bytes 393224 | tf_op jit(solution)/shard_map/ppermute | solution.py:49
  109.6 1.7 %collective-permute-start.23 = (bf16[128,512]{1,0:T(8,128)(2,1)S(1)}, bf16[128,512]{1,0:T(8,128)(2,1)S(1)}, u32[]{:S(2)}, u32[]{:S(2)}) collective-permute-start(bf16[128,512]{1,0:T(8,128)(2,1)S(1)} %get-tuple-element.38), channel_id=1, source_target_pairs={{0,4},{1,5},{2,6},{3,7},{4,0},{5,1},{6,2},{7,3},{8,12},{9,13},{10,... | collective-permute-start | bytes 393224 | tf_op jit(solution)/shard_map/ppermute | solution.py:49
  111.3 3.0 %collective-permute-start.24 = (bf16[128,512]{1,0:T(8,128)(2,1)S(1)}, bf16[128,512]{1,0:T(8,128)(2,1)S(1)}, u32[]{:S(2)}, u32[]{:S(2)}) collective-permute-start(bf16[128,512]{1,0:T(8,128)(2,1)S(1)} %get-tuple-element.39), channel_id=1, source_target_pairs={{0,6},{1,7},{2,4},{3,5},{4,2},{5,3},{6,0},{7,1},{8,14},{9,15},{10,... | collective-permute-start | bytes 393224 | tf_op jit(solution)/shard_map/ppermute | solution.py:49
  114.3 1.7 %collective-permute-done.27 = bf16[128,512]{1,0:T(8,128)(2,1)S(1)} collective-permute-done((bf16[128,512]{1,0:T(8,128)(2,1)S(1)}, bf16[128,512]{1,0:T(8,128)(2,1)S(1)}, u32[]{:S(2)}, u32[]{:S(2)}) %collective-permute-start.27) | collective-permute-done | bytes 131104 | tf_op jit(solution)/shard_map/ppermute | solution.py:49
  116.0 3.1 %collective-permute-start.28 = (bf16[128,512]{1,0:T(8,128)(2,1)S(1)}, bf16[128,512]{1,0:T(8,128)(2,1)S(1)}, u32[]{:S(2)}, u32[]{:S(2)}) collective-permute-start(bf16[128,512]{1,0:T(8,128)(2,1)S(1)} %add_convert_fusion.1), channel_id=1, source_target_pairs={{0,8},{1,9},{2,10},{3,11},{4,12},{5,13},{6,14},{7,15},{8,0},{9,1},... | collective-permute-start | bytes 393224 | tf_op jit(solution)/shard_map/ppermute | solution.py:49
  120.0 2.6 %collective-permute-done.28 = bf16[128,512]{1,0:T(8,128)(2,1)S(1)} collective-permute-done((bf16[128,512]{1,0:T(8,128)(2,1)S(1)}, bf16[128,512]{1,0:T(8,128)(2,1)S(1)}, u32[]{:S(2)}, u32[]{:S(2)}) %collective-permute-start.28) | collective-permute-done | bytes 131104 | tf_op jit(solution)/shard_map/ppermute | solution.py:49
  (116 shorter events, 21.9 us)
Async XLA Ops:
  0.6 6.9 %collective-permute-start = (bf16[128,512]{1,0:T(8,128)(2,1)}, bf16[128,512]{1,0:T(8,128)(2,1)S(1)}, u32[]{:S(2)}, u32[]{:S(2)}) collective-permute-start(bf16[128,512]{1,0:T(8,128)(2,1)} %bitcast.25), channel_id=1, source_target_pairs={{0,8},{1,9},{2,10},{3,11},{4,12},{5,13},{6,14},{7,15},{8,0},{9,1},... | collective-permute-start | bytes 393224 | tf_op jit(solution)/shard_map/ppermute | solution.py:49
  15.3 45.6 %collective-permute-start.7 = (bf16[8,512,512]{2,1,0:T(8,128)(2,1)}, bf16[8,512,512]{2,1,0:T(8,128)(2,1)}, u32[]{:S(2)}, u32[]{:S(2)}) collective-permute-start(bf16[8,512,512]{2,1,0:T(8,128)(2,1)} %get-tuple-element.25), channel_id=1, source_target_pairs={{0,1},{1,0},{2,3},{3,2},{4,5},{5,4},{6,7},{7,6},{8,9},{9,8},{10,11... | collective-permute-start | bytes 12582920 | tf_op jit(solution)/shard_map/ppermute | solution.py:49
  15.3 18.1 %collective-permute-start.1 = (bf16[128,512]{1,0:T(8,128)(2,1)S(1)}, bf16[128,512]{1,0:T(8,128)(2,1)}, u32[]{:S(2)}, u32[]{:S(2)}) collective-permute-start(bf16[128,512]{1,0:T(8,128)(2,1)S(1)} %bitcast.26), channel_id=1, source_target_pairs={{0,2},{1,3},{2,0},{3,1},{4,6},{5,7},{6,4},{7,5},{8,10},{9,11},{10,... | collective-permute-start | bytes 393224 | tf_op jit(solution)/shard_map/ppermute | solution.py:49
  17.1 16.3 %collective-permute-start.2 = (bf16[128,512]{1,0:T(8,128)(2,1)S(1)}, bf16[128,512]{1,0:T(8,128)(2,1)}, u32[]{:S(2)}, u32[]{:S(2)}) collective-permute-start(bf16[128,512]{1,0:T(8,128)(2,1)S(1)} %bitcast.27), channel_id=1, source_target_pairs={{0,4},{1,5},{2,6},{3,7},{4,0},{5,1},{6,2},{7,3},{8,12},{9,13},{10,... | collective-permute-start | bytes 393224 | tf_op jit(solution)/shard_map/ppermute | solution.py:49
  24.9 36.0 %copy-start.2 = (bf16[8192,128]{1,0:T(8,128)(2,1)S(1)}, bf16[8192,128]{1,0:T(8,128)(2,1)}, u32[]{:S(2)}) copy-start(bf16[8192,128]{1,0:T(8,128)(2,1)} %refs_10_.1) | copy-start | bytes 6291460
  24.9 74.4 %collective-permute-start.21 = (bf16[8,512,512]{2,1,0:T(8,128)(2,1)}, bf16[8,512,512]{2,1,0:T(8,128)(2,1)}, u32[]{:S(2)}, u32[]{:S(2)}) collective-permute-start(bf16[8,512,512]{2,1,0:T(8,128)(2,1)} %shard_map.109), channel_id=1, source_target_pairs={{0,1},{1,0},{2,3},{3,2},{4,5},{5,4},{6,7},{7,6},{8,9},{9,8},{10,11... | collective-permute-start | bytes 12582920 | tf_op jit(solution)/shard_map/ppermute | solution.py:49
  27.0 33.9 %collective-permute-start.8 = (bf16[8,512,128]{2,1,0:T(8,128)(2,1)}, bf16[8,512,128]{2,1,0:T(8,128)(2,1)S(1)}, u32[]{:S(2)}, u32[]{:S(2)}) collective-permute-start(bf16[8,512,128]{2,1,0:T(8,128)(2,1)} %copy-done.11), channel_id=1, source_target_pairs={{0,1},{1,0},{2,3},{3,2},{4,5},{5,4},{6,7},{7,6},{8,9},{9,8},{10,11... | collective-permute-start | bytes 3145736 | tf_op jit(solution)/shard_map/ppermute | solution.py:49
  33.4 6.6 %collective-permute-start.3 = (bf16[128,512]{1,0:T(8,128)(2,1)S(1)}, bf16[128,512]{1,0:T(8,128)(2,1)S(1)}, u32[]{:S(2)}, u32[]{:S(2)}) collective-permute-start(bf16[128,512]{1,0:T(8,128)(2,1)S(1)} %bitcast.28), channel_id=1, source_target_pairs={{0,6},{1,7},{2,4},{3,5},{4,2},{5,3},{6,0},{7,1},{8,14},{9,15},{10,... | collective-permute-start | bytes 393224 | tf_op jit(solution)/shard_map/ppermute | solution.py:49
  33.4 11.2 %collective-permute-start.4 = (bf16[128,512]{1,0:T(8,128)(2,1)}, bf16[128,512]{1,0:T(8,128)(2,1)S(1)}, u32[]{:S(2)}, u32[]{:S(2)}) collective-permute-start(bf16[128,512]{1,0:T(8,128)(2,1)} %copy-done.4), channel_id=1, source_target_pairs={{0,2},{1,3},{2,0},{3,1},{4,6},{5,7},{6,4},{7,5},{8,10},{9,11},{10,... | collective-permute-start | bytes 393224 | tf_op jit(solution)/shard_map/ppermute | solution.py:49
  40.7 12.3 %collective-permute-start.14 = (bf16[4,128,256]{2,1,0:T(8,128)(2,1)}, bf16[4,128,256]{2,1,0:T(8,128)(2,1)}, u32[]{:S(2)}, u32[]{:S(2)}) collective-permute-start(bf16[4,128,256]{2,1,0:T(8,128)(2,1)} %get-tuple-element.31), channel_id=1, source_target_pairs={{0,64},{16,80},{32,96},{48,112},{64,0},{80,16},{96,32},{112,48},{1... | collective-permute-start | bytes 786440 | tf_op jit(solution)/shard_map/ppermute | solution.py:49
  45.2 6.8 %collective-permute-start.5 = (bf16[128,512]{1,0:T(8,128)(2,1)}, bf16[128,512]{1,0:T(8,128)(2,1)}, u32[]{:S(2)}, u32[]{:S(2)}) collective-permute-start(bf16[128,512]{1,0:T(8,128)(2,1)} %copy-done.4), channel_id=1, source_target_pairs={{0,4},{1,5},{2,6},{3,7},{4,0},{5,1},{6,2},{7,3},{8,12},{9,13},{10,... | collective-permute-start | bytes 393224 | tf_op jit(solution)/shard_map/ppermute | solution.py:49
  52.0 17.1 %collective-permute-start.11 = (bf16[4,128,256]{2,1,0:T(8,128)(2,1)S(1)}, bf16[4,128,256]{2,1,0:T(8,128)(2,1)S(1)}, u32[]{:S(2)}, u32[]{:S(2)}) collective-permute-start(bf16[4,128,256]{2,1,0:T(8,128)(2,1)S(1)} %get-tuple-element.30), channel_id=1, source_target_pairs={{0,32},{16,48},{32,0},{48,16},{64,96},{80,112},{96,64},{112,80},{1... | collective-permute-start | bytes 786440 | tf_op jit(solution)/shard_map/ppermute | solution.py:49
  53.0 6.4 %collective-permute-start.6 = (bf16[128,512]{1,0:T(8,128)(2,1)}, bf16[128,512]{1,0:T(8,128)(2,1)S(1)}, u32[]{:S(2)}, u32[]{:S(2)}) collective-permute-start(bf16[128,512]{1,0:T(8,128)(2,1)} %copy-done.4), channel_id=1, source_target_pairs={{0,6},{1,7},{2,4},{3,5},{4,2},{5,3},{6,0},{7,1},{8,14},{9,15},{10,... | collective-permute-start | bytes 393224 | tf_op jit(solution)/shard_map/ppermute | solution.py:49
  53.3 26.6 %copy-start.23 = (pred[4]{0:T(512)(128)(4,1)S(1)}, pred[4]{0:T(512)(128)(4,1)}, u32[]{:S(2)}) copy-start(pred[4]{0:T(512)(128)(4,1)} %get-tuple-element.60) | copy-start | bytes 16
  59.4 11.0 %collective-permute-start.15 = (bf16[4,128,256]{2,1,0:T(8,128)(2,1)S(1)}, bf16[4,128,256]{2,1,0:T(8,128)(2,1)S(1)}, u32[]{:S(2)}, u32[]{:S(2)}) collective-permute-start(bf16[4,128,256]{2,1,0:T(8,128)(2,1)S(1)} %broadcast_select_fusion), channel_id=1, source_target_pairs={{0,16},{16,0},{32,48},{48,32},{64,80},{80,64},{96,112},{112,96},{1... | collective-permute-start | bytes 786440 | tf_op jit(solution)/shard_map/ppermute | solution.py:49
  68.9 11.7 %collective-permute-start.9 = (f32[128,1408]{1,0:T(8,128)S(1)}, f32[128,1408]{1,0:T(8,128)S(1)}, u32[]{:S(2)}, u32[]{:S(2)}) collective-permute-start(f32[128,1408]{1,0:T(8,128)S(1)} %shard_map.105.refs_0_), channel_id=1, source_target_pairs={{0,1},{1,0},{2,3},{3,2},{4,5},{5,4},{6,7},{7,6},{8,9},{9,8},{10,11... | collective-permute-start | bytes 2162696 | tf_op jit(solution)/shard_map/ppermute | solution.py:49
  69.2 19.9 %copy-start.21 = (pred[4]{0:T(512)(128)(4,1)S(1)}, pred[4]{0:T(512)(128)(4,1)}, u32[]{:S(2)}) copy-start(pred[4]{0:T(512)(128)(4,1)} %get-tuple-element.64) | copy-start | bytes 16
  69.2 10.7 %collective-permute-start.12 = (bf16[4,128,256]{2,1,0:T(8,128)(2,1)S(1)}, bf16[4,128,256]{2,1,0:T(8,128)(2,1)S(1)}, u32[]{:S(2)}, u32[]{:S(2)}) collective-permute-start(bf16[4,128,256]{2,1,0:T(8,128)(2,1)S(1)} %broadcast_select_fusion.3), channel_id=1, source_target_pairs={{0,64},{16,80},{32,96},{48,112},{64,0},{80,16},{96,32},{112,48},{1... | collective-permute-start | bytes 786440 | tf_op jit(solution)/shard_map/ppermute | solution.py:49
  70.5 15.3 %collective-permute-start.16 = (bf16[4,128,256]{2,1,0:T(8,128)(2,1)S(1)}, bf16[4,128,256]{2,1,0:T(8,128)(2,1)S(1)}, u32[]{:S(2)}, u32[]{:S(2)}) collective-permute-start(bf16[4,128,256]{2,1,0:T(8,128)(2,1)S(1)} %broadcast_select_fusion.1), channel_id=1, source_target_pairs={{0,32},{16,48},{32,0},{48,16},{64,96},{80,112},{96,64},{112,80},{1... | collective-permute-start | bytes 786440 | tf_op jit(solution)/shard_map/ppermute | solution.py:49
  80.0 9.1 %collective-permute-start.13 = (bf16[4,128,256]{2,1,0:T(8,128)(2,1)S(1)}, bf16[4,128,256]{2,1,0:T(8,128)(2,1)S(1)}, u32[]{:S(2)}, u32[]{:S(2)}) collective-permute-start(bf16[4,128,256]{2,1,0:T(8,128)(2,1)S(1)} %broadcast_select_fusion.4), channel_id=1, source_target_pairs={{0,16},{16,0},{32,48},{48,32},{64,80},{80,64},{96,112},{112,96},{1... | collective-permute-start | bytes 786440 | tf_op jit(solution)/shard_map/ppermute | solution.py:49
  84.3 3.7 %collective-permute-start.18 = (bf16[8,256]{1,0:T(8,128)(2,1)S(1)}, bf16[8,256]{1,0:T(8,128)(2,1)S(1)}, u32[]{:S(2)}, u32[]{:S(2)}) collective-permute-start(bf16[8,256]{1,0:T(8,128)(2,1)S(1)} %convert_element_type.47), channel_id=1, source_target_pairs={{0,16},{16,0},{32,48},{48,32},{64,80},{80,64},{96,112},{112,96},{1... | collective-permute-start | bytes 12296 | tf_op jit(solution)/shard_map/ppermute | solution.py:49
  88.0 6.0 %collective-permute-start.19 = (bf16[8,256]{1,0:T(8,128)(2,1)S(1)}, bf16[8,256]{1,0:T(8,128)(2,1)S(1)}, u32[]{:S(2)}, u32[]{:S(2)}) collective-permute-start(bf16[8,256]{1,0:T(8,128)(2,1)S(1)} %broadcast_select_fusion.6), channel_id=1, source_target_pairs={{0,32},{16,48},{32,0},{48,16},{64,96},{80,112},{96,64},{112,80},{1... | collective-permute-start | bytes 12296 | tf_op jit(solution)/shard_map/ppermute | solution.py:49
  93.2 6.1 %collective-permute-start.17 = (f32[520,128]{1,0:T(8,128)S(1)}, f32[520,128]{1,0:T(8,128)S(1)}, u32[]{:S(2)}, u32[]{:S(2)}) collective-permute-start(f32[520,128]{1,0:T(8,128)S(1)} %get-tuple-element.32.refs_4_), channel_id=1, source_target_pairs={{0,1},{1,0},{2,3},{3,2},{4,5},{5,4},{6,7},{7,6},{8,9},{9,8},{10,11... | collective-permute-start | bytes 798728 | tf_op jit(solution)/shard_map/ppermute | solution.py:49
  93.5 5.8 %collective-permute-start.10 = (f32[520,128]{1,0:T(8,128)S(1)}, f32[520,128]{1,0:T(8,128)S(1)}, u32[]{:S(2)}, u32[]{:S(2)}) collective-permute-start(f32[520,128]{1,0:T(8,128)S(1)} %get-tuple-element.27.refs_0_), channel_id=1, source_target_pairs={{0,1},{1,0},{2,3},{3,2},{4,5},{5,4},{6,7},{7,6},{8,9},{9,8},{10,11... | collective-permute-start | bytes 798728 | tf_op jit(solution)/shard_map/ppermute | solution.py:49
  94.1 5.1 %collective-permute-start.20 = (bf16[8,256]{1,0:T(8,128)(2,1)S(1)}, bf16[8,256]{1,0:T(8,128)(2,1)S(1)}, u32[]{:S(2)}, u32[]{:S(2)}) collective-permute-start(bf16[8,256]{1,0:T(8,128)(2,1)S(1)} %broadcast_select_fusion.7), channel_id=1, source_target_pairs={{0,64},{16,80},{32,96},{48,112},{64,0},{80,16},{96,32},{112,48},{1... | collective-permute-start | bytes 12296 | tf_op jit(solution)/shard_map/ppermute | solution.py:49
  104.8 6.5 %collective-permute-start.25 = (bf16[128,512]{1,0:T(8,128)(2,1)S(1)}, bf16[128,512]{1,0:T(8,128)(2,1)S(1)}, u32[]{:S(2)}, u32[]{:S(2)}) collective-permute-start(bf16[128,512]{1,0:T(8,128)(2,1)S(1)} %get-tuple-element.41), channel_id=1, source_target_pairs={{0,2},{1,3},{2,0},{3,1},{4,6},{5,7},{6,4},{7,5},{8,10},{9,11},{10,... | collective-permute-start | bytes 393224 | tf_op jit(solution)/shard_map/ppermute | solution.py:49
  104.9 9.4 %collective-permute-start.26 = (bf16[128,512]{1,0:T(8,128)(2,1)S(1)}, bf16[128,512]{1,0:T(8,128)(2,1)S(1)}, u32[]{:S(2)}, u32[]{:S(2)}) collective-permute-start(bf16[128,512]{1,0:T(8,128)(2,1)S(1)} %get-tuple-element.42), channel_id=1, source_target_pairs={{0,4},{1,5},{2,6},{3,7},{4,0},{5,1},{6,2},{7,3},{8,12},{9,13},{10,... | collective-permute-start | bytes 393224 | tf_op jit(solution)/shard_map/ppermute | solution.py:49
  106.6 9.3 %collective-permute-start.27 = (bf16[128,512]{1,0:T(8,128)(2,1)S(1)}, bf16[128,512]{1,0:T(8,128)(2,1)S(1)}, u32[]{:S(2)}, u32[]{:S(2)}) collective-permute-start(bf16[128,512]{1,0:T(8,128)(2,1)S(1)} %get-tuple-element.43), channel_id=1, source_target_pairs={{0,6},{1,7},{2,4},{3,5},{4,2},{5,3},{6,0},{7,1},{8,14},{9,15},{10,... | collective-permute-start | bytes 393224 | tf_op jit(solution)/shard_map/ppermute | solution.py:49
  109.6 10.4 %collective-permute-start.22 = (bf16[128,512]{1,0:T(8,128)(2,1)S(1)}, bf16[128,512]{1,0:T(8,128)(2,1)S(1)}, u32[]{:S(2)}, u32[]{:S(2)}) collective-permute-start(bf16[128,512]{1,0:T(8,128)(2,1)S(1)} %get-tuple-element.37), channel_id=1, source_target_pairs={{0,2},{1,3},{2,0},{3,1},{4,6},{5,7},{6,4},{7,5},{8,10},{9,11},{10,... | collective-permute-start | bytes 393224 | tf_op jit(solution)/shard_map/ppermute | solution.py:49
  109.6 10.4 %collective-permute-start.23 = (bf16[128,512]{1,0:T(8,128)(2,1)S(1)}, bf16[128,512]{1,0:T(8,128)(2,1)S(1)}, u32[]{:S(2)}, u32[]{:S(2)}) collective-permute-start(bf16[128,512]{1,0:T(8,128)(2,1)S(1)} %get-tuple-element.38), channel_id=1, source_target_pairs={{0,4},{1,5},{2,6},{3,7},{4,0},{5,1},{6,2},{7,3},{8,12},{9,13},{10,... | collective-permute-start | bytes 393224 | tf_op jit(solution)/shard_map/ppermute | solution.py:49
  111.3 8.7 %collective-permute-start.24 = (bf16[128,512]{1,0:T(8,128)(2,1)S(1)}, bf16[128,512]{1,0:T(8,128)(2,1)S(1)}, u32[]{:S(2)}, u32[]{:S(2)}) collective-permute-start(bf16[128,512]{1,0:T(8,128)(2,1)S(1)} %get-tuple-element.39), channel_id=1, source_target_pairs={{0,6},{1,7},{2,4},{3,5},{4,2},{5,3},{6,0},{7,1},{8,14},{9,15},{10,... | collective-permute-start | bytes 393224 | tf_op jit(solution)/shard_map/ppermute | solution.py:49
  116.0 6.6 %collective-permute-start.28 = (bf16[128,512]{1,0:T(8,128)(2,1)S(1)}, bf16[128,512]{1,0:T(8,128)(2,1)S(1)}, u32[]{:S(2)}, u32[]{:S(2)}) collective-permute-start(bf16[128,512]{1,0:T(8,128)(2,1)S(1)} %add_convert_fusion.1), channel_id=1, source_target_pairs={{0,8},{1,9},{2,10},{3,11},{4,12},{5,13},{6,14},{7,15},{8,0},{9,1},... | collective-permute-start | bytes 393224 | tf_op jit(solution)/shard_map/ppermute | solution.py:49
  (23 other events, 182.0 us)

commit v3 on v2

v3 whole, which is shorter than its diff:
```python
import functools
import math

import jax
import jax.numpy as jnp
import numpy as np
from jax import lax
from jax.experimental import pallas as pl
from jax.experimental.pallas import tpu as pltpu
from jax.sharding import PartitionSpec as P

BF = jnp.bfloat16
F32 = jnp.float32
EPS = 1e-05
ROPE_BASE = 500000.0
FLOOR = -1e30
HD = 128
BLK = 128
REQ = 64
HEADS = 8
SHARD = 512
CHIPS = 8
MOVE = 8
QW = HEADS * HD
OWN = SHARD + HD
ANY = pl.BlockSpec(memory_space=pl.ANY)
VMEM = pl.BlockSpec(memory_space=pltpu.VMEM)
SMEM = pl.BlockSpec(memory_space=pltpu.SMEM)
MIB = 1024 * 1024


def call(body, ins, outs, scratch, out_shapes, flops, moved, limit=48):
    return pl.pallas_call(
        body,
        out_shape=out_shapes,
        in_specs=ins,
        out_specs=outs,
        scratch_shapes=scratch,
        compiler_params=pltpu.CompilerParams(vmem_limit_bytes=limit * MIB),
        cost_estimate=pl.CostEstimate(flops=flops, bytes_accessed=moved, transcendentals=0),
    )


def shape(dims, kind):
    return jax.ShapeDtypeStruct(dims, kind)


def swap(value, axis, mask):
    count = lax.axis_size(axis)
    return lax.ppermute(value, axis, [(i, i ^ mask) for i in range(count)])


def prepare(
    where, moved, masks, lengths, frequency, cache, wo,
    slots, own_lens, next_lens, tables, rows, wo_out, held, angle, sems, row_sems,
):
    other = 1 - where[0] % 2
    instance = where[1]
    row_copies = [
        pltpu.make_async_copy(cache.at[moved[instance, j]], rows.at[j], row_sems.at[j])
        for j in range(MOVE)
    ]
    reads = []
    writes = []
    for b in range(CHIPS):
        cols = pl.ds(pl.multiple_of((2 * b + other) * SHARD, SHARD), SHARD)
        reads.append(pltpu.make_async_copy(wo.at[:, cols], held.at[b], sems.at[b, 0]))
        writes.append(pltpu.make_async_copy(held.at[b], wo_out.at[b], sems.at[b, 1]))
    for copy in reads + row_copies:
        copy.start()
    for r in range(REQ):
        length = lengths[instance * REQ + r]
        own_lens[r] = length
        next_lens[r] = length
        angle[pl.ds(r, 1), :] = jnp.full((1, HD), length.astype(F32))
        angle[pl.ds(REQ + r, 1), :] = jnp.full((1, HD), (length + 1).astype(F32))
    for j in range(MOVE):
        slot = moved[instance, j]
        partner = instance ^ masks[j]
        length = lengths[partner * REQ + moved[partner, j]]
        slots[j] = slot
        next_lens[slot] = length
        angle[pl.ds(REQ + slot, 1), :] = jnp.full((1, HD), (length + 1).astype(F32))
    turn = angle[...] * frequency[...]
    low = lax.broadcasted_iota(jnp.int32, turn.shape, 1) < HD // 2
    wave = jnp.sin(turn)
    tables[0] = jnp.cos(turn)
    tables[1] = jnp.where(low, -wave, wave)
    for read, write in zip(reads, writes):
        read.wait()
        write.start()
    for copy in row_copies + writes:
        copy.wait()


def project(where, slots, *refs):
    near, (near_sib,) = refs[: CHIPS // 2], refs[CHIPS // 2 : CHIPS // 2 + 1]
    far, (far_sib,) = refs[CHIPS // 2 + 1 : CHIPS + 1], refs[CHIPS + 1 : CHIPS + 2]
    gain, wq, wkv, tables, out, sent, acc, wide = refs[CHIPS + 2 :]
    me = where[0]
    half = CHIPS // 2
    squares = None
    for i in range(2 * CHIPS):
        src = me ^ (2 * (i % half) + (0, 1, 8, 9)[i // half])
        rows = pl.ds(pl.multiple_of(src * SHARD, SHARD), SHARD)
        ref = (near[i % half], near_sib, far[i % half], far_sib)[i // half]
        x = (ref[i % half] if i // half % 2 else ref[...]).astype(F32)
        scaled = (x * gain[pl.ds(src, 1), :]).astype(BF)
        sq = x * x
        part = sq[:, :HD] + sq[:, HD : 2 * HD] + sq[:, 2 * HD : 3 * HD] + sq[:, 3 * HD :]
        squares = part if squares is None else squares + part
        for at, weight in ((pl.ds(0, SHARD), wq), (pl.ds(SHARD, HD), wkv)):
            term = jnp.dot(scaled, weight[rows, :], preferred_element_type=F32)
            if i == 0:
                acc[:, at] = term
            else:
                acc[:, at] += term
    mean = jnp.sum(squares, -1, keepdims=True) * (1.0 / (2 * CHIPS * SHARD))
    scale = lax.rsqrt(mean + EPS)
    cos = tables[0]
    sin = tables[1]

    def turned(vec):
        return vec * cos + pltpu.roll(vec, HD // 2, 1) * sin

    for h in range(SHARD // HD):
        at = pl.ds(h * HD, HD)
        out[:, at] = turned(acc[:, at] * scale).astype(BF)
    raw = acc[:, pl.ds(SHARD, HD)] * scale
    kept = jnp.where(me % 2 == 0, turned(raw), raw).astype(BF)
    out[:, pl.ds(SHARD, HD)] = kept
    wide[...] = kept.astype(F32)
    sent[...] = jnp.zeros_like(sent)
    for j in range(MOVE):
        sent[pl.ds(j, 1), :] = wide[pl.ds(slots[j], 1), :]


def block_terms(queries, blocks, lens):
    scores = []
    for p, block in enumerate(blocks):
        both = jnp.concatenate(queries[2 * p : 2 * p + 2], 0).astype(BF)
        pair = lax.dot_general(
            both, block[:, :HD], (((1,), (1,)), ((), ())), preferred_element_type=F32
        )
        scores += [pair[:HEADS, :BLK], pair[HEADS:, BLK:]]
    lane = lax.broadcasted_iota(jnp.int32, (HEADS, BLK), 1)
    visible = jnp.concatenate([(lane < length).astype(F32) for length in lens], 0) > 0.0
    scores = jnp.where(visible, jnp.concatenate(scores, 0) * (1.0 / math.sqrt(HD)), FLOOR)
    top = jnp.max(scores, -1, keepdims=True)
    weights = jnp.where(visible, jnp.exp(scores - top), 0.0).astype(BF).astype(F32)
    total = jnp.sum(weights, -1, keepdims=True)
    zero = jnp.zeros((HEADS, BLK), F32)
    mixes = []
    for p, block in enumerate(blocks):
        at = 2 * p * HEADS
        one, two = weights[at : at + HEADS], weights[at + HEADS : at + 2 * HEADS]
        both = jnp.concatenate(
            [jnp.concatenate([one, zero], 1), jnp.concatenate([zero, two], 1)], 0
        ).astype(BF)
        mixes.append(jnp.dot(both, block[:, HD:], preferred_element_type=F32))
    return top, total, mixes


def noted(stats, slot, top, total):
    lane = lax.broadcasted_iota(jnp.int32, (HEADS, HD), 1)
    stats = jnp.where(lane == slot, top, stats)
    return jnp.where(lane == slot + REQ, total, stats)


def attend(step, where, lens, mine, recv, cache, terms, q_out, fresh_out, kv, sems):
    core = where[0] % 2
    base = core * BLK
    chunks = 4
    per = REQ // chunks
    copies = []
    for i in range(chunks):
        copies.append(
            pltpu.make_async_copy(cache.at[pl.ds(i * per, per)], kv.at[pl.ds(i * per, per)], sems.at[i])
        )
    for copy in copies:
        copy.start()
    rows = pl.ds(step * REQ, REQ)
    first = core == 0
    own = HEADS // 2

    def either(low_core, col):
        one = mine[rows, pl.ds(col, HD)].astype(F32)
        two = recv[rows, pl.ds(col, HD)].astype(F32)
        return jnp.where(first, one, two) if low_core else jnp.where(first, two, one)

    for h in range(HEADS):
        q_out[pl.ds(h, REQ, stride=HEADS), :] = either(h < own, (h % own) * HD)
    fresh_out[:, pl.ds(0, HD)] = either(True, SHARD)
    fresh_out[:, pl.ds(HD, HD)] = either(False, SHARD)

    stats = jnp.zeros((HEADS, HD), F32)
    for i in range(chunks):
        copies[i].wait()
        mine_r = range(i * per, (i + 1) * per)
        top, total, mixes = block_terms(
            [q_out[pl.ds(r * HEADS, HEADS), :] for r in mine_r],
            [kv[pl.ds(r, 2)].reshape(2 * BLK, 2 * HD) for r in mine_r[::2]],
            [jnp.clip(lens[r] - base, 0, BLK) for r in mine_r],
        )
        for j, r in enumerate(mine_r):
            at = slice(j * HEADS, (j + 1) * HEADS)
            stats = noted(stats, r, top[at], total[at])
            if j % 2 == 0:
                terms[pl.ds(r * HEADS, 2 * HEADS), :] = mixes[j // 2]
    terms[pl.ds(REQ * HEADS, HEADS), :] = stats


def attend_arrived(where, lens, slots, q, arrived, terms):
    base = where[0] % 2 * BLK
    top, total, mixes = block_terms(
        [q[pl.ds(pl.multiple_of(slots[j] * HEADS, HEADS), HEADS), :] for j in range(MOVE)],
        [arrived[pl.ds(j, 2)].reshape(2 * BLK, 2 * HD) for j in range(0, MOVE, 2)],
        [jnp.clip(lens[slots[j]] - base, 0, BLK) for j in range(MOVE)],
    )
    stats = jnp.zeros((HEADS, HD), F32)
    for j in range(MOVE):
        at = slice(j * HEADS, (j + 1) * HEADS)
        stats = noted(stats, j, top[at], total[at])
        if j % 2 == 0:
            terms[pl.ds(j * HEADS, 2 * HEADS), :] = mixes[j // 2]
    terms[pl.ds(MOVE * HEADS, HEADS), :] = stats


def attended(mine, recv, q, fresh, flat, att):
    lane = lax.broadcasted_iota(jnp.int32, (HEADS, REQ), 1)
    stats_m = mine[pl.ds(REQ * HEADS, HEADS), :]
    stats_r = recv[pl.ds(REQ * HEADS, HEADS), :]
    tops = [stats_m[:, :REQ], stats_r[:, :REQ]]
    sums = [stats_m[:, REQ:], stats_r[:, REQ:]]
    for row in fresh:
        keys = row[:, pl.ds(0, HD)].astype(BF)
        scores = lax.dot_general(
            q[...].astype(BF), keys, (((1,), (1,)), ((), ())), preferred_element_type=F32
        )
        taken = [
            jnp.where(lane == r, scores[r * HEADS : (r + 1) * HEADS], 0.0) for r in range(REQ)
        ]
        while len(taken) > 1:
            taken = [taken[i] + taken[i + 1] for i in range(0, len(taken), 2)]
        tops.append(taken[0] * (1.0 / math.sqrt(HD)))
        sums.append(1.0)
    overall = functools.reduce(jnp.maximum, tops)
    factors = [jnp.exp(top - overall) for top in tops]
    below = functools.reduce(jnp.add, [f * s for f, s in zip(factors, sums)])
    factors = [f / below for f in factors]
    for r in range(REQ):
        at = pl.ds(r * HEADS, HEADS)
        mixes = [mine[at, :], recv[at, :]] + [row[pl.ds(r, 1), pl.ds(HD, HD)] for row in fresh]
        flat[at, :] = functools.reduce(
            jnp.add, [f[:, r : r + 1] * mix for f, mix in zip(factors, mixes)]
        )
    for h in range(HEADS):
        att[:, pl.ds(h * HD, HD)] = flat[
            pl.ds(h, REQ, stride=HEADS), :
        ].astype(BF)


def out_copies(where, blocks, wo, wos, own_buf, sib_buf, sems):
    me = where[0]
    pending = []
    for n, i in enumerate(blocks):
        dst = me ^ (8 + 2 * i if i < 4 else 2 * (i - 4))
        cols = pl.ds(pl.multiple_of(dst * SHARD, SHARD), SHARD)
        group = [
            pltpu.make_async_copy(wo.at[:, cols], own_buf.at[n], sems.at[n, 0]),
            pltpu.make_async_copy(wos.at[dst // 2], sib_buf.at[n], sems.at[n, 1]),
        ]
        for copy in group:
            copy.start()
        pending.append(group)
    return pending


def out_blocks(where, att, pending, own_buf, sib_buf):
    core = where[0] % 2
    own = att[:, pl.ds(pl.multiple_of(core * SHARD, SHARD), SHARD)]
    sib = att[:, pl.ds(pl.multiple_of(SHARD - core * SHARD, SHARD), SHARD)]
    for n, group in enumerate(pending):
        for copy in group:
            copy.wait()
        yield (
            jnp.dot(own, own_buf[n], preferred_element_type=F32)
            + jnp.dot(sib, sib_buf[n], preferred_element_type=F32)
        ).astype(BF)


def finish_first(where, mine, recv, q, fresh, wo, wos, *refs):
    outs = refs[:CHIPS]
    own_buf, sib_buf, flat, att, sems = refs[CHIPS:]
    pending = out_copies(where, range(CHIPS), wo, wos, own_buf, sib_buf, sems)
    attended(mine, recv, q, [fresh], flat, att)
    for out, block in zip(outs, out_blocks(where, att, pending, own_buf, sib_buf)):
        out[...] = block


def finish_other(where, slots, mine, recv, late, late_sib, q, f1, f2, came, came_sib, wo, wos, *refs):
    half = CHIPS // 2
    before, outs = refs[:half], refs[half : 2 * half]
    att, own_buf, sib_buf, carried, flat, own_terms, sib_terms, sems = refs[2 * half :]
    pending = out_copies(where, range(half), wo, wos, own_buf, sib_buf, sems)
    carried[...] = f1[...]
    first = where[0] % 2 == 0
    keys = jnp.where(first, came[...], came_sib[...])
    values = jnp.where(first, came_sib[...], came[...])
    arrived = jnp.concatenate([keys, values], 1)
    for j in range(MOVE):
        carried[pl.ds(slots[j], 1), :] = arrived[j : j + 1]
    for kept, whole, some in ((own_terms, mine, late), (sib_terms, recv, late_sib)):
        kept[...] = whole[...]
        stats = kept[pl.ds(REQ * HEADS, HEADS), :]
        fixes = some[pl.ds(MOVE * HEADS, HEADS), :]
        for j in range(MOVE):
            at = pl.ds(pl.multiple_of(slots[j] * HEADS, HEADS), HEADS)
            kept[at, :] = some[pl.ds(j * HEADS, HEADS), :]
            stats = noted(stats, slots[j], fixes[:, j : j + 1], fixes[:, REQ + j : REQ + j + 1])
        kept[pl.ds(REQ * HEADS, HEADS), :] = stats
    attended(own_terms, sib_terms, q, [carried, f2], flat, att)
    for old, out, block in zip(before, outs, out_blocks(where, att, pending, own_buf, sib_buf)):
        out[pl.ds(0, REQ), :] = old[...]
        out[pl.ds(REQ, REQ), :] = block


def finish_same(where, att, wo, wos, *refs):
    half = CHIPS // 2
    before, outs = refs[:half], refs[half : 2 * half]
    own_buf, sib_buf, sems = refs[2 * half :]
    pending = out_copies(where, range(half, CHIPS), wo, wos, own_buf, sib_buf, sems)
    for old, out, block in zip(before, outs, out_blocks(where, att, pending, own_buf, sib_buf)):
        out[pl.ds(0, REQ), :] = old[...]
        out[pl.ds(REQ, REQ), :] = block


def shards(
    x_steps, norm_gain, w_query, w_keyval, w_out, key_cache, lengths, moved_slots, partner_mask
):
    dma = pltpu.SemaphoreType.DMA
    me = lax.axis_index("tp")
    instance = lax.axis_index("inst")
    where = jnp.reshape(me, (1,)).astype(jnp.int32)
    cache = key_cache[:, 0]

    rows = 2 * REQ
    powers = ROPE_BASE ** (-(np.arange(HD // 2, dtype=np.float32) * 2.0) / HD)
    frequency = jnp.asarray(np.concatenate([powers, powers])[None].astype(np.float32))
    slots, own_lengths, next_lengths, tables, moving, wo_send = call(
        prepare,
        [SMEM] * 4 + [VMEM] + [ANY] * 2,
        [SMEM] * 3 + [VMEM] * 2 + [ANY],
        [
            pltpu.VMEM((CHIPS, SHARD, SHARD), BF),
            pltpu.VMEM((rows, HD), F32),
            dma((CHIPS, 2)),
            dma((MOVE,)),
        ],
        [
            shape((MOVE,), jnp.int32),
            shape((REQ,), jnp.int32),
            shape((REQ,), jnp.int32),
            shape((2, rows, HD), F32),
            shape((MOVE, BLK, 2 * HD), BF),
            shape((CHIPS, SHARD, SHARD), BF),
        ],
        0,
        10 << 20,
        58,
    )(jnp.stack([me, instance]).astype(jnp.int32), moved_slots, partner_mask, lengths, frequency, cache, w_out)
    own_x = x_steps.reshape(2 * REQ, SHARD)
    own_x, slots, own_lengths, next_lengths, tables, moving, wo_send = (
        lax.optimization_barrier(
            (own_x, slots, own_lengths, next_lengths, tables, moving, wo_send)
        )
    )

    far_x = swap(own_x, "tp", 8)
    near = [own_x] + [swap(own_x, "tp", 2 * i) for i in (1, 2, 3)]
    far = [far_x] + [swap(far_x, "tp", 2 * i) for i in (1, 2, 3)]
    near_sib = swap(jnp.stack(near), "tp", 1)

    def hop(part, bit, masks):
        took = ((masks >> bit) & 1 == 1).reshape((-1,) + (1,) * (part.ndim - 1))
        return jnp.where(took, swap(part, "inst", 1 << bit), part)

    moving = hop(moving, 2, partner_mask)
    far_all, moving = lax.optimization_barrier((jnp.stack(far), moving))
    far_sib = swap(far_all, "tp", 1)
    moving = hop(moving, 1, partner_mask)

    half_chips = CHIPS // 2
    gain = norm_gain.reshape(2 * CHIPS, SHARD)
    queries, sent = call(
        project,
        [SMEM] * 2 + [VMEM] * (CHIPS + 6),
        [VMEM] * 2,
        [pltpu.VMEM((rows, OWN), F32), pltpu.VMEM((rows, HD), F32)],
        [shape((rows, OWN), BF), shape((2 * MOVE, HD), F32)],
        2 * rows * 2 * CHIPS * SHARD * OWN,
        12 << 20,
        20,
    )(
        where,
        slots,
        *near,
        near_sib,
        *far,
        far_sib,
        gain,
        w_query,
        w_keyval,
        tables,
    )
    queries_sib = swap(queries, "tp", 1)
    wos = swap(wo_send, "tp", 1)
    came = sent.astype(BF)
    masks = jnp.concatenate([partner_mask, partner_mask])
    came = hop(came, 0, masks)
    came, queries_sib, moving = lax.optimization_barrier((came, queries_sib, moving))
    moving = hop(moving, 0, partner_mask)
    came = hop(came, 1, masks)

    term_shape = shape((REQ * HEADS + HEADS, HD), F32)
    q_shape = shape((REQ * HEADS, HD), F32)
    fresh_shape = shape((REQ, 2 * HD), F32)
    kv_scratch = pltpu.VMEM((REQ, BLK, 2 * HD), BF)
    t1, q1, f1 = call(
        functools.partial(attend, 0),
        [SMEM] * 2 + [VMEM] * 2 + [ANY],
        [VMEM] * 3,
        [kv_scratch, dma((4,))],
        [term_shape, q_shape, fresh_shape],
        4 * REQ * HEADS * BLK * HD,
        6 << 20,
    )(where, own_lengths, queries, queries_sib, cache)
    t1, came = lax.optimization_barrier((t1, came))
    t1_sib = swap(t1, "tp", 1)
    came = hop(came, 2, masks)
    t2, q2, f2 = call(
        functools.partial(attend, 1),
        [SMEM] * 2 + [VMEM] * 2 + [ANY],
        [VMEM] * 3,
        [kv_scratch, dma((4,))],
        [term_shape, q_shape, fresh_shape],
        4 * REQ * HEADS * BLK * HD,
        6 << 20,
    )(where, next_lengths, queries, queries_sib, cache)
    t2, came = lax.optimization_barrier((t2, came))
    t2_sib = swap(t2, "tp", 1)
    came_sib = swap(came, "tp", 1)

    def weights(count):
        return [pltpu.VMEM((count, SHARD, SHARD), BF)] * 2

    flat = pltpu.VMEM((REQ * HEADS, HD), F32)
    block = shape((REQ, SHARD), BF)
    both = shape((rows, SHARD), BF)
    firsts = call(
        finish_first,
        [SMEM] + [VMEM] * 4 + [ANY] * 2,
        [VMEM] * CHIPS,
        weights(CHIPS) + [flat, pltpu.VMEM((REQ, QW), BF), dma((CHIPS, 2))],
        [block] * CHIPS,
        2 * REQ * QW * CHIPS * SHARD,
        10 << 20,
    )(where, t1, t1_sib, q1, f1, w_out, wos)
    first_half, moving = lax.optimization_barrier((firsts[:half_chips], moving))
    t3 = call(
        attend_arrived,
        [SMEM] * 3 + [VMEM] * 2,
        VMEM,
        [],
        shape((MOVE * HEADS + HEADS, HD), F32),
        4 * MOVE * HEADS * BLK * HD,
        1 << 20,
    )(where, next_lengths, slots, q2, moving)
    t3_sib = swap(t3, "tp", 1)
    *others, att = call(
        finish_other,
        [SMEM] * 2 + [VMEM] * 9 + [ANY] * 2 + [VMEM] * half_chips,
        [VMEM] * (half_chips + 1),
        weights(half_chips)
        + [pltpu.VMEM((REQ, 2 * HD), F32), flat]
        + [pltpu.VMEM(term_shape.shape, F32)] * 2
        + [dma((half_chips, 2))],
        [both] * half_chips + [shape((REQ, QW), BF)],
        REQ * QW * CHIPS * SHARD,
        6 << 20,
    )(
        where, slots, t2, t2_sib, t3, t3_sib, q2, f1, f2, came.astype(F32), came_sib.astype(F32), w_out, wos,
        *first_half,
    )
    sames = call(
        finish_same,
        [SMEM] + [VMEM] + [ANY] * 2 + [VMEM] * half_chips,
        [VMEM] * half_chips,
        weights(half_chips) + [dma((half_chips, 2))],
        [both] * half_chips,
        REQ * QW * CHIPS * SHARD,
        5 << 20,
    )(where, att, w_out, wos, *firsts[half_chips:])
    parts = list(others) + list(sames)

    def added(values):
        return functools.reduce(jnp.add, [value.astype(F32) for value in values])

    other = added([parts[0]] + [swap(parts[i], "tp", 2 * i) for i in (1, 2, 3)]).astype(BF)
    crossed = swap(other, "tp", 8)
    same = added([parts[4]] + [swap(parts[4 + i], "tp", 2 * i) for i in (1, 2, 3)])
    out = (same + crossed.astype(F32)).astype(BF)
    return out.reshape(2, REQ, SHARD), moving[:, None]


def solution(mesh):
    placed = (
        P(None, "inst", "tp"),
        P(),
        P(None, "tp"),
        P(None, "tp"),
        P("tp", None),
        P("inst", "tp", None, None),
        P(),
        P(),
        P(),
    )
    return jax.shard_map(
        shards,
        mesh=mesh,
        in_specs=placed,
        out_specs=(P(None, "inst", "tp"), P("inst", "tp", None, None)),
        check_vma=False,
    )
```

time: 124 us -> 94.6 us (0.76)
  waiting for transfers between devices: 36.5 us -> 18.3 us
  local copies, waits for them, and re-layouts: 13.5 us -> 5.11 us
  Pallas kernels: 28.5 us -> 25.6 us
  starting transfers between devices: 35.7 us -> 37.5 us
    ppermute x29 -> x28, waiting for transfers between devices: 36.5 us -> 18.3 us  [swap(): return lax.ppermute(value, axis, [(i, i ^ mask) for i in range(count)])]
    unnamed x53 -> x24, local copies, waits for them, and re-layouts: 10.3 us -> 5.11 us
    pallas_call x7 -> x8, Pallas kernels: 28.5 us -> 25.6 us  [the longest x1 6.03 us: shards(): call(prepare, [SMEM] * 4 + [VMEM] + [ANY] * 2, [SMEM] * 3 + [VMEM] * 2 +...]
    another operation x0 -> x3, other arithmetic: none -> 2.38 us  [the longest x1 0.88 us: shards(): near_sib = swap(jnp.stack(near), 'tp', 1)]
    select_n x8 -> x6, other arithmetic: 1.78 us -> 3.64 us  [hop(): return jnp.where(took, swap(part, 'inst', 1 << bit), part)]
    ppermute x29 -> x28, starting transfers between devices: 35.7 us -> 37.5 us  [swap(): return lax.ppermute(value, axis, [(i, i ^ mask) for i in range(count)])]
    neg x1 -> x0, other arithmetic: 1.62 us -> none  [tables(): return (jnp.concatenate([cos, cos], 1), jnp.concatenate([-sin, sin], 1))]
    reshape x1, local copies, waits for them, and re-layouts: 1.37 us -> 0.01 us  [shards(): gain = norm_gain.reshape(2 * CHIPS, SHARD)]
  transfers between devices with their start and end apart: 29 -> 28, of which waited for: 9 -> 10; matrix products, arithmetic and copies ran while one was open for 9% -> 6% of each run, Pallas kernels for 15% -> 17%
where the time goes in v3:
time: 94.6 us; the launch traced here: 94.3 us
  starting transfers between devices  37.5 us (40%)
  Pallas kernels  25.6 us (27%)
  waiting for transfers between devices  18.3 us (19%)
  other arithmetic  6.93 us (7%)
  local copies, waits for them, and re-layouts  5.11 us (5%)
    ppermute x28, starting transfers between devices, swap(): return lax.ppermute(value, axis, [(i, i ^ mask) for i in range(count)])  37.5 us
    ppermute x28, waiting for transfers between devices, swap(): return lax.ppermute(value, axis, [(i, i ^ mask) for i in range(count)])  18.3 us
    pallas_call x1, Pallas kernels, shards(): call(prepare, [SMEM] * 4 + [VMEM] + [ANY] * 2, [SMEM] * 3 + [VMEM] * 2 +...  6.03 us
    unnamed x24, local copies, waits for them, and re-layouts  5.11 us
    pallas_call x1, Pallas kernels, shards(): call(finish_first, [SMEM] + [VMEM] * 4 + [ANY] * 2, [VMEM] * CHIPS, weigh...  4.12 us
    select_n x6, other arithmetic, hop(): return jnp.where(took, swap(part, 'inst', 1 << bit), part)  3.64 us
    pallas_call x1, Pallas kernels, shards(): call(finish_other, [SMEM] * 2 + [VMEM] * 9 + [ANY] * 2 + [VMEM] * half_ch...  3.23 us
    pallas_call x1, Pallas kernels, shards(): call(project, [SMEM] * 2 + [VMEM] * (CHIPS + 6), [VMEM] * 2, [pltpu.VMEM(...  3.18 us
  transfers between devices with their start and end apart: 28, of which 10 were waited for; matrix products, arithmetic and copies ran while one was open for 6% of the time, Pallas kernels for 17%

profile of v3, /device:TPU:0, one launch (start us, length us, event | category | flops | bytes accessed | tf_op | source)
XLA Modules:
  0.0 94.3 jit_solution(11892355783650485567)
XLA Ops:
  1.3 6.0 %shard_map.113 = (s32[8]{0:T(128)}, s32[64]{0:T(128)}, s32[64]{0:T(128)}, f32[2,128,128]{2,1,0:T(8,128)}, bf16[8,128,256]{2,1,0:T(8,128)(2,1)}, /*index=5*/bf16[8,512,512]{2,1,0:T(8,128)(2,1)}) custom-call(s32[2]{0:T(128)} %pad_add_fusion.where, s32[8,8]{1,0:T(8,128)} %moved.1, s32[8]{0:T(128)} %masks.1, s32[512]{0:T(512)} %lengths.1, ...), custom_call_target="tpu_custom_call" | custom-call | bytes 10485760 | tf_op jit(solution)/shard_map/pallas_call | solution.py:350
  7.4 3.2 %collective-permute-start.4 = (bf16[128,512]{1,0:T(8,128)(2,1)S(1)}, bf16[128,512]{1,0:T(8,128)(2,1)S(1)}, u32[]{:S(2)}, u32[]{:S(2)}) collective-permute-start(bf16[128,512]{1,0:T(8,128)(2,1)S(1)} %bitcast.20), channel_id=1, source_target_pairs={{0,8},{1,9},{2,10},{3,11},{4,12},{5,13},{6,14},{7,15},{8,0},{9,1},... | collective-permute-start | bytes 393224 | tf_op jit(solution)/shard_map/ppermute | solution.py:50
  10.6 1.6 %collective-permute-start = (bf16[128,512]{1,0:T(8,128)(2,1)S(1)}, bf16[128,512]{1,0:T(8,128)(2,1)S(1)}, u32[]{:S(2)}, u32[]{:S(2)}) collective-permute-start(bf16[128,512]{1,0:T(8,128)(2,1)S(1)} %bitcast.21), channel_id=1, source_target_pairs={{0,2},{1,3},{2,0},{3,1},{4,6},{5,7},{6,4},{7,5},{8,10},{9,11},{10,... | collective-permute-start | bytes 393224 | tf_op jit(solution)/shard_map/ppermute | solution.py:50
  12.2 2.9 %collective-permute-start.1 = (bf16[128,512]{1,0:T(8,128)(2,1)S(1)}, bf16[128,512]{1,0:T(8,128)(2,1)S(1)}, u32[]{:S(2)}, u32[]{:S(2)}) collective-permute-start(bf16[128,512]{1,0:T(8,128)(2,1)S(1)} %bitcast.22), channel_id=1, source_target_pairs={{0,4},{1,5},{2,6},{3,7},{4,0},{5,1},{6,2},{7,3},{8,12},{9,13},{10,... | collective-permute-start | bytes 393224 | tf_op jit(solution)/shard_map/ppermute | solution.py:50
  15.3 3.9 %collective-permute-start.8 = (bf16[8,128,256]{2,1,0:T(8,128)(2,1)}, bf16[8,128,256]{2,1,0:T(8,128)(2,1)S(1)}, u32[]{:S(2)}, u32[]{:S(2)}) collective-permute-start(bf16[8,128,256]{2,1,0:T(8,128)(2,1)} %get-tuple-element.63), channel_id=1, source_target_pairs={{0,64},{16,80},{32,96},{48,112},{64,0},{80,16},{96,32},{112,48},{1... | collective-permute-start | bytes 1572872 | tf_op jit(solution)/shard_map/ppermute | solution.py:50
  19.2 2.8 %collective-permute-start.6 = (bf16[128,512]{1,0:T(8,128)(2,1)S(1)}, bf16[128,512]{1,0:T(8,128)(2,1)S(1)}, u32[]{:S(2)}, u32[]{:S(2)}) collective-permute-start(bf16[128,512]{1,0:T(8,128)(2,1)S(1)} %collective-permute-done.4.refs_5_), channel_id=1, source_target_pairs={{0,4},{1,5},{2,6},{3,7},{4,0},{5,1},{6,2},{7,3},{8,12},{9,13},{10,... | collective-permute-start | bytes 393224 | tf_op jit(solution)/shard_map/ppermute | solution.py:50
  22.0 1.1 %collective-permute-start.7 = (bf16[128,512]{1,0:T(8,128)(2,1)S(1)}, bf16[128,512]{1,0:T(8,128)(2,1)S(1)}, u32[]{:S(2)}, u32[]{:S(2)}) collective-permute-start(bf16[128,512]{1,0:T(8,128)(2,1)S(1)} %collective-permute-done.4.refs_5_), channel_id=1, source_target_pairs={{0,6},{1,7},{2,4},{3,5},{4,2},{5,3},{6,0},{7,1},{8,14},{9,15},{10,... | collective-permute-start | bytes 393224 | tf_op jit(solution)/shard_map/ppermute | solution.py:50
  23.1 4.1 %collective-permute-done.2.refs_3_ = bf16[128,512]{1,0:T(8,128)(2,1)S(1)} collective-permute-done((bf16[128,512]{1,0:T(8,128)(2,1)S(1)}, bf16[128,512]{1,0:T(8,128)(2,1)S(1)}, u32[]{:S(2)}, u32[]{:S(2)}) %collective-permute-start.2) | collective-permute-done | bytes 131104 | tf_op jit(solution)/shard_map/ppermute | solution.py:50
  28.1 1.3 %collective-permute-done.7.refs_8_ = bf16[128,512]{1,0:T(8,128)(2,1)S(1)} collective-permute-done((bf16[128,512]{1,0:T(8,128)(2,1)S(1)}, bf16[128,512]{1,0:T(8,128)(2,1)S(1)}, u32[]{:S(2)}, u32[]{:S(2)}) %collective-permute-start.7) | collective-permute-done | bytes 131104 | tf_op jit(solution)/shard_map/ppermute | solution.py:50
  29.4 2.8 %collective-permute-done.5.refs_6_ = bf16[128,512]{1,0:T(8,128)(2,1)S(1)} collective-permute-done((bf16[128,512]{1,0:T(8,128)(2,1)S(1)}, bf16[128,512]{1,0:T(8,128)(2,1)S(1)}, u32[]{:S(2)}, u32[]{:S(2)}) %collective-permute-start.5) | collective-permute-done | bytes 131104 | tf_op jit(solution)/shard_map/ppermute | solution.py:50
  33.0 2.0 %broadcast_select_fusion.2 = bf16[8,128,256]{2,1,0:T(8,128)(2,1)} fusion(bf16[8,128,256]{2,1,0:T(8,128)(2,1)S(1)} %collective-permute-done.8, bf16[8,128,256]{2,1,0:T(8,128)(2,1)} %get-tuple-element.63, pred[8]{0:T(512)(128)(4,1)S(1)} %get-tuple-element.109), kind=kLoop, calls=%fused_computation.4 | loop fusion | flops 262144 | bytes 1572872 | tf_op jit(solution)/shard_map/jit(_where)/select_n | solution.py:386
  35.0 1.9 %collective-permute-start.12 = (bf16[8,128,256]{2,1,0:T(8,128)(2,1)}, bf16[8,128,256]{2,1,0:T(8,128)(2,1)}, u32[]{:S(2)}, u32[]{:S(2)}) collective-permute-start(bf16[8,128,256]{2,1,0:T(8,128)(2,1)} %broadcast_select_fusion.2), channel_id=1, source_target_pairs={{0,32},{16,48},{32,0},{48,16},{64,96},{80,112},{96,64},{112,80},{1... | collective-permute-start | bytes 1572872 | tf_op jit(solution)/shard_map/ppermute | solution.py:50
  37.2 3.5 %copy-done.1 = bf16[8192,512]{1,0:T(8,128)(2,1)S(1)} copy-done((bf16[8192,512]{1,0:T(8,128)(2,1)S(1)}, bf16[8192,512]{1,0:T(8,128)(2,1)}, u32[]{:S(2)}) %copy-start.1) | copy-done | bytes 8388632
  42.3 3.2 %shard_map.114 = (bf16[128,640]{1,0:T(8,128)(2,1)S(1)}, f32[16,128]{1,0:T(8,128)S(1)}) custom-call(s32[1]{0:T(128)} %bitcast.where, s32[8]{0:T(128)S(1)} %copy-done.6, bf16[128,512]{1,0:T(8,128)(2,1)S(1)} %bitcast.25, bf16[128,512]{1,0:T(8,128)(2,1)S(1)} %collective-permute-done.refs_1_, bf16[128,512]{1,0:T(8,128)(2,1)S(1)} %collective-permute-done.1.refs_2_, ...), custom_call_target="tpu_custom_call" | custom-call | flops 1342177280 | bytes 12582912 | tf_op jit(solution)/shard_map/pallas_call | solution.py:395
  46.3 3.5 %collective-permute-done.12 = bf16[8,128,256]{2,1,0:T(8,128)(2,1)} collective-permute-done((bf16[8,128,256]{2,1,0:T(8,128)(2,1)}, bf16[8,128,256]{2,1,0:T(8,128)(2,1)}, u32[]{:S(2)}, u32[]{:S(2)}) %collective-permute-start.12) | collective-permute-done | bytes 524320 | tf_op jit(solution)/shard_map/ppermute | solution.py:50
  49.8 1.3 %broadcast_select_fusion.1 = bf16[8,128,256]{2,1,0:T(8,128)(2,1)S(1)} fusion(bf16[8,128,256]{2,1,0:T(8,128)(2,1)} %collective-permute-done.12, bf16[8,128,256]{2,1,0:T(8,128)(2,1)} %broadcast_select_fusion.2, pred[8]{0:T(512)(128)(4,1)S(1)} %get-tuple-element.110), kind=kLoop, calls=%fused_computation.3 | loop fusion | flops 262144 | bytes 1572872 | tf_op jit(solution)/shard_map/jit(_where)/select_n | solution.py:386
  51.8 1.7 %collective-permute-start.13 = (bf16[16,128]{1,0:T(8,128)(2,1)S(1)}, bf16[16,128]{1,0:T(8,128)(2,1)S(1)}, u32[]{:S(2)}, u32[]{:S(2)}) collective-permute-start(bf16[16,128]{1,0:T(8,128)(2,1)S(1)} %broadcast_select_fusion.5), channel_id=1, source_target_pairs={{0,32},{16,48},{32,0},{48,16},{64,96},{80,112},{96,64},{112,80},{1... | collective-permute-start | bytes 12296 | tf_op jit(solution)/shard_map/ppermute | solution.py:50
  53.6 2.8 %shard_map.116 = (f32[520,128]{1,0:T(8,128)S(1)}, f32[512,128]{1,0:T(8,128)S(1)}, f32[64,256]{1,0:T(8,128)S(1)}) custom-call(s32[1]{0:T(128)} %bitcast.where, s32[64]{0:T(128)S(1)} %copy-done.9, bf16[128,640]{1,0:T(8,128)(2,1)S(1)} %get-tuple-element.66.mine, bf16[128,640]{1,0:T(8,128)(2,1)S(1)} %collective-permute-done.11.recv, ...), custom_call_target="tpu_custom_call" | custom-call | flops 33554432 | bytes 6291456 | tf_op jit(solution)/shard_map/pallas_call | solution.py:429
  56.4 3.6 %collective-permute-start.14 = (bf16[16,128]{1,0:T(8,128)(2,1)S(1)}, bf16[16,128]{1,0:T(8,128)(2,1)S(1)}, u32[]{:S(2)}, u32[]{:S(2)}) collective-permute-start(bf16[16,128]{1,0:T(8,128)(2,1)S(1)} %broadcast_select_fusion.3), channel_id=1, source_target_pairs={{0,64},{16,80},{32,96},{48,112},{64,0},{80,16},{96,32},{112,48},{1... | collective-permute-start | bytes 12296 | tf_op jit(solution)/shard_map/ppermute | solution.py:50
  60.1 2.8 %shard_map.115 = (f32[520,128]{1,0:T(8,128)S(1)}, f32[512,128]{1,0:T(8,128)S(1)}, f32[64,256]{1,0:T(8,128)S(1)}) custom-call(s32[1]{0:T(128)} %bitcast.where, s32[64]{0:T(128)S(1)} %copy-done.8, bf16[128,640]{1,0:T(8,128)(2,1)S(1)} %get-tuple-element.66.mine, bf16[128,640]{1,0:T(8,128)(2,1)S(1)} %collective-permute-done.11.recv, ...), custom_call_target="tpu_custom_call" | custom-call | flops 33554432 | bytes 6291456 | tf_op jit(solution)/shard_map/pallas_call | solution.py:441
  63.7 1.2 %collective-permute-done.18 = bf16[8,128,256]{2,1,0:T(8,128)(2,1)S(1)} collective-permute-done((bf16[8,128,256]{2,1,0:T(8,128)(2,1)S(1)}, bf16[8,128,256]{2,1,0:T(8,128)(2,1)S(1)}, u32[]{:S(2)}, u32[]{:S(2)}) %collective-permute-start.18) | collective-permute-done | bytes 524320 | tf_op jit(solution)/shard_map/ppermute | solution.py:50
  65.1 4.1 %shard_map.117 = (bf16[64,512]{1,0:T(8,128)(2,1)S(1)}, bf16[64,512]{1,0:T(8,128)(2,1)S(1)}, bf16[64,512]{1,0:T(8,128)(2,1)S(1)}, bf16[64,512]{1,0:T(8,128)(2,1)S...) custom-call(s32[1]{0:T(128)} %bitcast.where, ...), custom_call_target="tpu_custom_call" | custom-call | flops 536870912 | bytes 10485760 | tf_op jit(solution)/shard_map/pallas_call | solution.py:460
  69.2 0.9 shard_map.118.late
  71.6 3.2 %shard_map.119 = (bf16[128,512]{1,0:T(8,128)(2,1)S(1)}, bf16[128,512]{1,0:T(8,128)(2,1)S(1)}, bf16[128,512]{1,0:T(8,128)(2,1)S(1)}, bf16[128,512]{1,0:T(8,128)(2,1)S(1)}, bf16[64,1024]{1,0:T(8,128)(2,1)S(1)}) custom-call(s32[1]{0:T(128)} %bitcast.where, s32[8]{0:T(128)S(1)} %copy-done.7, f32[520,128]{1,0:T(8,128)S(1)} %get-tuple-element.75.mine, ...), custom_call_target="tpu_custom_call" | custom-call | flops 268435456 | bytes 6291456 | tf_op jit(solution)/shard_map/pallas_call | solution.py:480
  74.9 2.0 %collective-permute-start.25 = (bf16[128,512]{1,0:T(8,128)(2,1)S(1)}, bf16[128,512]{1,0:T(8,128)(2,1)S(1)}, u32[]{:S(2)}, u32[]{:S(2)}) collective-permute-start(bf16[128,512]{1,0:T(8,128)(2,1)S(1)} %get-tuple-element.104), channel_id=1, source_target_pairs={{0,4},{1,5},{2,6},{3,7},{4,0},{5,1},{6,2},{7,3},{8,12},{9,13},{10,... | collective-permute-start | bytes 393224 | tf_op jit(solution)/shard_map/ppermute | solution.py:50
  76.9 2.7 %collective-permute-start.26 = (bf16[128,512]{1,0:T(8,128)(2,1)S(1)}, bf16[128,512]{1,0:T(8,128)(2,1)S(1)}, u32[]{:S(2)}, u32[]{:S(2)}) collective-permute-start(bf16[128,512]{1,0:T(8,128)(2,1)S(1)} %get-tuple-element.105), channel_id=1, source_target_pairs={{0,6},{1,7},{2,4},{3,5},{4,2},{5,3},{6,0},{7,1},{8,14},{9,15},{10,... | collective-permute-start | bytes 393224 | tf_op jit(solution)/shard_map/ppermute | solution.py:50
  79.6 2.5 %shard_map.120 = (bf16[128,512]{1,0:T(8,128)(2,1)S(1)}, bf16[128,512]{1,0:T(8,128)(2,1)S(1)}, bf16[128,512]{1,0:T(8,128)(2,1)S(1)}, bf16[128,512]{1,0:T(8,128)(2,1)S(1)}) custom-call(s32[1]{0:T(128)} %bitcast.where, bf16[64,1024]{1,0:T(8,128)(2,1)S(1)} %get-tuple-element.93.att, bf16[512,8192]{1,0:T(8,128)(2,1)} %wo.7, ...), custom_call_target="tpu_custom_call" | custom-call | flops 268435456 | bytes 5242880 | tf_op jit(solution)/shard_map/pallas_call | solution.py:495
  82.2 2.0 %collective-permute-start.22 = (bf16[128,512]{1,0:T(8,128)(2,1)S(1)}, bf16[128,512]{1,0:T(8,128)(2,1)S(1)}, u32[]{:S(2)}, u32[]{:S(2)}) collective-permute-start(bf16[128,512]{1,0:T(8,128)(2,1)S(1)} %get-tuple-element.100), channel_id=1, source_target_pairs={{0,4},{1,5},{2,6},{3,7},{4,0},{5,1},{6,2},{7,3},{8,12},{9,13},{10,... | collective-permute-start | bytes 393224 | tf_op jit(solution)/shard_map/ppermute | solution.py:50
  84.2 2.7 %collective-permute-start.23 = (bf16[128,512]{1,0:T(8,128)(2,1)S(1)}, bf16[128,512]{1,0:T(8,128)(2,1)S(1)}, u32[]{:S(2)}, u32[]{:S(2)}) collective-permute-start(bf16[128,512]{1,0:T(8,128)(2,1)S(1)} %get-tuple-element.101), channel_id=1, source_target_pairs={{0,6},{1,7},{2,4},{3,5},{4,2},{5,3},{6,0},{7,1},{8,14},{9,15},{10,... | collective-permute-start | bytes 393224 | tf_op jit(solution)/shard_map/ppermute | solution.py:50
  87.0 2.3 %collective-permute-start.27 = (bf16[128,512]{1,0:T(8,128)(2,1)S(1)}, bf16[128,512]{1,0:T(8,128)(2,1)S(1)}, u32[]{:S(2)}, u32[]{:S(2)}) collective-permute-start(bf16[128,512]{1,0:T(8,128)(2,1)S(1)} %add_convert_fusion.1), channel_id=1, source_target_pairs={{0,8},{1,9},{2,10},{3,11},{4,12},{5,13},{6,14},{7,15},{8,0},{9,1},... | collective-permute-start | bytes 393224 | tf_op jit(solution)/shard_map/ppermute | solution.py:50
  90.1 2.0 %collective-permute-done.23 = bf16[128,512]{1,0:T(8,128)(2,1)S(1)} collective-permute-done((bf16[128,512]{1,0:T(8,128)(2,1)S(1)}, bf16[128,512]{1,0:T(8,128)(2,1)S(1)}, u32[]{:S(2)}, u32[]{:S(2)}) %collective-permute-start.23) | collective-permute-done | bytes 131104 | tf_op jit(solution)/shard_map/ppermute | solution.py:50
  92.0 1.5 %collective-permute-done.27 = bf16[128,512]{1,0:T(8,128)(2,1)S(1)} collective-permute-done((bf16[128,512]{1,0:T(8,128)(2,1)S(1)}, bf16[128,512]{1,0:T(8,128)(2,1)S(1)}, u32[]{:S(2)}, u32[]{:S(2)}) %collective-permute-start.27) | collective-permute-done | bytes 131104 | tf_op jit(solution)/shard_map/ppermute | solution.py:50
  (73 shorter events, 10.3 us)
Async XLA Ops:
  1.3 25.9 %copy-start.11 = (s32[8]{0:T(128)S(1)}, s32[8]{0:T(128)}, u32[]{:S(2)}) copy-start(s32[8]{0:T(128)} %masks.1) | copy-start | bytes 100
  1.3 35.6 %copy-start.10 = (f32[8192]{0:T(1024)S(1)}, f32[8192]{0:T(1024)}, u32[]{:S(2)}) copy-start(f32[8192]{0:T(1024)} %param.11) | copy-start | bytes 98308
  7.3 29.9 %copy-start.2 = (bf16[8192,128]{1,0:T(8,128)(2,1)S(1)}, bf16[8192,128]{1,0:T(8,128)(2,1)}, u32[]{:S(2)}) copy-start(bf16[8192,128]{1,0:T(8,128)(2,1)} %refs_12_.1) | copy-start | bytes 6291460
  7.3 57.7 %collective-permute-start.17 = (bf16[8,512,512]{2,1,0:T(8,128)(2,1)}, bf16[8,512,512]{2,1,0:T(8,128)(2,1)}, u32[]{:S(2)}, u32[]{:S(2)}) collective-permute-start(bf16[8,512,512]{2,1,0:T(8,128)(2,1)} %get-tuple-element.80), channel_id=1, source_target_pairs={{0,1},{1,0},{2,3},{3,2},{4,5},{5,4},{6,7},{7,6},{8,9},{9,8},{10,11... | collective-permute-start | bytes 12582920 | tf_op jit(solution)/shard_map/ppermute | solution.py:50
  7.4 7.9 %collective-permute-start.4 = (bf16[128,512]{1,0:T(8,128)(2,1)S(1)}, bf16[128,512]{1,0:T(8,128)(2,1)S(1)}, u32[]{:S(2)}, u32[]{:S(2)}) collective-permute-start(bf16[128,512]{1,0:T(8,128)(2,1)S(1)} %bitcast.20), channel_id=1, source_target_pairs={{0,8},{1,9},{2,10},{3,11},{4,12},{5,13},{6,14},{7,15},{8,0},{9,1},... | collective-permute-start | bytes 393224 | tf_op jit(solution)/shard_map/ppermute | solution.py:50
  10.6 8.6 %collective-permute-start = (bf16[128,512]{1,0:T(8,128)(2,1)S(1)}, bf16[128,512]{1,0:T(8,128)(2,1)S(1)}, u32[]{:S(2)}, u32[]{:S(2)}) collective-permute-start(bf16[128,512]{1,0:T(8,128)(2,1)S(1)} %bitcast.21), channel_id=1, source_target_pairs={{0,2},{1,3},{2,0},{3,1},{4,6},{5,7},{6,4},{7,5},{8,10},{9,11},{10,... | collective-permute-start | bytes 393224 | tf_op jit(solution)/shard_map/ppermute | solution.py:50
  12.2 9.8 %collective-permute-start.1 = (bf16[128,512]{1,0:T(8,128)(2,1)S(1)}, bf16[128,512]{1,0:T(8,128)(2,1)S(1)}, u32[]{:S(2)}, u32[]{:S(2)}) collective-permute-start(bf16[128,512]{1,0:T(8,128)(2,1)S(1)} %bitcast.22), channel_id=1, source_target_pairs={{0,4},{1,5},{2,6},{3,7},{4,0},{5,1},{6,2},{7,3},{8,12},{9,13},{10,... | collective-permute-start | bytes 393224 | tf_op jit(solution)/shard_map/ppermute | solution.py:50
  15.1 12.1 %collective-permute-start.2 = (bf16[128,512]{1,0:T(8,128)(2,1)S(1)}, bf16[128,512]{1,0:T(8,128)(2,1)S(1)}, u32[]{:S(2)}, u32[]{:S(2)}) collective-permute-start(bf16[128,512]{1,0:T(8,128)(2,1)S(1)} %bitcast.23), channel_id=1, source_target_pairs={{0,6},{1,7},{2,4},{3,5},{4,2},{5,3},{6,0},{7,1},{8,14},{9,15},{10,... | collective-permute-start | bytes 393224 | tf_op jit(solution)/shard_map/ppermute | solution.py:50
  15.3 17.7 %collective-permute-start.8 = (bf16[8,128,256]{2,1,0:T(8,128)(2,1)}, bf16[8,128,256]{2,1,0:T(8,128)(2,1)S(1)}, u32[]{:S(2)}, u32[]{:S(2)}) collective-permute-start(bf16[8,128,256]{2,1,0:T(8,128)(2,1)} %get-tuple-element.63), channel_id=1, source_target_pairs={{0,64},{16,80},{32,96},{48,112},{64,0},{80,16},{96,32},{112,48},{1... | collective-permute-start | bytes 1572872 | tf_op jit(solution)/shard_map/ppermute | solution.py:50
  19.2 8.9 %collective-permute-start.6 = (bf16[128,512]{1,0:T(8,128)(2,1)S(1)}, bf16[128,512]{1,0:T(8,128)(2,1)S(1)}, u32[]{:S(2)}, u32[]{:S(2)}) collective-permute-start(bf16[128,512]{1,0:T(8,128)(2,1)S(1)} %collective-permute-done.4.refs_5_), channel_id=1, source_target_pairs={{0,4},{1,5},{2,6},{3,7},{4,0},{5,1},{6,2},{7,3},{8,12},{9,13},{10,... | collective-permute-start | bytes 393224 | tf_op jit(solution)/shard_map/ppermute | solution.py:50
  22.0 7.4 %collective-permute-start.7 = (bf16[128,512]{1,0:T(8,128)(2,1)S(1)}, bf16[128,512]{1,0:T(8,128)(2,1)S(1)}, u32[]{:S(2)}, u32[]{:S(2)}) collective-permute-start(bf16[128,512]{1,0:T(8,128)(2,1)S(1)} %collective-permute-done.4.refs_5_), channel_id=1, source_target_pairs={{0,6},{1,7},{2,4},{3,5},{4,2},{5,3},{6,0},{7,1},{8,14},{9,15},{10,... | collective-permute-start | bytes 393224 | tf_op jit(solution)/shard_map/ppermute | solution.py:50
  27.2 5.0 %collective-permute-start.5 = (bf16[128,512]{1,0:T(8,128)(2,1)S(1)}, bf16[128,512]{1,0:T(8,128)(2,1)S(1)}, u32[]{:S(2)}, u32[]{:S(2)}) collective-permute-start(bf16[128,512]{1,0:T(8,128)(2,1)S(1)} %collective-permute-done.4.refs_5_), channel_id=1, source_target_pairs={{0,2},{1,3},{2,0},{3,1},{4,6},{5,7},{6,4},{7,5},{8,10},{9,11},{10,... | collective-permute-start | bytes 393224 | tf_op jit(solution)/shard_map/ppermute | solution.py:50
  28.1 8.9 %collective-permute-start.3 = (bf16[4,128,512]{2,1,0:T(8,128)(2,1)}, bf16[4,128,512]{2,1,0:T(8,128)(2,1)}, u32[]{:S(2)}, u32[]{:S(2)}) collective-permute-start(bf16[4,128,512]{2,1,0:T(8,128)(2,1)} %pad_maximum_fusion), channel_id=1, source_target_pairs={{0,1},{1,0},{2,3},{3,2},{4,5},{5,4},{6,7},{7,6},{8,9},{9,8},{10,11... | collective-permute-start | bytes 1572872 | tf_op jit(solution)/shard_map/ppermute | solution.py:50
  35.0 2.3 %collective-permute-start.9 = (bf16[4,128,512]{2,1,0:T(8,128)(2,1)}, bf16[4,128,512]{2,1,0:T(8,128)(2,1)}, u32[]{:S(2)}, u32[]{:S(2)}) collective-permute-start(bf16[4,128,512]{2,1,0:T(8,128)(2,1)} %pad_maximum_fusion.1), channel_id=1, source_target_pairs={{0,1},{1,0},{2,3},{3,2},{4,5},{5,4},{6,7},{7,6},{8,9},{9,8},{10,11... | collective-permute-start | bytes 1572872 | tf_op jit(solution)/shard_map/ppermute | solution.py:50
  35.0 14.8 %collective-permute-start.12 = (bf16[8,128,256]{2,1,0:T(8,128)(2,1)}, bf16[8,128,256]{2,1,0:T(8,128)(2,1)}, u32[]{:S(2)}, u32[]{:S(2)}) collective-permute-start(bf16[8,128,256]{2,1,0:T(8,128)(2,1)} %broadcast_select_fusion.2), channel_id=1, source_target_pairs={{0,32},{16,48},{32,0},{48,16},{64,96},{80,112},{96,64},{112,80},{1... | collective-permute-start | bytes 1572872 | tf_op jit(solution)/shard_map/ppermute | solution.py:50
  36.9 16.7 %copy-start.9 = (s32[64]{0:T(128)S(1)}, s32[64]{0:T(128)}, u32[]{:S(2)}) copy-start(s32[64]{0:T(128)} %get-tuple-element.71.lens) | copy-start | bytes 772
  45.5 5.7 %collective-permute-start.11 = (bf16[128,640]{1,0:T(8,128)(2,1)S(1)}, bf16[128,640]{1,0:T(8,128)(2,1)S(1)}, u32[]{:S(2)}, u32[]{:S(2)}) collective-permute-start(bf16[128,640]{1,0:T(8,128)(2,1)S(1)} %get-tuple-element.66.mine), channel_id=1, source_target_pairs={{0,1},{1,0},{2,3},{3,2},{4,5},{5,4},{6,7},{7,6},{8,9},{9,8},{10,11... | collective-permute-start | bytes 491528 | tf_op jit(solution)/shard_map/ppermute | solution.py:50
  45.7 5.4 %collective-permute-start.10 = (bf16[16,128]{1,0:T(8,128)(2,1)S(1)}, bf16[16,128]{1,0:T(8,128)(2,1)S(1)}, u32[]{:S(2)}, u32[]{:S(2)}) collective-permute-start(bf16[16,128]{1,0:T(8,128)(2,1)S(1)} %convert_element_type.42), channel_id=1, source_target_pairs={{0,16},{16,0},{32,48},{48,32},{64,80},{80,64},{96,112},{112,96},{1... | collective-permute-start | bytes 12296 | tf_op jit(solution)/shard_map/ppermute | solution.py:50
  51.2 13.7 %collective-permute-start.18 = (bf16[8,128,256]{2,1,0:T(8,128)(2,1)S(1)}, bf16[8,128,256]{2,1,0:T(8,128)(2,1)S(1)}, u32[]{:S(2)}, u32[]{:S(2)}) collective-permute-start(bf16[8,128,256]{2,1,0:T(8,128)(2,1)S(1)} %broadcast_select_fusion.1), channel_id=1, source_target_pairs={{0,16},{16,0},{32,48},{48,32},{64,80},{80,64},{96,112},{112,96},{1... | collective-permute-start | bytes 1572872 | tf_op jit(solution)/shard_map/ppermute | solution.py:50
  51.8 4.5 %collective-permute-start.13 = (bf16[16,128]{1,0:T(8,128)(2,1)S(1)}, bf16[16,128]{1,0:T(8,128)(2,1)S(1)}, u32[]{:S(2)}, u32[]{:S(2)}) collective-permute-start(bf16[16,128]{1,0:T(8,128)(2,1)S(1)} %broadcast_select_fusion.5), channel_id=1, source_target_pairs={{0,32},{16,48},{32,0},{48,16},{64,96},{80,112},{96,64},{112,80},{1... | collective-permute-start | bytes 12296 | tf_op jit(solution)/shard_map/ppermute | solution.py:50
  56.4 6.5 %collective-permute-start.14 = (bf16[16,128]{1,0:T(8,128)(2,1)S(1)}, bf16[16,128]{1,0:T(8,128)(2,1)S(1)}, u32[]{:S(2)}, u32[]{:S(2)}) collective-permute-start(bf16[16,128]{1,0:T(8,128)(2,1)S(1)} %broadcast_select_fusion.3), channel_id=1, source_target_pairs={{0,64},{16,80},{32,96},{48,112},{64,0},{80,16},{96,32},{112,48},{1... | collective-permute-start | bytes 12296 | tf_op jit(solution)/shard_map/ppermute | solution.py:50
  62.8 2.2 %collective-permute-start.16 = (f32[520,128]{1,0:T(8,128)S(1)}, f32[520,128]{1,0:T(8,128)S(1)}, u32[]{:S(2)}, u32[]{:S(2)}) collective-permute-start(f32[520,128]{1,0:T(8,128)S(1)} %get-tuple-element.77.mine), channel_id=1, source_target_pairs={{0,1},{1,0},{2,3},{3,2},{4,5},{5,4},{6,7},{7,6},{8,9},{9,8},{10,11... | collective-permute-start | bytes 798728 | tf_op jit(solution)/shard_map/ppermute | solution.py:50
  63.0 8.6 %collective-permute-start.15 = (f32[520,128]{1,0:T(8,128)S(1)}, f32[520,128]{1,0:T(8,128)S(1)}, u32[]{:S(2)}, u32[]{:S(2)}) collective-permute-start(f32[520,128]{1,0:T(8,128)S(1)} %get-tuple-element.75.mine), channel_id=1, source_target_pairs={{0,1},{1,0},{2,3},{3,2},{4,5},{5,4},{6,7},{7,6},{8,9},{9,8},{10,11... | collective-permute-start | bytes 798728 | tf_op jit(solution)/shard_map/ppermute | solution.py:50
  70.2 1.4 %collective-permute-start.19 = (f32[72,128]{1,0:T(8,128)S(1)}, f32[72,128]{1,0:T(8,128)S(1)}, u32[]{:S(2)}, u32[]{:S(2)}) collective-permute-start(f32[72,128]{1,0:T(8,128)S(1)} %shard_map.118.late), channel_id=1, source_target_pairs={{0,1},{1,0},{2,3},{3,2},{4,5},{5,4},{6,7},{7,6},{8,9},{9,8},{10,11... | collective-permute-start | bytes 110600 | tf_op jit(solution)/shard_map/ppermute | solution.py:50
  70.2 1.3 %collective-permute-start.20 = (bf16[16,128]{1,0:T(8,128)(2,1)S(1)}, bf16[16,128]{1,0:T(8,128)(2,1)S(1)}, u32[]{:S(2)}, u32[]{:S(2)}) collective-permute-start(bf16[16,128]{1,0:T(8,128)(2,1)S(1)} %broadcast_select_fusion.4), channel_id=1, source_target_pairs={{0,1},{1,0},{2,3},{3,2},{4,5},{5,4},{6,7},{7,6},{8,9},{9,8},{10,11... | collective-permute-start | bytes 12296 | tf_op jit(solution)/shard_map/ppermute | solution.py:50
  74.8 9.4 %collective-permute-start.24 = (bf16[128,512]{1,0:T(8,128)(2,1)S(1)}, bf16[128,512]{1,0:T(8,128)(2,1)S(1)}, u32[]{:S(2)}, u32[]{:S(2)}) collective-permute-start(bf16[128,512]{1,0:T(8,128)(2,1)S(1)} %get-tuple-element.103), channel_id=1, source_target_pairs={{0,2},{1,3},{2,0},{3,1},{4,6},{5,7},{6,4},{7,5},{8,10},{9,11},{10,... | collective-permute-start | bytes 393224 | tf_op jit(solution)/shard_map/ppermute | solution.py:50
  74.9 12.0 %collective-permute-start.25 = (bf16[128,512]{1,0:T(8,128)(2,1)S(1)}, bf16[128,512]{1,0:T(8,128)(2,1)S(1)}, u32[]{:S(2)}, u32[]{:S(2)}) collective-permute-start(bf16[128,512]{1,0:T(8,128)(2,1)S(1)} %get-tuple-element.104), channel_id=1, source_target_pairs={{0,4},{1,5},{2,6},{3,7},{4,0},{5,1},{6,2},{7,3},{8,12},{9,13},{10,... | collective-permute-start | bytes 393224 | tf_op jit(solution)/shard_map/ppermute | solution.py:50
  76.9 10.0 %collective-permute-start.26 = (bf16[128,512]{1,0:T(8,128)(2,1)S(1)}, bf16[128,512]{1,0:T(8,128)(2,1)S(1)}, u32[]{:S(2)}, u32[]{:S(2)}) collective-permute-start(bf16[128,512]{1,0:T(8,128)(2,1)S(1)} %get-tuple-element.105), channel_id=1, source_target_pairs={{0,6},{1,7},{2,4},{3,5},{4,2},{5,3},{6,0},{7,1},{8,14},{9,15},{10,... | collective-permute-start | bytes 393224 | tf_op jit(solution)/shard_map/ppermute | solution.py:50
  82.1 7.2 %collective-permute-start.21 = (bf16[128,512]{1,0:T(8,128)(2,1)S(1)}, bf16[128,512]{1,0:T(8,128)(2,1)S(1)}, u32[]{:S(2)}, u32[]{:S(2)}) collective-permute-start(bf16[128,512]{1,0:T(8,128)(2,1)S(1)} %get-tuple-element.99), channel_id=1, source_target_pairs={{0,2},{1,3},{2,0},{3,1},{4,6},{5,7},{6,4},{7,5},{8,10},{9,11},{10,... | collective-permute-start | bytes 393224 | tf_op jit(solution)/shard_map/ppermute | solution.py:50
  82.2 7.8 %collective-permute-start.22 = (bf16[128,512]{1,0:T(8,128)(2,1)S(1)}, bf16[128,512]{1,0:T(8,128)(2,1)S(1)}, u32[]{:S(2)}, u32[]{:S(2)}) collective-permute-start(bf16[128,512]{1,0:T(8,128)(2,1)S(1)} %get-tuple-element.100), channel_id=1, source_target_pairs={{0,4},{1,5},{2,6},{3,7},{4,0},{5,1},{6,2},{7,3},{8,12},{9,13},{10,... | collective-permute-start | bytes 393224 | tf_op jit(solution)/shard_map/ppermute | solution.py:50
  84.2 7.8 %collective-permute-start.23 = (bf16[128,512]{1,0:T(8,128)(2,1)S(1)}, bf16[128,512]{1,0:T(8,128)(2,1)S(1)}, u32[]{:S(2)}, u32[]{:S(2)}) collective-permute-start(bf16[128,512]{1,0:T(8,128)(2,1)S(1)} %get-tuple-element.101), channel_id=1, source_target_pairs={{0,6},{1,7},{2,4},{3,5},{4,2},{5,3},{6,0},{7,1},{8,14},{9,15},{10,... | collective-permute-start | bytes 393224 | tf_op jit(solution)/shard_map/ppermute | solution.py:50
  87.0 6.6 %collective-permute-start.27 = (bf16[128,512]{1,0:T(8,128)(2,1)S(1)}, bf16[128,512]{1,0:T(8,128)(2,1)S(1)}, u32[]{:S(2)}, u32[]{:S(2)}) collective-permute-start(bf16[128,512]{1,0:T(8,128)(2,1)S(1)} %add_convert_fusion.1), channel_id=1, source_target_pairs={{0,8},{1,9},{2,10},{3,11},{4,12},{5,13},{6,14},{7,15},{8,0},{9,1},... | collective-permute-start | bytes 393224 | tf_op jit(solution)/shard_map/ppermute | solution.py:50
  (8 other events, 50.7 us)

commit v4 on v3

--- a/solution.py
+++ b/solution.py
@@ -96,7 +96,9 @@
 def project(where, slots, *refs):
     near, (near_sib,) = refs[: CHIPS // 2], refs[CHIPS // 2 : CHIPS // 2 + 1]
     far, (far_sib,) = refs[CHIPS // 2 + 1 : CHIPS + 1], refs[CHIPS + 1 : CHIPS + 2]
-    gain, wq, wkv, tables, out, sent, acc, wide = refs[CHIPS + 2 :]
+    gain, wq, wkv, tables_in, out, sent, acc, wide, tables, sem = refs[CHIPS + 2 :]
+    turns = pltpu.make_async_copy(tables_in, tables, sem)
+    turns.start()
     me = where[0]
     half = CHIPS // 2
     squares = None
@@ -115,6 +117,7 @@
                 acc[:, at] = term
             else:
                 acc[:, at] += term
+    turns.wait()
     mean = jnp.sum(squares, -1, keepdims=True) * (1.0 / (2 * CHIPS * SHARD))
     scale = lax.rsqrt(mean + EPS)
     cos = tables[0]
@@ -289,24 +292,19 @@
         ).astype(BF)
 
 
-def finish_first(where, mine, recv, q, fresh, wo, wos, *refs):
-    outs = refs[:CHIPS]
-    own_buf, sib_buf, flat, att, sems = refs[CHIPS:]
-    pending = out_copies(where, range(CHIPS), wo, wos, own_buf, sib_buf, sems)
+def combine_first(mine, recv, q, fresh, att, flat):
     attended(mine, recv, q, [fresh], flat, att)
-    for out, block in zip(outs, out_blocks(where, att, pending, own_buf, sib_buf)):
-        out[...] = block
-
-
-def finish_other(where, slots, mine, recv, late, late_sib, q, f1, f2, came, came_sib, wo, wos, *refs):
+
+
+def finish_other(where, slots, mine, recv, late, late_sib, q, f1, f2, came, came_sib, wo, wos, first, *refs):
     half = CHIPS // 2
-    before, outs = refs[:half], refs[half : 2 * half]
-    att, own_buf, sib_buf, carried, flat, own_terms, sib_terms, sems = refs[2 * half :]
+    outs = refs[:half]
+    att, own_buf, sib_buf, carried, flat, own_terms, sib_terms, sems = refs[half:]
     pending = out_copies(where, range(half), wo, wos, own_buf, sib_buf, sems)
     carried[...] = f1[...]
-    first = where[0] % 2 == 0
-    keys = jnp.where(first, came[...], came_sib[...])
-    values = jnp.where(first, came_sib[...], came[...])
+    low = where[0] % 2 == 0
+    keys = jnp.where(low, came[...], came_sib[...])
+    values = jnp.where(low, came_sib[...], came[...])
     arrived = jnp.concatenate([keys, values], 1)
     for j in range(MOVE):
         carried[pl.ds(slots[j], 1), :] = arrived[j : j + 1]
@@ -319,20 +317,19 @@
             kept[at, :] = some[pl.ds(j * HEADS, HEADS), :]
             stats = noted(stats, slots[j], fixes[:, j : j + 1], fixes[:, REQ + j : REQ + j + 1])
         kept[pl.ds(REQ * HEADS, HEADS), :] = stats
-    attended(own_terms, sib_terms, q, [carried, f2], flat, att)
-    for old, out, block in zip(before, outs, out_blocks(where, att, pending, own_buf, sib_buf)):
-        out[pl.ds(0, REQ), :] = old[...]
-        out[pl.ds(REQ, REQ), :] = block
+    att[pl.ds(0, REQ), :] = first[...]
+    attended(own_terms, sib_terms, q, [carried, f2], flat, att.at[pl.ds(REQ, REQ), :])
+    for out, block in zip(outs, out_blocks(where, att, pending, own_buf, sib_buf)):
+        out[...] = block
 
 
 def finish_same(where, att, wo, wos, *refs):
     half = CHIPS // 2
-    before, outs = refs[:half], refs[half : 2 * half]
-    own_buf, sib_buf, sems = refs[2 * half :]
+    outs = refs[:half]
+    own_buf, sib_buf, sems = refs[half:]
     pending = out_copies(where, range(half, CHIPS), wo, wos, own_buf, sib_buf, sems)
-    for old, out, block in zip(before, outs, out_blocks(where, att, pending, own_buf, sib_buf)):
-        out[pl.ds(0, REQ), :] = old[...]
-        out[pl.ds(REQ, REQ), :] = block
+    for out, block in zip(outs, out_blocks(where, att, pending, own_buf, sib_buf)):
+        out[...] = block
 
 
 def shards(
@@ -386,17 +383,21 @@
         return jnp.where(took, swap(part, "inst", 1 << bit), part)
 
     moving = hop(moving, 2, partner_mask)
-    far_all, moving = lax.optimization_barrier((jnp.stack(far), moving))
-    far_sib = swap(far_all, "tp", 1)
+    far_sib = swap(jnp.stack(far), "tp", 1)
     moving = hop(moving, 1, partner_mask)
 
     half_chips = CHIPS // 2
     gain = norm_gain.reshape(2 * CHIPS, SHARD)
     queries, sent = call(
         project,
-        [SMEM] * 2 + [VMEM] * (CHIPS + 6),
+        [SMEM] * 2 + [VMEM] * (CHIPS + 5) + [ANY],
         [VMEM] * 2,
-        [pltpu.VMEM((rows, OWN), F32), pltpu.VMEM((rows, HD), F32)],
+        [
+            pltpu.VMEM((rows, OWN), F32),
+            pltpu.VMEM((rows, HD), F32),
+            pltpu.VMEM((2, rows, HD), F32),
+            dma,
+        ],
         [shape((rows, OWN), BF), shape((2 * MOVE, HD), F32)],
         2 * rows * 2 * CHIPS * SHARD * OWN,
         12 << 20,
@@ -437,7 +438,6 @@
     )(where, own_lengths, queries, queries_sib, cache)
     t1, came = lax.optimization_barrier((t1, came))
     t1_sib = swap(t1, "tp", 1)
-    came = hop(came, 2, masks)
     t2, q2, f2 = call(
         functools.partial(attend, 1),
         [SMEM] * 2 + [VMEM] * 2 + [ANY],
@@ -449,24 +449,23 @@
     )(where, next_lengths, queries, queries_sib, cache)
     t2, came = lax.optimization_barrier((t2, came))
     t2_sib = swap(t2, "tp", 1)
+    came = hop(came, 2, masks)
     came_sib = swap(came, "tp", 1)
 
     def weights(count):
         return [pltpu.VMEM((count, SHARD, SHARD), BF)] * 2
 
     flat = pltpu.VMEM((REQ * HEADS, HD), F32)
-    block = shape((REQ, SHARD), BF)
     both = shape((rows, SHARD), BF)
-    firsts = call(
-        finish_first,
-        [SMEM] + [VMEM] * 4 + [ANY] * 2,
-        [VMEM] * CHIPS,
-        weights(CHIPS) + [flat, pltpu.VMEM((REQ, QW), BF), dma((CHIPS, 2))],
-        [block] * CHIPS,
-        2 * REQ * QW * CHIPS * SHARD,
-        10 << 20,
-    )(where, t1, t1_sib, q1, f1, w_out, wos)
-    first_half, moving = lax.optimization_barrier((firsts[:half_chips], moving))
+    att_first = call(
+        combine_first,
+        [VMEM] * 4,
+        VMEM,
+        [flat],
+        shape((REQ, QW), BF),
+        1 << 20,
+        1 << 20,
+    )(t1, t1_sib, q1, f1)
     t3 = call(
         attend_arrived,
         [SMEM] * 3 + [VMEM] * 2,
@@ -479,28 +478,28 @@
     t3_sib = swap(t3, "tp", 1)
     *others, att = call(
         finish_other,
-        [SMEM] * 2 + [VMEM] * 9 + [ANY] * 2 + [VMEM] * half_chips,
+        [SMEM] * 2 + [VMEM] * 9 + [ANY] * 2 + [VMEM],
         [VMEM] * (half_chips + 1),
         weights(half_chips)
         + [pltpu.VMEM((REQ, 2 * HD), F32), flat]
         + [pltpu.VMEM(term_shape.shape, F32)] * 2
         + [dma((half_chips, 2))],
-        [both] * half_chips + [shape((REQ, QW), BF)],
-        REQ * QW * CHIPS * SHARD,
+        [both] * half_chips + [shape((rows, QW), BF)],
+        2 * REQ * QW * CHIPS * SHARD,
         6 << 20,
     )(
         where, slots, t2, t2_sib, t3, t3_sib, q2, f1, f2, came.astype(F32), came_sib.astype(F32), w_out, wos,
-        *first_half,
+        att_first,
     )
     sames = call(
         finish_same,
-        [SMEM] + [VMEM] + [ANY] * 2 + [VMEM] * half_chips,
+        [SMEM] + [VMEM] + [ANY] * 2,
         [VMEM] * half_chips,
         weights(half_chips) + [dma((half_chips, 2))],
         [both] * half_chips,
         REQ * QW * CHIPS * SHARD,
         5 << 20,
-    )(where, att, w_out, wos, *firsts[half_chips:])
+    )(where, att, w_out, wos)
     parts = list(others) + list(sames)
 
     def added(values):

time: 94.6 us -> 90.8 us (0.960)
  Pallas kernels: 25.6 us -> 22.4 us
  starting transfers between devices: 37.5 us -> 35.9 us
  waiting for transfers between devices: 18.3 us -> 19.3 us
    pallas_call x4, Pallas kernels: 13.1 us -> 9.89 us  [the longest x1 3.46 us: shards(): call(project, [SMEM] * 2 + [VMEM] * (CHIPS + 5) + [ANY], [VMEM] * 2, [plt...]
    ppermute x28, starting transfers between devices: 37.5 us -> 35.9 us  [swap(): return lax.ppermute(value, axis, [(i, i ^ mask) for i in range(count)])]
    ppermute x28, waiting for transfers between devices: 18.3 us -> 19.3 us  [swap(): return lax.ppermute(value, axis, [(i, i ^ mask) for i in range(count)])]
    select_n x6 -> x5, other arithmetic: 3.64 us -> 3.54 us  [hop(): return jnp.where(took, swap(part, 'inst', 1 << bit), part)]
  transfers between devices with their start and end apart: 28 -> 28, of which waited for: 10 -> 13; matrix products, arithmetic and copies ran while one was open for 6% -> 6% of each run, Pallas kernels for 17% -> 14%
where the time goes in v4:
time: 90.8 us; the launch traced here: 90.6 us
  starting transfers between devices  35.9 us (40%)
  Pallas kernels  22.4 us (25%)
  waiting for transfers between devices  19.3 us (21%)
  other arithmetic  6.9 us (8%)
  local copies, waits for them, and re-layouts  5.18 us (6%)
  between operations  0.93 us (1%)
    ppermute x28, starting transfers between devices, swap(): return lax.ppermute(value, axis, [(i, i ^ mask) for i in range(count)])  35.9 us
    ppermute x28, waiting for transfers between devices, swap(): return lax.ppermute(value, axis, [(i, i ^ mask) for i in range(count)])  19.3 us
    pallas_call x1, Pallas kernels, shards(): call(prepare, [SMEM] * 4 + [VMEM] + [ANY] * 2, [SMEM] * 3 + [VMEM] * 2 +...  6.03 us
    unnamed x24, local copies, waits for them, and re-layouts  5.17 us
    select_n x5, other arithmetic, hop(): return jnp.where(took, swap(part, 'inst', 1 << bit), part)  3.54 us
    pallas_call x1, Pallas kernels, shards(): call(project, [SMEM] * 2 + [VMEM] * (CHIPS + 5) + [ANY], [VMEM] * 2, [plt...  3.46 us
    pallas_call x1, Pallas kernels, shards(): call(finish_other, [SMEM] * 2 + [VMEM] * 9 + [ANY] * 2 + [VMEM], [VMEM] *...  3.28 us
    pallas_call x1, Pallas kernels, shards(): call(functools.partial(attend, 1), [SMEM] * 2 + [VMEM] * 2 + [ANY], [VMEM...  2.77 us
  transfers between devices with their start and end apart: 28, of which 13 were waited for; matrix products, arithmetic and copies ran while one was open for 6% of the time, Pallas kernels for 14%

profile of v4, /device:TPU:0, one launch (start us, length us, event | category | flops | bytes accessed | tf_op | source)
XLA Modules:
  0.0 90.6 jit_solution(3308219675021991151)
XLA Ops:
  1.3 6.0 %shard_map.113 = (s32[8]{0:T(128)}, s32[64]{0:T(128)}, s32[64]{0:T(128)}, f32[2,128,128]{2,1,0:T(8,128)}, bf16[8,128,256]{2,1,0:T(8,128)(2,1)}, /*index=5*/bf16[8,512,512]{2,1,0:T(8,128)(2,1)}) custom-call(s32[2]{0:T(128)} %pad_add_fusion.where, s32[8,8]{1,0:T(8,128)} %moved.1, s32[8]{0:T(128)} %masks.1, s32[512]{0:T(512)} %lengths.1, ...), custom_call_target="tpu_custom_call" | custom-call | bytes 10485760 | tf_op jit(solution)/shard_map/pallas_call | solution.py:347
  7.4 3.2 %collective-permute-start.4 = (bf16[128,512]{1,0:T(8,128)(2,1)S(1)}, bf16[128,512]{1,0:T(8,128)(2,1)S(1)}, u32[]{:S(2)}, u32[]{:S(2)}) collective-permute-start(bf16[128,512]{1,0:T(8,128)(2,1)S(1)} %bitcast.20), channel_id=1, source_target_pairs={{0,8},{1,9},{2,10},{3,11},{4,12},{5,13},{6,14},{7,15},{8,0},{9,1},... | collective-permute-start | bytes 393224 | tf_op jit(solution)/shard_map/ppermute | solution.py:50
  10.6 3.0 %collective-permute-start.2 = (bf16[128,512]{1,0:T(8,128)(2,1)S(1)}, bf16[128,512]{1,0:T(8,128)(2,1)S(1)}, u32[]{:S(2)}, u32[]{:S(2)}) collective-permute-start(bf16[128,512]{1,0:T(8,128)(2,1)S(1)} %bitcast.21), channel_id=1, source_target_pairs={{0,6},{1,7},{2,4},{3,5},{4,2},{5,3},{6,0},{7,1},{8,14},{9,15},{10,... | collective-permute-start | bytes 393224 | tf_op jit(solution)/shard_map/ppermute | solution.py:50
  14.8 4.0 %collective-permute-start.11 = (bf16[8,128,256]{2,1,0:T(8,128)(2,1)}, bf16[8,128,256]{2,1,0:T(8,128)(2,1)S(1)}, u32[]{:S(2)}, u32[]{:S(2)}) collective-permute-start(bf16[8,128,256]{2,1,0:T(8,128)(2,1)} %get-tuple-element.51), channel_id=1, source_target_pairs={{0,64},{16,80},{32,96},{48,112},{64,0},{80,16},{96,32},{112,48},{1... | collective-permute-start | bytes 1572872 | tf_op jit(solution)/shard_map/ppermute | solution.py:50
  19.5 3.7 %collective-permute-start.7 = (bf16[128,512]{1,0:T(8,128)(2,1)S(1)}, bf16[128,512]{1,0:T(8,128)(2,1)S(1)}, u32[]{:S(2)}, u32[]{:S(2)}) collective-permute-start(bf16[128,512]{1,0:T(8,128)(2,1)S(1)} %collective-permute-done.4.refs_5_), channel_id=1, source_target_pairs={{0,6},{1,7},{2,4},{3,5},{4,2},{5,3},{6,0},{7,1},{8,14},{9,15},{10,... | collective-permute-start | bytes 393224 | tf_op jit(solution)/shard_map/ppermute | solution.py:50
  23.2 0.9 collective-permute-start.5
  24.1 0.9 pad_maximum_fusion
  24.9 3.7 %collective-permute-done.7.refs_8_ = bf16[128,512]{1,0:T(8,128)(2,1)S(1)} collective-permute-done((bf16[128,512]{1,0:T(8,128)(2,1)S(1)}, bf16[128,512]{1,0:T(8,128)(2,1)S(1)}, u32[]{:S(2)}, u32[]{:S(2)}) %collective-permute-start.7) | collective-permute-done | bytes 131104 | tf_op jit(solution)/shard_map/ppermute | solution.py:50
  28.7 2.3 %collective-permute-done.6.refs_7_ = bf16[128,512]{1,0:T(8,128)(2,1)S(1)} collective-permute-done((bf16[128,512]{1,0:T(8,128)(2,1)S(1)}, bf16[128,512]{1,0:T(8,128)(2,1)S(1)}, u32[]{:S(2)}, u32[]{:S(2)}) %collective-permute-start.6) | collective-permute-done | bytes 131104 | tf_op jit(solution)/shard_map/ppermute | solution.py:50
  31.0 0.9 pad_maximum_fusion.1
  31.9 2.0 %broadcast_select_fusion.1 = bf16[8,128,256]{2,1,0:T(8,128)(2,1)} fusion(bf16[8,128,256]{2,1,0:T(8,128)(2,1)S(1)} %collective-permute-done.11, bf16[8,128,256]{2,1,0:T(8,128)(2,1)} %get-tuple-element.51, pred[8]{0:T(512)(128)(4,1)S(1)} %get-tuple-element.85), kind=kLoop, calls=%fused_computation.3 | loop fusion | flops 262144 | bytes 1572872 | tf_op jit(solution)/shard_map/jit(_where)/select_n | solution.py:383
  33.8 1.9 %collective-permute-start.12 = (bf16[8,128,256]{2,1,0:T(8,128)(2,1)}, bf16[8,128,256]{2,1,0:T(8,128)(2,1)}, u32[]{:S(2)}, u32[]{:S(2)}) collective-permute-start(bf16[8,128,256]{2,1,0:T(8,128)(2,1)} %broadcast_select_fusion.1), channel_id=1, source_target_pairs={{0,32},{16,48},{32,0},{48,16},{64,96},{80,112},{96,64},{112,80},{1... | collective-permute-start | bytes 1572872 | tf_op jit(solution)/shard_map/ppermute | solution.py:50
  35.8 3.5 %copy-done.1 = bf16[8192,512]{1,0:T(8,128)(2,1)S(1)} copy-done((bf16[8192,512]{1,0:T(8,128)(2,1)S(1)}, bf16[8192,512]{1,0:T(8,128)(2,1)}, u32[]{:S(2)}) %copy-start.1) | copy-done | bytes 8388632
  39.3 1.0 %copy-done.5 = f32[2,128,128]{2,1,0:T(8,128)S(1)} copy-done((f32[2,128,128]{2,1,0:T(8,128)S(1)}, f32[2,128,128]{2,1,0:T(8,128)}, u32[]{:S(2)}) %copy-start.5) | copy-done | bytes 131096
  40.9 3.5 %shard_map.114 = (bf16[128,640]{1,0:T(8,128)(2,1)S(1)}, f32[16,128]{1,0:T(8,128)S(1)}) custom-call(s32[1]{0:T(128)} %bitcast.where, s32[8]{0:T(128)S(1)} %copy-done.6, bf16[128,512]{1,0:T(8,128)(2,1)S(1)} %bitcast.25, bf16[128,512]{1,0:T(8,128)(2,1)S(1)} %collective-permute-done.refs_1_, bf16[128,512]{1,0:T(8,128)(2,1)S(1)} %collective-permute-done.1.refs_2_, ...), custom_call_target="tpu_custom_call" | custom-call | flops 1342177280 | bytes 12582912 | tf_op jit(solution)/shard_map/pallas_call | solution.py:391
  45.2 2.9 %collective-permute-done.9 = bf16[16,128]{1,0:T(8,128)(2,1)S(1)} collective-permute-done((bf16[16,128]{1,0:T(8,128)(2,1)S(1)}, bf16[16,128]{1,0:T(8,128)(2,1)S(1)}, u32[]{:S(2)}, u32[]{:S(2)}) %collective-permute-start.9) | collective-permute-done | bytes 4128 | tf_op jit(solution)/shard_map/ppermute | solution.py:50
  48.7 1.3 %broadcast_select_fusion.2 = bf16[8,128,256]{2,1,0:T(8,128)(2,1)S(1)} fusion(bf16[8,128,256]{2,1,0:T(8,128)(2,1)} %collective-permute-done.12, bf16[8,128,256]{2,1,0:T(8,128)(2,1)} %broadcast_select_fusion.1, pred[8]{0:T(512)(128)(4,1)S(1)} %get-tuple-element.84), kind=kLoop, calls=%fused_computation.4 | loop fusion | flops 262144 | bytes 1572872 | tf_op jit(solution)/shard_map/jit(_where)/select_n | solution.py:383
  50.7 1.7 %collective-permute-start.13 = (bf16[16,128]{1,0:T(8,128)(2,1)S(1)}, bf16[16,128]{1,0:T(8,128)(2,1)S(1)}, u32[]{:S(2)}, u32[]{:S(2)}) collective-permute-start(bf16[16,128]{1,0:T(8,128)(2,1)S(1)} %broadcast_select_fusion.5), channel_id=1, source_target_pairs={{0,32},{16,48},{32,0},{48,16},{64,96},{80,112},{96,64},{112,80},{1... | collective-permute-start | bytes 12296 | tf_op jit(solution)/shard_map/ppermute | solution.py:50
  52.4 2.8 %shard_map.116 = (f32[520,128]{1,0:T(8,128)S(1)}, f32[512,128]{1,0:T(8,128)S(1)}, f32[64,256]{1,0:T(8,128)S(1)}) custom-call(s32[1]{0:T(128)} %bitcast.where, s32[64]{0:T(128)S(1)} %copy-done.9, bf16[128,640]{1,0:T(8,128)(2,1)S(1)} %get-tuple-element.49.mine, bf16[128,640]{1,0:T(8,128)(2,1)S(1)} %collective-permute-done.10.recv, ...), custom_call_target="tpu_custom_call" | custom-call | flops 33554432 | bytes 6291456 | tf_op jit(solution)/shard_map/pallas_call | solution.py:430
  55.2 2.8 %shard_map.115 = (f32[520,128]{1,0:T(8,128)S(1)}, f32[512,128]{1,0:T(8,128)S(1)}, f32[64,256]{1,0:T(8,128)S(1)}) custom-call(s32[1]{0:T(128)} %bitcast.where, s32[64]{0:T(128)S(1)} %copy-done.8, bf16[128,640]{1,0:T(8,128)(2,1)S(1)} %get-tuple-element.49.mine, bf16[128,640]{1,0:T(8,128)(2,1)S(1)} %collective-permute-done.10.recv, ...), custom_call_target="tpu_custom_call" | custom-call | flops 33554432 | bytes 6291456 | tf_op jit(solution)/shard_map/pallas_call | solution.py:441
  58.1 3.6 %collective-permute-start.17 = (bf16[16,128]{1,0:T(8,128)(2,1)S(1)}, bf16[16,128]{1,0:T(8,128)(2,1)S(1)}, u32[]{:S(2)}, u32[]{:S(2)}) collective-permute-start(bf16[16,128]{1,0:T(8,128)(2,1)S(1)} %broadcast_select_fusion.4), channel_id=1, source_target_pairs={{0,64},{16,80},{32,96},{48,112},{64,0},{80,16},{96,32},{112,48},{1... | collective-permute-start | bytes 12296 | tf_op jit(solution)/shard_map/ppermute | solution.py:50
  62.2 1.6 %collective-permute-done.15 = bf16[8,128,256]{2,1,0:T(8,128)(2,1)S(1)} collective-permute-done((bf16[8,128,256]{2,1,0:T(8,128)(2,1)S(1)}, bf16[8,128,256]{2,1,0:T(8,128)(2,1)S(1)}, u32[]{:S(2)}, u32[]{:S(2)}) %collective-permute-start.15) | collective-permute-done | bytes 524320 | tf_op jit(solution)/shard_map/ppermute | solution.py:50
  63.9 0.9 %shard_map.117.late = f32[72,128]{1,0:T(8,128)S(1)} custom-call(s32[1]{0:T(128)} %bitcast.where, s32[64]{0:T(128)S(1)} %copy-done.8, s32[8]{0:T(128)S(1)} %copy-done.7, f32[512,128]{1,0:T(8,128)S(1)} %get-tuple-element.59.q, bf16[8,128,256]{2,1,0:T(8,128)(2,1)S(1)} %broadcast_select_fusion.arrived), custom_call_target="tpu_custom_call" | custom-call | flops 4194304 | bytes 1048576 | tf_op jit(solution)/shard_map/pallas_call | solution.py:469
  67.1 3.3 %shard_map.119 = (bf16[128,512]{1,0:T(8,128)(2,1)S(1)}, bf16[128,512]{1,0:T(8,128)(2,1)S(1)}, bf16[128,512]{1,0:T(8,128)(2,1)S(1)}, bf16[128,512]{1,0:T(8,128)(2,1)S(1)}, bf16[128,1024]{1,0:T(8,128)(2,1)S(1)}) custom-call(s32[1]{0:T(128)} %bitcast.where, s32[8]{0:T(128)S(1)} %copy-done.7, f32[520,128]{1,0:T(8,128)S(1)} %get-tuple-element.58.mine, ...), custom_call_target="tpu_custom_call" | custom-call | flops 536870912 | bytes 6291456 | tf_op jit(solution)/shard_map/pallas_call | solution.py:479
  70.6 3.4 %collective-permute-start.25 = (bf16[128,512]{1,0:T(8,128)(2,1)S(1)}, bf16[128,512]{1,0:T(8,128)(2,1)S(1)}, u32[]{:S(2)}, u32[]{:S(2)}) collective-permute-start(bf16[128,512]{1,0:T(8,128)(2,1)S(1)} %get-tuple-element.74), channel_id=1, source_target_pairs={{0,4},{1,5},{2,6},{3,7},{4,0},{5,1},{6,2},{7,3},{8,12},{9,13},{10,... | collective-permute-start | bytes 393224 | tf_op jit(solution)/shard_map/ppermute | solution.py:50
  73.9 1.3 %collective-permute-start.26 = (bf16[128,512]{1,0:T(8,128)(2,1)S(1)}, bf16[128,512]{1,0:T(8,128)(2,1)S(1)}, u32[]{:S(2)}, u32[]{:S(2)}) collective-permute-start(bf16[128,512]{1,0:T(8,128)(2,1)S(1)} %get-tuple-element.75), channel_id=1, source_target_pairs={{0,6},{1,7},{2,4},{3,5},{4,2},{5,3},{6,0},{7,1},{8,14},{9,15},{10,... | collective-permute-start | bytes 393224 | tf_op jit(solution)/shard_map/ppermute | solution.py:50
  75.2 2.5 %shard_map.120 = (bf16[128,512]{1,0:T(8,128)(2,1)S(1)}, bf16[128,512]{1,0:T(8,128)(2,1)S(1)}, bf16[128,512]{1,0:T(8,128)(2,1)S(1)}, bf16[128,512]{1,0:T(8,128)(2,1)S(1)}) custom-call(s32[1]{0:T(128)} %bitcast.where, bf16[128,1024]{1,0:T(8,128)(2,1)S(1)} %get-tuple-element.67.att, bf16[512,8192]{1,0:T(8,128)(2,1)} %wo.5, ...), custom_call_target="tpu_custom_call" | custom-call | flops 268435456 | bytes 5242880 | tf_op jit(solution)/shard_map/pallas_call | solution.py:494
  77.8 3.4 %collective-permute-start.22 = (bf16[128,512]{1,0:T(8,128)(2,1)S(1)}, bf16[128,512]{1,0:T(8,128)(2,1)S(1)}, u32[]{:S(2)}, u32[]{:S(2)}) collective-permute-start(bf16[128,512]{1,0:T(8,128)(2,1)S(1)} %get-tuple-element.70), channel_id=1, source_target_pairs={{0,4},{1,5},{2,6},{3,7},{4,0},{5,1},{6,2},{7,3},{8,12},{9,13},{10,... | collective-permute-start | bytes 393224 | tf_op jit(solution)/shard_map/ppermute | solution.py:50
  81.3 1.3 %collective-permute-start.23 = (bf16[128,512]{1,0:T(8,128)(2,1)S(1)}, bf16[128,512]{1,0:T(8,128)(2,1)S(1)}, u32[]{:S(2)}, u32[]{:S(2)}) collective-permute-start(bf16[128,512]{1,0:T(8,128)(2,1)S(1)} %get-tuple-element.71), channel_id=1, source_target_pairs={{0,6},{1,7},{2,4},{3,5},{4,2},{5,3},{6,0},{7,1},{8,14},{9,15},{10,... | collective-permute-start | bytes 393224 | tf_op jit(solution)/shard_map/ppermute | solution.py:50
  84.1 2.9 %collective-permute-done.22 = bf16[128,512]{1,0:T(8,128)(2,1)S(1)} collective-permute-done((bf16[128,512]{1,0:T(8,128)(2,1)S(1)}, bf16[128,512]{1,0:T(8,128)(2,1)S(1)}, u32[]{:S(2)}, u32[]{:S(2)}) %collective-permute-start.22) | collective-permute-done | bytes 131104 | tf_op jit(solution)/shard_map/ppermute | solution.py:50
  87.0 1.9 %collective-permute-done.23 = bf16[128,512]{1,0:T(8,128)(2,1)S(1)} collective-permute-done((bf16[128,512]{1,0:T(8,128)(2,1)S(1)}, bf16[128,512]{1,0:T(8,128)(2,1)S(1)}, u32[]{:S(2)}, u32[]{:S(2)}) %collective-permute-start.23) | collective-permute-done | bytes 131104 | tf_op jit(solution)/shard_map/ppermute | solution.py:50
  88.9 0.9 collective-permute-done.27
  (72 shorter events, 10.9 us)
Async XLA Ops:
  1.3 30.6 %copy-start.11 = (s32[8]{0:T(128)S(1)}, s32[8]{0:T(128)}, u32[]{:S(2)}) copy-start(s32[8]{0:T(128)} %masks.1) | copy-start | bytes 100
  1.3 34.5 %copy-start.10 = (f32[8192]{0:T(1024)S(1)}, f32[8192]{0:T(1024)}, u32[]{:S(2)}) copy-start(f32[8192]{0:T(1024)} %param.11) | copy-start | bytes 98308
  7.3 28.5 %copy-start.2 = (bf16[8192,128]{1,0:T(8,128)(2,1)S(1)}, bf16[8192,128]{1,0:T(8,128)(2,1)}, u32[]{:S(2)}) copy-start(bf16[8192,128]{1,0:T(8,128)(2,1)} %refs_12_.1) | copy-start | bytes 6291460
  7.3 59.8 %collective-permute-start.19 = (bf16[8,512,512]{2,1,0:T(8,128)(2,1)}, bf16[8,512,512]{2,1,0:T(8,128)(2,1)}, u32[]{:S(2)}, u32[]{:S(2)}) collective-permute-start(bf16[8,512,512]{2,1,0:T(8,128)(2,1)} %get-tuple-element.64), channel_id=1, source_target_pairs={{0,1},{1,0},{2,3},{3,2},{4,5},{5,4},{6,7},{7,6},{8,9},{9,8},{10,11... | collective-permute-start | bytes 12582920 | tf_op jit(solution)/shard_map/ppermute | solution.py:50
  7.4 7.4 %collective-permute-start.4 = (bf16[128,512]{1,0:T(8,128)(2,1)S(1)}, bf16[128,512]{1,0:T(8,128)(2,1)S(1)}, u32[]{:S(2)}, u32[]{:S(2)}) collective-permute-start(bf16[128,512]{1,0:T(8,128)(2,1)S(1)} %bitcast.20), channel_id=1, source_target_pairs={{0,8},{1,9},{2,10},{3,11},{4,12},{5,13},{6,14},{7,15},{8,0},{9,1},... | collective-permute-start | bytes 393224 | tf_op jit(solution)/shard_map/ppermute | solution.py:50
  10.6 8.9 %collective-permute-start.2 = (bf16[128,512]{1,0:T(8,128)(2,1)S(1)}, bf16[128,512]{1,0:T(8,128)(2,1)S(1)}, u32[]{:S(2)}, u32[]{:S(2)}) collective-permute-start(bf16[128,512]{1,0:T(8,128)(2,1)S(1)} %bitcast.21), channel_id=1, source_target_pairs={{0,6},{1,7},{2,4},{3,5},{4,2},{5,3},{6,0},{7,1},{8,14},{9,15},{10,... | collective-permute-start | bytes 393224 | tf_op jit(solution)/shard_map/ppermute | solution.py:50
  13.6 9.6 %collective-permute-start.1 = (bf16[128,512]{1,0:T(8,128)(2,1)S(1)}, bf16[128,512]{1,0:T(8,128)(2,1)S(1)}, u32[]{:S(2)}, u32[]{:S(2)}) collective-permute-start(bf16[128,512]{1,0:T(8,128)(2,1)S(1)} %bitcast.22), channel_id=1, source_target_pairs={{0,4},{1,5},{2,6},{3,7},{4,0},{5,1},{6,2},{7,3},{8,12},{9,13},{10,... | collective-permute-start | bytes 393224 | tf_op jit(solution)/shard_map/ppermute | solution.py:50
  14.3 8.9 %collective-permute-start = (bf16[128,512]{1,0:T(8,128)(2,1)S(1)}, bf16[128,512]{1,0:T(8,128)(2,1)S(1)}, u32[]{:S(2)}, u32[]{:S(2)}) collective-permute-start(bf16[128,512]{1,0:T(8,128)(2,1)S(1)} %bitcast.23), channel_id=1, source_target_pairs={{0,2},{1,3},{2,0},{3,1},{4,6},{5,7},{6,4},{7,5},{8,10},{9,11},{10,... | collective-permute-start | bytes 393224 | tf_op jit(solution)/shard_map/ppermute | solution.py:50
  14.8 17.0 %collective-permute-start.11 = (bf16[8,128,256]{2,1,0:T(8,128)(2,1)}, bf16[8,128,256]{2,1,0:T(8,128)(2,1)S(1)}, u32[]{:S(2)}, u32[]{:S(2)}) collective-permute-start(bf16[8,128,256]{2,1,0:T(8,128)(2,1)} %get-tuple-element.51), channel_id=1, source_target_pairs={{0,64},{16,80},{32,96},{48,112},{64,0},{80,16},{96,32},{112,48},{1... | collective-permute-start | bytes 1572872 | tf_op jit(solution)/shard_map/ppermute | solution.py:50
  19.5 9.2 %collective-permute-start.7 = (bf16[128,512]{1,0:T(8,128)(2,1)S(1)}, bf16[128,512]{1,0:T(8,128)(2,1)S(1)}, u32[]{:S(2)}, u32[]{:S(2)}) collective-permute-start(bf16[128,512]{1,0:T(8,128)(2,1)S(1)} %collective-permute-done.4.refs_5_), channel_id=1, source_target_pairs={{0,6},{1,7},{2,4},{3,5},{4,2},{5,3},{6,0},{7,1},{8,14},{9,15},{10,... | collective-permute-start | bytes 393224 | tf_op jit(solution)/shard_map/ppermute | solution.py:50
  23.2 7.8 %collective-permute-start.6 = (bf16[128,512]{1,0:T(8,128)(2,1)S(1)}, bf16[128,512]{1,0:T(8,128)(2,1)S(1)}, u32[]{:S(2)}, u32[]{:S(2)}) collective-permute-start(bf16[128,512]{1,0:T(8,128)(2,1)S(1)} %collective-permute-done.4.refs_5_), channel_id=1, source_target_pairs={{0,4},{1,5},{2,6},{3,7},{4,0},{5,1},{6,2},{7,3},{8,12},{9,13},{10,... | collective-permute-start | bytes 393224 | tf_op jit(solution)/shard_map/ppermute | solution.py:50
  23.2 7.8 %collective-permute-start.5 = (bf16[128,512]{1,0:T(8,128)(2,1)S(1)}, bf16[128,512]{1,0:T(8,128)(2,1)S(1)}, u32[]{:S(2)}, u32[]{:S(2)}) collective-permute-start(bf16[128,512]{1,0:T(8,128)(2,1)S(1)} %collective-permute-done.4.refs_5_), channel_id=1, source_target_pairs={{0,2},{1,3},{2,0},{3,1},{4,6},{5,7},{6,4},{7,5},{8,10},{9,11},{10,... | collective-permute-start | bytes 393224 | tf_op jit(solution)/shard_map/ppermute | solution.py:50
  28.7 7.1 %collective-permute-start.3 = (bf16[4,128,512]{2,1,0:T(8,128)(2,1)}, bf16[4,128,512]{2,1,0:T(8,128)(2,1)}, u32[]{:S(2)}, u32[]{:S(2)}) collective-permute-start(bf16[4,128,512]{2,1,0:T(8,128)(2,1)} %pad_maximum_fusion), channel_id=1, source_target_pairs={{0,1},{1,0},{2,3},{3,2},{4,5},{5,4},{6,7},{7,6},{8,9},{9,8},{10,11... | collective-permute-start | bytes 1572872 | tf_op jit(solution)/shard_map/ppermute | solution.py:50
  31.8 3.9 %collective-permute-start.8 = (bf16[4,128,512]{2,1,0:T(8,128)(2,1)}, bf16[4,128,512]{2,1,0:T(8,128)(2,1)}, u32[]{:S(2)}, u32[]{:S(2)}) collective-permute-start(bf16[4,128,512]{2,1,0:T(8,128)(2,1)} %pad_maximum_fusion.1), channel_id=1, source_target_pairs={{0,1},{1,0},{2,3},{3,2},{4,5},{5,4},{6,7},{7,6},{8,9},{9,8},{10,11... | collective-permute-start | bytes 1572872 | tf_op jit(solution)/shard_map/ppermute | solution.py:50
  33.8 14.8 %collective-permute-start.12 = (bf16[8,128,256]{2,1,0:T(8,128)(2,1)}, bf16[8,128,256]{2,1,0:T(8,128)(2,1)}, u32[]{:S(2)}, u32[]{:S(2)}) collective-permute-start(bf16[8,128,256]{2,1,0:T(8,128)(2,1)} %broadcast_select_fusion.1), channel_id=1, source_target_pairs={{0,32},{16,48},{32,0},{48,16},{64,96},{80,112},{96,64},{112,80},{1... | collective-permute-start | bytes 1572872 | tf_op jit(solution)/shard_map/ppermute | solution.py:50
  35.7 16.7 %copy-start.9 = (s32[64]{0:T(128)S(1)}, s32[64]{0:T(128)}, u32[]{:S(2)}) copy-start(s32[64]{0:T(128)} %get-tuple-element.54.lens) | copy-start | bytes 772
  44.4 3.7 %collective-permute-start.9 = (bf16[16,128]{1,0:T(8,128)(2,1)S(1)}, bf16[16,128]{1,0:T(8,128)(2,1)S(1)}, u32[]{:S(2)}, u32[]{:S(2)}) collective-permute-start(bf16[16,128]{1,0:T(8,128)(2,1)S(1)} %convert_element_type.42), channel_id=1, source_target_pairs={{0,16},{16,0},{32,48},{48,32},{64,80},{80,64},{96,112},{112,96},{1... | collective-permute-start | bytes 12296 | tf_op jit(solution)/shard_map/ppermute | solution.py:50
  45.2 4.8 %collective-permute-start.10 = (bf16[128,640]{1,0:T(8,128)(2,1)S(1)}, bf16[128,640]{1,0:T(8,128)(2,1)S(1)}, u32[]{:S(2)}, u32[]{:S(2)}) collective-permute-start(bf16[128,640]{1,0:T(8,128)(2,1)S(1)} %get-tuple-element.49.mine), channel_id=1, source_target_pairs={{0,1},{1,0},{2,3},{3,2},{4,5},{5,4},{6,7},{7,6},{8,9},{9,8},{10,11... | collective-permute-start | bytes 491528 | tf_op jit(solution)/shard_map/ppermute | solution.py:50
  50.0 13.7 %collective-permute-start.15 = (bf16[8,128,256]{2,1,0:T(8,128)(2,1)S(1)}, bf16[8,128,256]{2,1,0:T(8,128)(2,1)S(1)}, u32[]{:S(2)}, u32[]{:S(2)}) collective-permute-start(bf16[8,128,256]{2,1,0:T(8,128)(2,1)S(1)} %broadcast_select_fusion.2), channel_id=1, source_target_pairs={{0,16},{16,0},{32,48},{48,32},{64,80},{80,64},{96,112},{112,96},{1... | collective-permute-start | bytes 1572872 | tf_op jit(solution)/shard_map/ppermute | solution.py:50
  50.7 7.3 %collective-permute-start.13 = (bf16[16,128]{1,0:T(8,128)(2,1)S(1)}, bf16[16,128]{1,0:T(8,128)(2,1)S(1)}, u32[]{:S(2)}, u32[]{:S(2)}) collective-permute-start(bf16[16,128]{1,0:T(8,128)(2,1)S(1)} %broadcast_select_fusion.5), channel_id=1, source_target_pairs={{0,32},{16,48},{32,0},{48,16},{64,96},{80,112},{96,64},{112,80},{1... | collective-permute-start | bytes 12296 | tf_op jit(solution)/shard_map/ppermute | solution.py:50
  58.1 6.8 %collective-permute-start.17 = (bf16[16,128]{1,0:T(8,128)(2,1)S(1)}, bf16[16,128]{1,0:T(8,128)(2,1)S(1)}, u32[]{:S(2)}, u32[]{:S(2)}) collective-permute-start(bf16[16,128]{1,0:T(8,128)(2,1)S(1)} %broadcast_select_fusion.4), channel_id=1, source_target_pairs={{0,64},{16,80},{32,96},{48,112},{64,0},{80,16},{96,32},{112,48},{1... | collective-permute-start | bytes 12296 | tf_op jit(solution)/shard_map/ppermute | solution.py:50
  61.7 5.4 %collective-permute-start.14 = (f32[520,128]{1,0:T(8,128)S(1)}, f32[520,128]{1,0:T(8,128)S(1)}, u32[]{:S(2)}, u32[]{:S(2)}) collective-permute-start(f32[520,128]{1,0:T(8,128)S(1)} %get-tuple-element.58.mine), channel_id=1, source_target_pairs={{0,1},{1,0},{2,3},{3,2},{4,5},{5,4},{6,7},{7,6},{8,9},{9,8},{10,11... | collective-permute-start | bytes 798728 | tf_op jit(solution)/shard_map/ppermute | solution.py:50
  61.7 4.8 %collective-permute-start.20 = (f32[520,128]{1,0:T(8,128)S(1)}, f32[520,128]{1,0:T(8,128)S(1)}, u32[]{:S(2)}, u32[]{:S(2)}) collective-permute-start(f32[520,128]{1,0:T(8,128)S(1)} %get-tuple-element.65.mine), channel_id=1, source_target_pairs={{0,1},{1,0},{2,3},{3,2},{4,5},{5,4},{6,7},{7,6},{8,9},{9,8},{10,11... | collective-permute-start | bytes 798728 | tf_op jit(solution)/shard_map/ppermute | solution.py:50
  64.8 2.3 %collective-permute-start.16 = (f32[72,128]{1,0:T(8,128)S(1)}, f32[72,128]{1,0:T(8,128)S(1)}, u32[]{:S(2)}, u32[]{:S(2)}) collective-permute-start(f32[72,128]{1,0:T(8,128)S(1)} %shard_map.117.late), channel_id=1, source_target_pairs={{0,1},{1,0},{2,3},{3,2},{4,5},{5,4},{6,7},{7,6},{8,9},{9,8},{10,11... | collective-permute-start | bytes 110600 | tf_op jit(solution)/shard_map/ppermute | solution.py:50
  65.0 1.5 %collective-permute-start.18 = (bf16[16,128]{1,0:T(8,128)(2,1)S(1)}, bf16[16,128]{1,0:T(8,128)(2,1)S(1)}, u32[]{:S(2)}, u32[]{:S(2)}) collective-permute-start(bf16[16,128]{1,0:T(8,128)(2,1)S(1)} %get-tuple-element.79), channel_id=1, source_target_pairs={{0,1},{1,0},{2,3},{3,2},{4,5},{5,4},{6,7},{7,6},{8,9},{9,8},{10,11... | collective-permute-start | bytes 12296 | tf_op jit(solution)/shard_map/ppermute | solution.py:50
  70.4 10.8 %collective-permute-start.24 = (bf16[128,512]{1,0:T(8,128)(2,1)S(1)}, bf16[128,512]{1,0:T(8,128)(2,1)S(1)}, u32[]{:S(2)}, u32[]{:S(2)}) collective-permute-start(bf16[128,512]{1,0:T(8,128)(2,1)S(1)} %get-tuple-element.73), channel_id=1, source_target_pairs={{0,2},{1,3},{2,0},{3,1},{4,6},{5,7},{6,4},{7,5},{8,10},{9,11},{10,... | collective-permute-start | bytes 393224 | tf_op jit(solution)/shard_map/ppermute | solution.py:50
  70.6 12.0 %collective-permute-start.25 = (bf16[128,512]{1,0:T(8,128)(2,1)S(1)}, bf16[128,512]{1,0:T(8,128)(2,1)S(1)}, u32[]{:S(2)}, u32[]{:S(2)}) collective-permute-start(bf16[128,512]{1,0:T(8,128)(2,1)S(1)} %get-tuple-element.74), channel_id=1, source_target_pairs={{0,4},{1,5},{2,6},{3,7},{4,0},{5,1},{6,2},{7,3},{8,12},{9,13},{10,... | collective-permute-start | bytes 393224 | tf_op jit(solution)/shard_map/ppermute | solution.py:50
  73.9 9.3 %collective-permute-start.26 = (bf16[128,512]{1,0:T(8,128)(2,1)S(1)}, bf16[128,512]{1,0:T(8,128)(2,1)S(1)}, u32[]{:S(2)}, u32[]{:S(2)}) collective-permute-start(bf16[128,512]{1,0:T(8,128)(2,1)S(1)} %get-tuple-element.75), channel_id=1, source_target_pairs={{0,6},{1,7},{2,4},{3,5},{4,2},{5,3},{6,0},{7,1},{8,14},{9,15},{10,... | collective-permute-start | bytes 393224 | tf_op jit(solution)/shard_map/ppermute | solution.py:50
  77.7 6.4 %collective-permute-start.21 = (bf16[128,512]{1,0:T(8,128)(2,1)S(1)}, bf16[128,512]{1,0:T(8,128)(2,1)S(1)}, u32[]{:S(2)}, u32[]{:S(2)}) collective-permute-start(bf16[128,512]{1,0:T(8,128)(2,1)S(1)} %get-tuple-element.69), channel_id=1, source_target_pairs={{0,2},{1,3},{2,0},{3,1},{4,6},{5,7},{6,4},{7,5},{8,10},{9,11},{10,... | collective-permute-start | bytes 393224 | tf_op jit(solution)/shard_map/ppermute | solution.py:50
  77.8 9.2 %collective-permute-start.22 = (bf16[128,512]{1,0:T(8,128)(2,1)S(1)}, bf16[128,512]{1,0:T(8,128)(2,1)S(1)}, u32[]{:S(2)}, u32[]{:S(2)}) collective-permute-start(bf16[128,512]{1,0:T(8,128)(2,1)S(1)} %get-tuple-element.70), channel_id=1, source_target_pairs={{0,4},{1,5},{2,6},{3,7},{4,0},{5,1},{6,2},{7,3},{8,12},{9,13},{10,... | collective-permute-start | bytes 393224 | tf_op jit(solution)/shard_map/ppermute | solution.py:50
  81.3 7.7 %collective-permute-start.23 = (bf16[128,512]{1,0:T(8,128)(2,1)S(1)}, bf16[128,512]{1,0:T(8,128)(2,1)S(1)}, u32[]{:S(2)}, u32[]{:S(2)}) collective-permute-start(bf16[128,512]{1,0:T(8,128)(2,1)S(1)} %get-tuple-element.71), channel_id=1, source_target_pairs={{0,6},{1,7},{2,4},{3,5},{4,2},{5,3},{6,0},{7,1},{8,14},{9,15},{10,... | collective-permute-start | bytes 393224 | tf_op jit(solution)/shard_map/ppermute | solution.py:50
  83.3 6.6 %collective-permute-start.27 = (bf16[128,512]{1,0:T(8,128)(2,1)S(1)}, bf16[128,512]{1,0:T(8,128)(2,1)S(1)}, u32[]{:S(2)}, u32[]{:S(2)}) collective-permute-start(bf16[128,512]{1,0:T(8,128)(2,1)S(1)} %add_convert_fusion.1), channel_id=1, source_target_pairs={{0,8},{1,9},{2,10},{3,11},{4,12},{5,13},{6,14},{7,15},{8,0},{9,1},... | collective-permute-start | bytes 393224 | tf_op jit(solution)/shard_map/ppermute | solution.py:50
  (8 other events, 59.2 us)
